TPU v7x, 256 devices: a whole 4x4x8 slice. The times are simulated.
256 devices in a mesh: gx: 32 (over z_hi, x, core), gy: 8 (over y, z_lo).
Axes of the slice: x: 4, y: 4, z: 8 (z_hi: 4, z_lo: 2; z = z_hi * 2 + z_lo), core: 2. Of those that a mesh axis runs over, the one named last changes fastest.
Arguments:
- noisy_field: bfloat16 [16, 256, 1024], P(None, 'gx', 'gy'), may hold values from -6 to 6
- first_weight: bfloat16 [16, 1, 3, 3, 3], replicated, may hold values from -1.5 to 1.5
- down_weight: bfloat16 [32, 16, 3, 3, 3], replicated, may hold values from -0.375 to 0.375
- coarse_weight: bfloat16 [64, 32, 3, 3, 3], replicated, may hold values from -0.25 to 0.25
- middle_weight: bfloat16 [32, 96, 3, 3, 3], replicated, may hold values from -0.15625 to 0.15625
- fine_weight: bfloat16 [16, 48, 3, 3, 3], replicated, may hold values from -0.25 to 0.25
- head_weight: bfloat16 [16], replicated, may hold values from -1.5 to 1.5
Outputs:
- noise_estimate: float32 [16, 256, 1024], P(None, 'gx', 'gy')
All inputs are finite; a program needn't handle non-finite values.
Results may differ from a plain program's by a relative error of at most 0.005.
Values may be sent and summed in bfloat16 or wider, within the bound.
No kernel may reach another device: no remote copies, remote signals or barrier semaphores. Data moves between devices by JAX's collectives and lax.ppermute only.
A program may use at most 128 MiB of HBM per device.

v0:
```python
import jax
import jax.numpy as jnp
from jax import lax
from jax.experimental import pallas as pl
from jax.experimental.pallas import tpu as pltpu
from jax.sharding import PartitionSpec as P

BF = jnp.bfloat16
F32 = jnp.float32
J = 48
VMEM = pl.BlockSpec(memory_space=pltpu.VMEM)


def dot(a, b):
    return jnp.dot(a, b, preferred_element_type=F32)


def dot_nt(a, b):
    return lax.dot_general(a, b, (((1,), (1,)), ((), ())), preferred_element_type=F32)


def dot_tn(a, b):
    return lax.dot_general(a, b, (((0,), (0,)), ((), ())), preferred_element_type=F32)


def iota(shape, axis):
    return lax.broadcasted_iota(jnp.int32, shape, axis)


def natural(channels):
    return lambda lane: lane // channels


def halves(channels):
    return lambda lane: 2 * ((lane // channels) % (128 // channels)) + lane // 128


def repeat_matrix(channels):
    return (iota((channels, 256), 1) % channels == iota((channels, 256), 0)).astype(BF)


def ones_where(cond):
    return jnp.where(cond, 1.0, 0.0).astype(BF)


def band_masks(rows, depth, depth_of):
    place = depth_of(iota((rows, 256), 1))
    return [ones_where(place == depth + 1 - tap) for tap in range(3)]


def up_masks(rows, depth, depth_of):
    place = depth_of(iota((rows, 256), 1))
    inner = (place == 2 * depth) | (place == 2 * depth + 1)
    outer = (place == 2 * depth + 2) | (place == 2 * depth - 1)
    return ones_where(inner), ones_where(outer)


SETS = (((0,), (1, 2)), ((0, 1), (2,)))


def weights_kernel(
    first, down, coarse, middle, fine, head,
    w_first, w_down, w_coarse, w_mid_skip, w_mid_up, w_fine_skip, w_fine_up, w_head,
    tiled,
):
    r16, r32, r64 = repeat_matrix(16), repeat_matrix(32), repeat_matrix(64)

    w_first[...] = jnp.zeros_like(w_first)
    for dx in range(3):
        rows = [dot(first[dz * 3 + dx], r16) * 0.5 for dz in range(3)]
        place = halves(16)(iota((16, 256), 1))
        depth = iota((16, 256), 0)
        for dy in range(3):
            block = jnp.zeros((16, 256), F32)
            for dz in range(3):
                block = block + jnp.where(place == depth + 1 - dz, rows[dz][dy : dy + 1], 0.0)
            block = block.astype(BF)
            for even in range(2):
                w_first[even, pl.ds(dy * 64 + (even + dx) * 16, 16), :] = block

    def banded(out, taps, channels, row_depths, depth_of):
        size = channels * len(row_depths)
        for at, depth in enumerate(row_depths):
            masks = band_masks(channels, depth, depth_of)
            for xy in range(9):
                block = sum(masks[dz] * taps[dz][xy] for dz in range(3))
                out[pl.ds(xy * size + at * channels, channels), :] = block

    def folded(out, get, channels, depths, depth_of):
        size = channels * depths
        place = depth_of(iota((channels, 256), 1))
        even = place % 2 == 0
        masks = [up_masks(channels, depth, depth_of) for depth in range(depths)]
        for px in range(2):
            for tx in range(2):
                by_y = [
                    [sum(get(dz, dx, dy) for dx in SETS[px][tx]) for dy in range(3)]
                    for dz in range(3)
                ]
                for py in range(2):
                    for ty in range(2):
                        w0, w1, w2 = [
                            sum(by_y[dz][dy] for dy in SETS[py][ty]) for dz in range(3)
                        ]
                        inner = jnp.where(even, w1 + w2, w0 + w1).astype(BF)
                        outer = jnp.where(even, w0, w2).astype(BF)
                        for depth in range(depths):
                            block = masks[depth][0] * inner + masks[depth][1] * outer
                            at = (tx * 2 + ty) * size + depth * channels
                            out[px * 2 + py, pl.ds(at, channels), :] = block

    flat = down[...].reshape(27 * 16, 32)
    all_taps = (dot(flat, r32) * (1 / 16)).astype(BF)
    taps = [[all_taps[(dz * 9 + xy) * 16 : (dz * 9 + xy + 1) * 16] for xy in range(9)] for dz in range(3)]
    banded(w_down, taps, 16, list(range(8)), halves(32))

    flat = coarse[...].reshape(27 * 32, 64)
    all_taps = (dot(flat, r64) * (1 / 16)).astype(BF)
    taps = [[all_taps[(dz * 9 + xy) * 32 : (dz * 9 + xy + 1) * 32] for xy in range(9)] for dz in range(3)]
    banded(w_coarse, taps, 32, list(range(4)), natural(64))

    for tap in range(27):
        tiled[tap] = dot_tn(middle[tap], r32) * 0.5
    taps = [[tiled[dz * 9 + xy, 64:96, :].astype(BF) for xy in range(9)] for dz in range(3)]
    banded(w_mid_skip, taps, 32, [0, 2, 4, 6, 1, 3, 5, 7], natural(32))
    folded(w_mid_up, lambda dz, dx, dy: tiled[dz * 9 + dx * 3 + dy, 0:64, :], 64, 4, natural(32))

    for tap in range(27):
        tiled[tap, 0:48, :] = dot_tn(fine[tap], r16) * 0.5
    taps = [[tiled[dz * 9 + xy, 32:48, :].astype(BF) for xy in range(9)] for dz in range(3)]
    banded(w_fine_skip, taps, 16, list(range(0, 16, 2)) + list(range(1, 16, 2)), natural(16))
    folded(w_fine_up, lambda dz, dx, dy: tiled[dz * 9 + dx * 3 + dy, 0:32, :], 32, 8, natural(16))

    row = dot(jnp.broadcast_to(head[...], (16, 16)), r16)
    w_head[...] = jnp.where(iota((16, 256), 1) // 16 == iota((16, 256), 0), row, 0.0).astype(BF)


def join_kernel(own, high, low, out):
    near = iota((128, 128), 1) < 64
    mine = own[...].astype(F32).reshape(128, 128)
    rim = jnp.where(
        near, high[...].astype(F32).reshape(128, 128), low[...].astype(F32).reshape(128, 128)
    )
    both = jnp.concatenate([mine, rim], axis=1).astype(BF)
    row, col = iota((128, 128), 0), iota((128, 128), 1)
    swap = (col == (row % 16) * 8 + row // 16).astype(BF)
    out[...] = dot(swap, both).astype(BF)


def silu_half(h):
    return h + h * jnp.tanh(h)


def net_kernel(
    own, swap_in, swap_out, low2, high2,
    w_first, w_down, w_coarse, w_mid_skip, w_mid_up, w_fine_skip, w_fine_up, w_head,
    out,
    fine_s, pool_fine_s, mid_s, pool_mid_s, coarse_s, up_s, last_s,
):
    gx, gy = lax.axis_index("gx"), lax.axis_index("gy")
    cells_x, cells_y = lax.axis_size("gx") * 2, lax.axis_size("gy") * 32

    def row_flag(cell):
        at = gx * 2 + cell
        return jnp.where((at >= 0) & (at < cells_x), 1.0, 0.0)

    def cell_of(j):
        return jnp.where(j < 40, j, j - J)

    at_y = gy * 32 + cell_of(iota((J, 256), 0))
    y_mask = jnp.where((at_y >= 0) & (at_y < cells_y), 1.0, 0.0)

    odd = gx % 2 == 1
    inner, outer = swap_in[...], swap_out[...]
    flag = jnp.where(odd, 1.0, 0.0).astype(BF)
    keep = jnp.where(odd, 0.0, 1.0).astype(BF)
    low1 = inner * flag + outer * keep
    high1 = inner * keep + outer * flag
    field = jnp.concatenate([low2[...], low1, own[...], high1, high2[...]], axis=0)
    wide = field.astype(F32)
    shifted = [
        pltpu.roll(wide, 1, 1).astype(BF),
        field,
        pltpu.roll(wide, 255, 1).astype(BF),
    ]
    row = iota((4 * J, 256), 0)
    cell = cell_of(row % J)
    y = 4 * cell + row // J
    at_row = gy * 32 + cell
    pick = (
        (iota((4 * J, 256), 1) == (y + 256) % 256) & (at_row >= 0) & (at_row < cells_y)
    ).astype(BF)

    for m in range(-5, 9):
        at = (2 * m + 10) * 16
        window = jnp.concatenate([part[at : at + 64] for part in shifted], axis=0)
        lhs = (dot_nt(pick, window) * row_flag(m // 2)).astype(BF)
        pooled = [jnp.zeros((J, 128), F32) for _ in range(2)]
        for even in range(2):
            x = 2 * m + even
            value = silu_half(dot(lhs, w_first[even])).reshape(4, J, 256)
            for part in range(2):
                both = value[2 * part] + value[2 * part + 1]
                pooled[part] = pooled[part] + both[:, :128] + both[:, 128:]
            if -1 <= x <= 8:
                for group in range(4):
                    fine_s[group + 1, x + 1] = value[group, :32].astype(BF)
                fine_s[0, x + 1] = pltpu.roll(value[3], 1, 0)[:32].astype(BF)
                fine_s[5, x + 1] = pltpu.roll(value[0], J - 1, 0)[:32].astype(BF)
        pool_fine_s[0, m + 5] = pltpu.roll(pooled[1], 1, 0).astype(BF)
        pool_fine_s[1, m + 5] = pooled[0].astype(BF)
        pool_fine_s[2, m + 5] = pooled[1].astype(BF)
        pool_fine_s[3, m + 5] = pltpu.roll(pooled[0], J - 1, 0).astype(BF)

    sums = [jnp.zeros((J, 128), F32) for _ in range(6)]
    for py in range(2):
        lhs = jnp.concatenate(
            [
                pool_fine_s[py + dy, dx : dx + 12].reshape(12 * J, 128)
                for dx in range(3)
                for dy in range(3)
            ],
            axis=1,
        )
        value = silu_half(dot(lhs, w_down[...])).reshape(12, J, 256)
        for at in range(12):
            m = at - 4
            masked = value[at] * (y_mask * row_flag(m // 2))
            sums[at // 2] = sums[at // 2] + masked[:, :128] + masked[:, 128:]
            if -2 <= m <= 5:
                mid_s[py + 1, m + 2] = masked.astype(BF)
                shift = 1 if py else J - 1
                mid_s[0 if py else 3, m + 2] = pltpu.roll(masked, shift, 0).astype(BF)
    for at in range(6):
        pool_mid_s[0, at] = pltpu.roll(sums[at], 1, 0).astype(BF)
        pool_mid_s[1, at] = sums[at].astype(BF)
        pool_mid_s[2, at] = pltpu.roll(sums[at], J - 1, 0).astype(BF)

    lhs = jnp.concatenate(
        [
            pool_mid_s[dy, dx : dx + 4].reshape(4 * J, 128)
            for dx in range(3)
            for dy in range(3)
        ],
        axis=1,
    )
    value = silu_half(dot(lhs, w_coarse[...])).reshape(4, J, 256)
    for at in range(4):
        masked = value[at] * (y_mask * row_flag(at - 1))
        coarse_s[0, at] = pltpu.roll(masked, 1, 0).astype(BF)
        coarse_s[1, at] = masked.astype(BF)
        coarse_s[2, at] = pltpu.roll(masked, J - 1, 0).astype(BF)

    lhs = jnp.concatenate(
        [
            mid_s[dy : dy + 2, dx : dx + 6].reshape(12 * J, 256)
            for dx in range(3)
            for dy in range(3)
        ],
        axis=1,
    )
    skip = dot(lhs, w_mid_skip[...]).reshape(2, 6, J, 256)
    for py in range(2):
        lhs = jnp.concatenate(
            [
                coarse_s[py + ty, tx : tx + 3].reshape(3 * J, 256)
                for tx in range(2)
                for ty in range(2)
            ],
            axis=1,
        )
        for px in range(2):
            up = dot(lhs, w_mid_up[px * 2 + py]).reshape(3, J, 256)
            for k in range(3):
                at = 2 * k if px else 2 * k + 1
                value = silu_half(skip[py, at] + up[k])
                masked = value * (y_mask * row_flag((at - 1) // 2))
                up_s[py + 1, at] = masked[:32].astype(BF)
                shift = 1 if py else J - 1
                up_s[0 if py else 3, at] = pltpu.roll(masked, shift, 0)[:32].astype(BF)

    for py in range(2):
        skip = []
        for half in range(2):
            group = 2 * half + py
            lhs = jnp.concatenate(
                [
                    fine_s[group + dy, dx : dx + 8].reshape(256, 256)
                    for dx in range(3)
                    for dy in range(3)
                ],
                axis=1,
            )
            skip.append(dot(lhs, w_fine_skip[...]).reshape(8, 32, 256))
        for px in range(2):
            lhs = jnp.concatenate(
                [
                    up_s[py + ty : py + ty + 2, px + tx : px + tx + 4].reshape(256, 256)
                    for tx in range(2)
                    for ty in range(2)
                ],
                axis=1,
            )
            up = dot(lhs, w_fine_up[px * 2 + py]).reshape(2, 4, 32, 256)
            for half in range(2):
                group = 2 * half + py
                for k in range(4):
                    x = 2 * k + px
                    value = silu_half(skip[half][x] + up[half, k])
                    last_s[x, pl.ds(group * 32, 32), :] = value.astype(BF)

    heads = jnp.concatenate([dot_nt(w_head[...], last_s[x]) for x in range(8)], axis=0)
    high = heads.astype(BF)
    rest = heads - high.astype(F32)
    low = rest.astype(BF)
    lowest = (rest - low.astype(F32)).astype(BF)
    row, col = iota((128, 128), 0), iota((128, 128), 1)
    order = (col == 4 * (row % 32) + row // 32).astype(BF)
    noise = dot(
        jnp.concatenate([high, low, lowest], axis=1),
        jnp.concatenate([order, order, order], axis=0),
    ).reshape(8, 16, 128)
    for x in range(8):
        out[:, x, :] = noise[x]


def body(
    noisy_field, first_weight, down_weight, coarse_weight, middle_weight, fine_weight, head_weight
):
    def shape(*dims, kind=BF):
        return jax.ShapeDtypeStruct(dims, kind)

    weights = pl.pallas_call(
        weights_kernel,
        out_shape=(
            shape(2, 192, 256),
            shape(1152, 256),
            shape(1152, 256),
            shape(2304, 256),
            shape(4, 1024, 256),
            shape(2304, 256),
            shape(4, 1024, 256),
            shape(16, 256),
        ),
        in_specs=[VMEM] * 6,
        out_specs=(VMEM,) * 8,
        scratch_shapes=[pltpu.VMEM((27, 96, 256), F32)],
        compiler_params=pltpu.CompilerParams(vmem_limit_bytes=32 * 2**20),
        cost_estimate=pl.CostEstimate(
            flops=2 * 10**9, bytes_accessed=9 * 10**6, transcendentals=0
        ),
    )(
        first_weight.transpose(1, 2, 3, 4, 0).reshape(9, 3, 16),
        down_weight.transpose(2, 3, 4, 1, 0).reshape(27, 16, 32),
        coarse_weight.transpose(2, 3, 4, 1, 0).reshape(27, 32, 64),
        middle_weight.transpose(2, 3, 4, 0, 1).reshape(27, 32, 96),
        fine_weight.transpose(2, 3, 4, 0, 1).reshape(27, 16, 48),
        head_weight.reshape(1, 16),
    )

    count = lax.axis_size("gy")
    low = lax.ppermute(noisy_field, "gy", [(i, i + 1) for i in range(count - 1)])
    high = lax.ppermute(noisy_field, "gy", [(i + 1, i) for i in range(count - 1)])
    own = pl.pallas_call(
        join_kernel,
        out_shape=shape(128, 256),
        in_specs=[VMEM] * 3,
        out_specs=VMEM,
    )(noisy_field, high, low)

    count = lax.axis_size("gx")
    inner = [(i, i ^ 1) for i in range(count)]
    outer = [(i, ((i + 1) ^ 1) - 1) for i in range(1, count - 1)]
    swap_in = lax.ppermute(own, "gx", inner)
    swap_out = lax.ppermute(own, "gx", outer)
    low2 = lax.ppermute(own[80:], "gx", [(i, i + 2) for i in range(count - 2)])
    high2 = lax.ppermute(own[:48], "gx", [(i + 2, i) for i in range(count - 2)])

    return pl.pallas_call(
        net_kernel,
        out_shape=shape(16, 8, 128, kind=F32),
        in_specs=[VMEM] * 13,
        out_specs=VMEM,
        scratch_shapes=[
            pltpu.VMEM((6, 10, 32, 256), BF),
            pltpu.VMEM((4, 14, J, 128), BF),
            pltpu.VMEM((4, 8, J, 256), BF),
            pltpu.VMEM((3, 6, J, 128), BF),
            pltpu.VMEM((3, 4, J, 256), BF),
            pltpu.VMEM((4, 6, 32, 256), BF),
            pltpu.VMEM((8, 128, 256), BF),
        ],
        compiler_params=pltpu.CompilerParams(vmem_limit_bytes=40 * 2**20),
        cost_estimate=pl.CostEstimate(
            flops=6 * 10**9, bytes_accessed=9 * 10**6, transcendentals=10**6
        ),
    )(own, swap_in, swap_out, low2, high2, *weights)


def solution(mesh):
    placed = (P(None, "gx", "gy"), P(), P(), P(), P(), P(), P())
    return jax.shard_map(
        body, mesh=mesh, in_specs=placed, out_specs=P(None, "gx", "gy"), check_vma=False
    )
```

profile of v0, /device:TPU:94, one launch (start us, length us, event | category | flops | bytes accessed | tf_op | source)
XLA Modules:
  0.0 46.0 jit_solution(9804997848288684306)
XLA Ops:
  0.0 4.0 %collective-permute-start = (bf16[16,8,128]{2,1,0:T(8,128)(2,1)}, bf16[16,8,128]{2,1,0:T(8,128)(2,1)S(1)}, u32[]{:S(2)}, u32[]{:S(2)}) collective-permute-start(bf16[16,8,128]{2,1,0:T(8,128)(2,1)} %own.1), channel_id=1, source_target_pairs={{1,0},{2,1},{3,2},{4,3},{5,4},{6,5},{7,6},{9,8},{10,9},{11,10},{12... | collective-permute-start | bytes 98312 | tf_op jit(solution)/shard_map/ppermute | solution.py:363
  4.0 1.9 %collective-permute-start.1 = (bf16[16,8,128]{2,1,0:T(8,128)(2,1)}, bf16[16,8,128]{2,1,0:T(8,128)(2,1)S(1)}, u32[]{:S(2)}, u32[]{:S(2)}) collective-permute-start(bf16[16,8,128]{2,1,0:T(8,128)(2,1)} %own.1), channel_id=1, source_target_pairs={{0,1},{1,2},{2,3},{3,4},{4,5},{5,6},{6,7},{8,9},{9,10},{10,11},{11... | collective-permute-start | bytes 98312 | tf_op jit(solution)/shard_map/ppermute | solution.py:362
  5.9 0.1 collective-permute-done.high
  6.0 4.9 %collective-permute-done.1.low = bf16[16,8,128]{2,1,0:T(8,128)(2,1)S(1)} collective-permute-done((bf16[16,8,128]{2,1,0:T(8,128)(2,1)}, bf16[16,8,128]{2,1,0:T(8,128)(2,1)S(1)}, u32[]{:S(2)}, u32[]{:S(2)}) %collective-permute-start.1) | collective-permute-done | bytes 32800 | tf_op jit(solution)/shard_map/ppermute | solution.py:362
  10.9 0.6 %copy-done.8 = bf16[16,8,128]{2,1,0:T(8,128)(2,1)} copy-done((bf16[16,8,128]{2,1,0:T(8,128)(2,1)}, bf16[16,8,128]{2,1,0:T(8,128)(2,1)S(1)}, u32[]{:S(2)}) %copy-start.8) | copy-done | bytes 32792
  11.5 1.6 %shard_map.73.own = bf16[128,256]{1,0:T(8,128)(2,1)} custom-call(bf16[16,8,128]{2,1,0:T(8,128)(2,1)} %own.1, bf16[16,8,128]{2,1,0:T(8,128)(2,1)} %copy-done.7, bf16[16,8,128]{2,1,0:T(8,128)(2,1)} %copy-done.8), custom_call_target="tpu_custom_call" | custom-call | tf_op jit(solution)/shard_map/pallas_call | solution.py:364
  13.1 0.8 %fusion = (bf16[48,256]{1,0:T(8,128)(2,1)S(1)}, bf16[48,256]{1,0:T(8,128)(2,1)S(1)}) fusion(bf16[128,256]{1,0:T(8,128)(2,1)} %shard_map.73.own), kind=kLoop, calls=%fused_computation | loop fusion | bytes 98304 | tf_op jit(solution)/shard_map/slice | solution.py:377
  13.9 1.9 %collective-permute-start.3 = (bf16[128,256]{1,0:T(8,128)(2,1)}, bf16[128,256]{1,0:T(8,128)(2,1)S(1)}, u32[]{:S(2)}, u32[]{:S(2)}) collective-permute-start(bf16[128,256]{1,0:T(8,128)(2,1)} %shard_map.73.own), channel_id=1, source_target_pairs={{8,16},{16,8},{24,32},{32,24},{40,48},{48,40},{56,64},{64,56},{72,... | collective-permute-start | bytes 196616 | tf_op jit(solution)/shard_map/ppermute | solution.py:375
  15.8 3.7 %collective-permute-start.2 = (bf16[128,256]{1,0:T(8,128)(2,1)}, bf16[128,256]{1,0:T(8,128)(2,1)S(1)}, u32[]{:S(2)}, u32[]{:S(2)}) collective-permute-start(bf16[128,256]{1,0:T(8,128)(2,1)} %shard_map.73.own), channel_id=1, source_target_pairs={{0,8},{8,0},{16,24},{24,16},{32,40},{40,32},{48,56},{56,48},{64,72... | collective-permute-start | bytes 196616 | tf_op jit(solution)/shard_map/ppermute | solution.py:374
  19.5 1.9 %collective-permute-start.5 = (bf16[48,256]{1,0:T(8,128)(2,1)S(1)}, bf16[48,256]{1,0:T(8,128)(2,1)S(1)}, u32[]{:S(2)}, u32[]{:S(2)}) collective-permute-start(bf16[48,256]{1,0:T(8,128)(2,1)S(1)} %get-tuple-element.21), channel_id=1, source_target_pairs={{16,0},{24,8},{32,16},{40,24},{48,32},{56,40},{64,48},{72,56},{80,... | collective-permute-start | bytes 73736 | tf_op jit(solution)/shard_map/ppermute | solution.py:377
  21.4 8.1 %collective-permute-start.4 = (bf16[48,256]{1,0:T(8,128)(2,1)S(1)}, bf16[48,256]{1,0:T(8,128)(2,1)S(1)}, u32[]{:S(2)}, u32[]{:S(2)}) collective-permute-start(bf16[48,256]{1,0:T(8,128)(2,1)S(1)} %get-tuple-element.22), channel_id=1, source_target_pairs={{0,16},{8,24},{16,32},{24,40},{32,48},{40,56},{48,64},{56,72},{64,... | collective-permute-start | bytes 73736 | tf_op jit(solution)/shard_map/ppermute | solution.py:376
  29.5 0.0 copy-start.1
  29.6 0.9 %copy-done.1 = bf16[64,32,3,3,3]{0,1,4,3,2:T(8,128)(2,1)S(1)} copy-done((bf16[64,32,3,3,3]{0,1,4,3,2:T(8,128)(2,1)S(1)}, bf16[64,32,3,3,3]{0,1,4,3,2:T(8,128)(2,1)}, u32[]{:S(2)}) %copy-start.1) | copy-done | bytes 110616
  30.5 0.9 %copy-done.2 = bf16[32,96,3,3,3]{1,0,4,3,2:T(8,128)(2,1)S(1)} copy-done((bf16[32,96,3,3,3]{1,0,4,3,2:T(8,128)(2,1)S(1)}, bf16[32,96,3,3,3]{1,0,4,3,2:T(8,128)(2,1)}, u32[]{:S(2)}) %copy-start.2) | copy-done | bytes 165912
  31.4 0.9 %copy-done.3 = bf16[32,16,3,3,3]{0,1,4,3,2:T(8,128)(2,1)S(1)} copy-done((bf16[32,16,3,3,3]{0,1,4,3,2:T(8,128)(2,1)S(1)}, bf16[32,16,3,3,3]{0,1,4,3,2:T(8,128)(2,1)}, u32[]{:S(2)}) %copy-start.3) | copy-done | bytes 27672
  32.3 0.9 %copy-done.4 = bf16[16,48,3,3,3]{1,0,4,3,2:T(8,128)(2,1)S(1)} copy-done((bf16[16,48,3,3,3]{1,0,4,3,2:T(8,128)(2,1)S(1)}, bf16[16,48,3,3,3]{1,0,4,3,2:T(8,128)(2,1)}, u32[]{:S(2)}) %copy-start.4) | copy-done | bytes 41496
  33.2 0.7 %copy-done.5 = bf16[16,1,3,3,3]{0,4,3,2,1:T(4,128)(2,1)S(1)} copy-done((bf16[16,1,3,3,3]{0,4,3,2,1:T(4,128)(2,1)S(1)}, bf16[16,1,3,3,3]{0,4,3,2,1:T(4,128)(2,1)}, u32[]{:S(2)}) %copy-start.5) | copy-done | bytes 888
  33.9 0.7 %copy-done.6 = bf16[16]{0:T(256)(128)(2,1)S(1)} copy-done((bf16[16]{0:T(256)(128)(2,1)S(1)}, bf16[16]{0:T(256)(128)(2,1)}, u32[]{:S(2)}) %copy-start.6) | copy-done | bytes 56
  34.6 2.5 %shard_map.74 = (bf16[2,192,256]{2,1,0:T(8,128)(2,1)S(1)}, bf16[1152,256]{1,0:T(8,128)(2,1)S(1)}, bf16[1152,256]{1,0:T(8,128)(2,1)S(1)}, bf16[2304,256]{1,0:T(8,...) custom-call(bf16[9,3,16]{2,1,0:T(4,128)(2,1)S(1)} %bitcast.20, ...), custom_call_target="tpu_custom_call" | custom-call | flops 2000000000 | bytes 9000000 | tf_op jit(solution)/shard_map/pallas_call | solution.py:333
  37.1 0.0 collective-permute-done.5.high2
  37.1 0.0 collective-permute-done.4.low2
  37.1 0.0 collective-permute-done.3.swap_out
  37.1 0.0 collective-permute-done.2.swap_in
  37.2 8.8 %shard_map.75 = f32[16,8,128]{2,1,0:T(8,128)} custom-call(bf16[128,256]{1,0:T(8,128)(2,1)S(1)} %copy-done, bf16[128,256]{1,0:T(8,128)(2,1)S(1)} %collective-permute-done.2.swap_in, bf16[128,256]{1,0:T(8,128)(2,1)S(1)} %collective-permute-done.3.swap_out, bf16[48,256]{1,0:T(8,128)(2,1)S(1)} %collective-permute-done.4.low2, ...), custom_call_target="tpu_custom_call" | custom-call | flops 6000000000 | bytes 9000000 | tf_op jit(solution)/shard_map/pallas_call | solution.py:379
  (10 shorter events, 0.0 us)
Async XLA Ops:
  0.0 6.0 %collective-permute-start = (bf16[16,8,128]{2,1,0:T(8,128)(2,1)}, bf16[16,8,128]{2,1,0:T(8,128)(2,1)S(1)}, u32[]{:S(2)}, u32[]{:S(2)}) collective-permute-start(bf16[16,8,128]{2,1,0:T(8,128)(2,1)} %own.1), channel_id=1, source_target_pairs={{1,0},{2,1},{3,2},{4,3},{5,4},{6,5},{7,6},{9,8},{10,9},{11,10},{12... | collective-permute-start | bytes 98312 | tf_op jit(solution)/shard_map/ppermute | solution.py:363
  4.0 6.9 %collective-permute-start.1 = (bf16[16,8,128]{2,1,0:T(8,128)(2,1)}, bf16[16,8,128]{2,1,0:T(8,128)(2,1)S(1)}, u32[]{:S(2)}, u32[]{:S(2)}) collective-permute-start(bf16[16,8,128]{2,1,0:T(8,128)(2,1)} %own.1), channel_id=1, source_target_pairs={{0,1},{1,2},{2,3},{3,4},{4,5},{5,6},{6,7},{8,9},{9,10},{10,11},{11... | collective-permute-start | bytes 98312 | tf_op jit(solution)/shard_map/ppermute | solution.py:362
  6.0 4.9 %copy-start.7 = (bf16[16,8,128]{2,1,0:T(8,128)(2,1)}, bf16[16,8,128]{2,1,0:T(8,128)(2,1)S(1)}, u32[]{:S(2)}) copy-start(bf16[16,8,128]{2,1,0:T(8,128)(2,1)S(1)} %collective-permute-done.high) | copy-start | bytes 98308
  10.9 0.6 %copy-start.8 = (bf16[16,8,128]{2,1,0:T(8,128)(2,1)}, bf16[16,8,128]{2,1,0:T(8,128)(2,1)S(1)}, u32[]{:S(2)}) copy-start(bf16[16,8,128]{2,1,0:T(8,128)(2,1)S(1)} %collective-permute-done.1.low) | copy-start | bytes 98308
  13.9 23.2 %collective-permute-start.3 = (bf16[128,256]{1,0:T(8,128)(2,1)}, bf16[128,256]{1,0:T(8,128)(2,1)S(1)}, u32[]{:S(2)}, u32[]{:S(2)}) collective-permute-start(bf16[128,256]{1,0:T(8,128)(2,1)} %shard_map.73.own), channel_id=1, source_target_pairs={{8,16},{16,8},{24,32},{32,24},{40,48},{48,40},{56,64},{64,56},{72,... | collective-permute-start | bytes 196616 | tf_op jit(solution)/shard_map/ppermute | solution.py:375
  15.8 21.3 %collective-permute-start.2 = (bf16[128,256]{1,0:T(8,128)(2,1)}, bf16[128,256]{1,0:T(8,128)(2,1)S(1)}, u32[]{:S(2)}, u32[]{:S(2)}) collective-permute-start(bf16[128,256]{1,0:T(8,128)(2,1)} %shard_map.73.own), channel_id=1, source_target_pairs={{0,8},{8,0},{16,24},{24,16},{32,40},{40,32},{48,56},{56,48},{64,72... | collective-permute-start | bytes 196616 | tf_op jit(solution)/shard_map/ppermute | solution.py:374
  19.5 17.6 %collective-permute-start.5 = (bf16[48,256]{1,0:T(8,128)(2,1)S(1)}, bf16[48,256]{1,0:T(8,128)(2,1)S(1)}, u32[]{:S(2)}, u32[]{:S(2)}) collective-permute-start(bf16[48,256]{1,0:T(8,128)(2,1)S(1)} %get-tuple-element.21), channel_id=1, source_target_pairs={{16,0},{24,8},{32,16},{40,24},{48,32},{56,40},{64,48},{72,56},{80,... | collective-permute-start | bytes 73736 | tf_op jit(solution)/shard_map/ppermute | solution.py:377
  21.4 15.7 %collective-permute-start.4 = (bf16[48,256]{1,0:T(8,128)(2,1)S(1)}, bf16[48,256]{1,0:T(8,128)(2,1)S(1)}, u32[]{:S(2)}, u32[]{:S(2)}) collective-permute-start(bf16[48,256]{1,0:T(8,128)(2,1)S(1)} %get-tuple-element.22), channel_id=1, source_target_pairs={{0,16},{8,24},{16,32},{24,40},{32,48},{40,56},{48,64},{56,72},{64,... | collective-permute-start | bytes 73736 | tf_op jit(solution)/shard_map/ppermute | solution.py:376
  29.5 0.9 %copy-start.1 = (bf16[64,32,3,3,3]{0,1,4,3,2:T(8,128)(2,1)S(1)}, bf16[64,32,3,3,3]{0,1,4,3,2:T(8,128)(2,1)}, u32[]{:S(2)}) copy-start(bf16[64,32,3,3,3]{0,1,4,3,2:T(8,128)(2,1)} %param.10) | copy-start | bytes 331780
  30.5 0.9 %copy-start.2 = (bf16[32,96,3,3,3]{1,0,4,3,2:T(8,128)(2,1)S(1)}, bf16[32,96,3,3,3]{1,0,4,3,2:T(8,128)(2,1)}, u32[]{:S(2)}) copy-start(bf16[32,96,3,3,3]{1,0,4,3,2:T(8,128)(2,1)} %param.11) | copy-start | bytes 497668
  31.4 0.9 %copy-start.3 = (bf16[32,16,3,3,3]{0,1,4,3,2:T(8,128)(2,1)S(1)}, bf16[32,16,3,3,3]{0,1,4,3,2:T(8,128)(2,1)}, u32[]{:S(2)}) copy-start(bf16[32,16,3,3,3]{0,1,4,3,2:T(8,128)(2,1)} %param.9) | copy-start | bytes 82948
  32.3 0.9 %copy-start.4 = (bf16[16,48,3,3,3]{1,0,4,3,2:T(8,128)(2,1)S(1)}, bf16[16,48,3,3,3]{1,0,4,3,2:T(8,128)(2,1)}, u32[]{:S(2)}) copy-start(bf16[16,48,3,3,3]{1,0,4,3,2:T(8,128)(2,1)} %param.12) | copy-start | bytes 124420
  33.2 0.7 %copy-start.5 = (bf16[16,1,3,3,3]{0,4,3,2,1:T(4,128)(2,1)S(1)}, bf16[16,1,3,3,3]{0,4,3,2,1:T(4,128)(2,1)}, u32[]{:S(2)}) copy-start(bf16[16,1,3,3,3]{0,4,3,2,1:T(4,128)(2,1)} %param.8) | copy-start | bytes 2596
  33.9 0.7 %copy-start.6 = (bf16[16]{0:T(256)(128)(2,1)S(1)}, bf16[16]{0:T(256)(128)(2,1)}, u32[]{:S(2)}) copy-start(bf16[16]{0:T(256)(128)(2,1)} %param.13) | copy-start | bytes 100
  34.6 2.6 %copy-start = (bf16[128,256]{1,0:T(8,128)(2,1)S(1)}, bf16[128,256]{1,0:T(8,128)(2,1)}, u32[]{:S(2)}) copy-start(bf16[128,256]{1,0:T(8,128)(2,1)} %shard_map.73.own) | copy-start | bytes 196612
where the time goes:
time: 46.5 us; the launch traced here: 46 us
  starting transfers between devices  21.6 us (46%)
  Pallas kernels  12.9 us (28%)
  local copies, waits for them, and re-layouts  6.39 us (14%)
  waiting for transfers between devices  5 us (11%)
    pallas_call x1, Pallas kernels, body(): pl.pallas_call(net_kernel, out_shape=shape(16, 8, 128, kind=F32), in_spec...  8.84 us
    ppermute x1, starting transfers between devices, body(): low2 = lax.ppermute(own[80:], 'gx', [(i, i + 2) for i in range(count - 2)])  8.14 us
    unnamed x18, local copies, waits for them, and re-layouts  5.64 us
    ppermute x1, waiting for transfers between devices, body(): lax.ppermute(noisy_field, 'gy', [(i, i + 1) for i in range(count - 1)])  4.91 us
    ppermute x1, starting transfers between devices, body(): lax.ppermute(noisy_field, 'gy', [(i + 1, i) for i in range(count - 1)])  3.99 us
    ppermute x1, starting transfers between devices, body(): swap_in = lax.ppermute(own, 'gx', inner)  3.69 us
    pallas_call x1, Pallas kernels, body(): pl.pallas_call(weights_kernel, out_shape=(shape(2, 192, 256), shape(1152,...  2.52 us
    ppermute x1, starting transfers between devices, body(): lax.ppermute(noisy_field, 'gy', [(i, i + 1) for i in range(count - 1)])  1.92 us
  transfers between devices with their start and end apart: 6, of which 2 were waited for; matrix products, arithmetic and copies ran while one was open for 0% of the time, Pallas kernels for 5%

commit v1 on v0

--- a/solution.py
+++ b/solution.py
@@ -9,6 +9,7 @@
 F32 = jnp.float32
 J = 48
 VMEM = pl.BlockSpec(memory_space=pltpu.VMEM)
+ANY = pl.BlockSpec(memory_space=pl.ANY)
 
 
 def dot(a, b):
@@ -58,12 +59,20 @@
 SETS = (((0,), (1, 2)), ((0, 1), (2,)))
 
 
-def weights_kernel(
-    first, down, coarse, middle, fine, head,
-    w_first, w_down, w_coarse, w_mid_skip, w_mid_up, w_fine_skip, w_fine_up, w_head,
-    tiled,
-):
+def weights_kernel(*refs):
+    raw, refs = refs[:6], refs[6:]
+    w_first, w_down, w_coarse, w_mid_skip, w_mid_up, w_fine_skip, w_fine_up, w_head = refs[:8]
+    tiled, sems = refs[8], refs[-1]
+    first, down, coarse, middle, fine, head = refs[9:15]
+    copies = [
+        pltpu.make_async_copy(source, target, sems.at[at])
+        for at, (source, target) in enumerate(zip(raw, refs[9:15]))
+    ]
+    for copy in copies:
+        copy.start()
     r16, r32, r64 = repeat_matrix(16), repeat_matrix(32), repeat_matrix(64)
+    for copy in copies:
+        copy.wait()
 
     w_first[...] = jnp.zeros_like(w_first)
     for dx in range(3):
@@ -135,7 +144,7 @@
     w_head[...] = jnp.where(iota((16, 256), 1) // 16 == iota((16, 256), 0), row, 0.0).astype(BF)
 
 
-def join_kernel(own, high, low, out):
+def join_kernel(own, high, low, after, out, first_rows, last_rows):
     near = iota((128, 128), 1) < 64
     mine = own[...].astype(F32).reshape(128, 128)
     rim = jnp.where(
@@ -144,7 +153,10 @@
     both = jnp.concatenate([mine, rim], axis=1).astype(BF)
     row, col = iota((128, 128), 0), iota((128, 128), 1)
     swap = (col == (row % 16) * 8 + row // 16).astype(BF)
-    out[...] = dot(swap, both).astype(BF)
+    rows = dot(swap, both).astype(BF)
+    out[...] = rows
+    first_rows[...] = rows[:48]
+    last_rows[...] = rows[80:]
 
 
 def silu_half(h):
@@ -342,39 +354,55 @@
             shape(4, 1024, 256),
             shape(16, 256),
         ),
-        in_specs=[VMEM] * 6,
+        in_specs=[ANY] * 6,
         out_specs=(VMEM,) * 8,
-        scratch_shapes=[pltpu.VMEM((27, 96, 256), F32)],
+        scratch_shapes=[
+            pltpu.VMEM((27, 96, 256), F32),
+            pltpu.VMEM((9, 3, 16), BF),
+            pltpu.VMEM((27, 16, 32), BF),
+            pltpu.VMEM((27, 32, 64), BF),
+            pltpu.VMEM((27, 32, 96), BF),
+            pltpu.VMEM((27, 16, 48), BF),
+            pltpu.VMEM((1, 16), BF),
+            pltpu.SemaphoreType.DMA((6,)),
+        ],
         compiler_params=pltpu.CompilerParams(vmem_limit_bytes=32 * 2**20),
         cost_estimate=pl.CostEstimate(
             flops=2 * 10**9, bytes_accessed=9 * 10**6, transcendentals=0
         ),
     )(
-        first_weight.transpose(1, 2, 3, 4, 0).reshape(9, 3, 16),
-        down_weight.transpose(2, 3, 4, 1, 0).reshape(27, 16, 32),
-        coarse_weight.transpose(2, 3, 4, 1, 0).reshape(27, 32, 64),
-        middle_weight.transpose(2, 3, 4, 0, 1).reshape(27, 32, 96),
-        fine_weight.transpose(2, 3, 4, 0, 1).reshape(27, 16, 48),
-        head_weight.reshape(1, 16),
+        *(
+            pltpu.with_memory_space_constraint(weight, pltpu.HBM)
+            for weight in (
+                first_weight.transpose(1, 2, 3, 4, 0).reshape(9, 3, 16),
+                down_weight.transpose(2, 3, 4, 1, 0).reshape(27, 16, 32),
+                coarse_weight.transpose(2, 3, 4, 1, 0).reshape(27, 32, 64),
+                middle_weight.transpose(2, 3, 4, 0, 1).reshape(27, 32, 96),
+                fine_weight.transpose(2, 3, 4, 0, 1).reshape(27, 16, 48),
+                head_weight.reshape(1, 16),
+            )
+        )
     )
 
     count = lax.axis_size("gy")
     low = lax.ppermute(noisy_field, "gy", [(i, i + 1) for i in range(count - 1)])
     high = lax.ppermute(noisy_field, "gy", [(i + 1, i) for i in range(count - 1)])
-    own = pl.pallas_call(
+    own, first_rows, last_rows = pl.pallas_call(
         join_kernel,
-        out_shape=shape(128, 256),
-        in_specs=[VMEM] * 3,
-        out_specs=VMEM,
-    )(noisy_field, high, low)
+        out_shape=(shape(128, 256), shape(48, 256), shape(48, 256)),
+        in_specs=[VMEM] * 3 + [ANY],
+        out_specs=(VMEM,) * 3,
+        compiler_params=pltpu.CompilerParams(vmem_limit_bytes=4 * 2**20),
+        cost_estimate=pl.CostEstimate(flops=10**7, bytes_accessed=2 * 10**5, transcendentals=0),
+    )(noisy_field, high, low, weights[-1])
 
     count = lax.axis_size("gx")
     inner = [(i, i ^ 1) for i in range(count)]
     outer = [(i, ((i + 1) ^ 1) - 1) for i in range(1, count - 1)]
     swap_in = lax.ppermute(own, "gx", inner)
     swap_out = lax.ppermute(own, "gx", outer)
-    low2 = lax.ppermute(own[80:], "gx", [(i, i + 2) for i in range(count - 2)])
-    high2 = lax.ppermute(own[:48], "gx", [(i + 2, i) for i in range(count - 2)])
+    low2 = lax.ppermute(last_rows, "gx", [(i, i + 2) for i in range(count - 2)])
+    high2 = lax.ppermute(first_rows, "gx", [(i + 2, i) for i in range(count - 2)])
 
     return pl.pallas_call(
         net_kernel,

time: 46.5 us -> 39 us (0.84)
  local copies, waits for them, and re-layouts: 6.39 us -> 0.01 us
  starting transfers between devices: 21.6 us -> 17.4 us
  waiting for transfers between devices: 5 us -> 8.69 us
    ppermute x2, waiting for transfers between devices: 0.01 us -> 7.48 us  [the longest x1 7.48 us: body(): lax.ppermute(first_rows, 'gx', [(i + 2, i) for i in range(count - 2)])]
    unnamed x18 -> x2, local copies, waits for them, and re-layouts: 5.64 us -> 0.01 us
    ppermute x2, starting transfers between devices: 10 us -> 5.83 us  [the longest x1 3.39 us: body(): low2 = lax.ppermute(last_rows, 'gx', [(i, i + 2) for i in range(count - 2)])]
    ppermute x1, waiting for transfers between devices: 4.91 us -> 1.2 us  [body(): lax.ppermute(noisy_field, 'gy', [(i, i + 1) for i in range(count - 1)])]
    pallas_call x1, Pallas kernels: 1.58 us -> 0.15 us  [body(): pl.pallas_call(join_kernel, out_shape=(shape(128, 256), shape(48, 256), s...]
    pallas_call x1, Pallas kernels: 2.52 us -> 3.76 us  [body(): pl.pallas_call(weights_kernel, out_shape=(shape(2, 192, 256), shape(1152,...]
    slice x1 -> x0, local copies, waits for them, and re-layouts: 0.76 us -> none  [body(): high2 = lax.ppermute(own[:48], 'gx', [(i + 2, i) for i in range(count - 2)])]
  transfers between devices with their start and end apart: 6 -> 6, of which waited for: 2 -> 2; matrix products, arithmetic and copies ran while one was open for 0% -> 0% of each run, Pallas kernels for 5% -> 10%
where the time goes in v1:
time: 39 us; the launch traced here: 38.8 us
  starting transfers between devices  17.4 us (45%)
  Pallas kernels  12.7 us (33%)
  waiting for transfers between devices  8.69 us (22%)
    pallas_call x1, Pallas kernels, body(): pl.pallas_call(net_kernel, out_shape=shape(16, 8, 128, kind=F32), in_spec...  8.77 us
    ppermute x1, waiting for transfers between devices, body(): lax.ppermute(first_rows, 'gx', [(i + 2, i) for i in range(count - 2)])  7.48 us
    ppermute x1, starting transfers between devices, body(): lax.ppermute(noisy_field, 'gy', [(i + 1, i) for i in range(count - 1)])  3.99 us
    pallas_call x1, Pallas kernels, body(): pl.pallas_call(weights_kernel, out_shape=(shape(2, 192, 256), shape(1152,...  3.76 us
    ppermute x1, starting transfers between devices, body(): swap_in = lax.ppermute(own, 'gx', inner)  3.69 us
    ppermute x1, starting transfers between devices, body(): low2 = lax.ppermute(last_rows, 'gx', [(i, i + 2) for i in range(count - 2)])  3.39 us
    ppermute x1, starting transfers between devices, body(): lax.ppermute(first_rows, 'gx', [(i + 2, i) for i in range(count - 2)])  2.44 us
    ppermute x1, starting transfers between devices, body(): swap_out = lax.ppermute(own, 'gx', outer)  1.92 us
  transfers between devices with their start and end apart: 6, of which 2 were waited for; matrix products, arithmetic and copies ran while one was open for 0% of the time, Pallas kernels for 10%

profile of v1, /device:TPU:94, one launch (start us, length us, event | category | flops | bytes accessed | tf_op | source)
XLA Modules:
  0.0 38.8 jit_solution(16224304163069002327)
XLA Ops:
  0.0 4.0 %collective-permute-start = (bf16[16,8,128]{2,1,0:T(8,128)(2,1)}, bf16[16,8,128]{2,1,0:T(8,128)(2,1)S(1)}, u32[]{:S(2)}, u32[]{:S(2)}) collective-permute-start(bf16[16,8,128]{2,1,0:T(8,128)(2,1)} %own.1), channel_id=1, source_target_pairs={{1,0},{2,1},{3,2},{4,3},{5,4},{6,5},{7,6},{9,8},{10,9},{11,10},{12... | collective-permute-start | bytes 98312 | tf_op jit(solution)/shard_map/ppermute | solution.py:389
  4.0 1.9 %collective-permute-start.1 = (bf16[16,8,128]{2,1,0:T(8,128)(2,1)}, bf16[16,8,128]{2,1,0:T(8,128)(2,1)S(1)}, u32[]{:S(2)}, u32[]{:S(2)}) collective-permute-start(bf16[16,8,128]{2,1,0:T(8,128)(2,1)} %own.1), channel_id=1, source_target_pairs={{0,1},{1,2},{2,3},{3,4},{4,5},{5,6},{6,7},{8,9},{9,10},{10,11},{11... | collective-permute-start | bytes 98312 | tf_op jit(solution)/shard_map/ppermute | solution.py:388
  5.9 0.0 copy-start
  5.9 3.8 %shard_map.73 = (bf16[2,192,256]{2,1,0:T(8,128)(2,1)S(1)}, bf16[1152,256]{1,0:T(8,128)(2,1)S(1)}, bf16[1152,256]{1,0:T(8,128)(2,1)S(1)}, bf16[2304,256]{1,0:T(8,...) custom-call(bf16[9,3,16]{2,1,0:T(4,128)(2,1)} %bitcast.20, ...), custom_call_target="tpu_custom_call" | custom-call | flops 2000000000 | bytes 9000000 | tf_op jit(solution)/shard_map/pallas_call | solution.py:345
  9.7 0.0 collective-permute-done.high
  9.7 1.2 %collective-permute-done.1.low = bf16[16,8,128]{2,1,0:T(8,128)(2,1)S(1)} collective-permute-done((bf16[16,8,128]{2,1,0:T(8,128)(2,1)}, bf16[16,8,128]{2,1,0:T(8,128)(2,1)S(1)}, u32[]{:S(2)}, u32[]{:S(2)}) %collective-permute-start.1) | collective-permute-done | bytes 32800 | tf_op jit(solution)/shard_map/ppermute | solution.py:388
  10.9 0.0 copy-done
  10.9 0.2 shard_map.74
  11.1 1.9 %collective-permute-start.3 = (bf16[128,256]{1,0:T(8,128)(2,1)S(1)}, bf16[128,256]{1,0:T(8,128)(2,1)S(1)}, u32[]{:S(2)}, u32[]{:S(2)}) collective-permute-start(bf16[128,256]{1,0:T(8,128)(2,1)S(1)} %get-tuple-element.17.own), channel_id=1, source_target_pairs={{8,16},{16,8},{24,32},{32,24},{40,48},{48,40},{56,64},{64,56},{72,... | collective-permute-start | bytes 196616 | tf_op jit(solution)/shard_map/ppermute | solution.py:403
  13.0 3.7 %collective-permute-start.2 = (bf16[128,256]{1,0:T(8,128)(2,1)S(1)}, bf16[128,256]{1,0:T(8,128)(2,1)S(1)}, u32[]{:S(2)}, u32[]{:S(2)}) collective-permute-start(bf16[128,256]{1,0:T(8,128)(2,1)S(1)} %get-tuple-element.17.own), channel_id=1, source_target_pairs={{0,8},{8,0},{16,24},{24,16},{32,40},{40,32},{48,56},{56,48},{64,72... | collective-permute-start | bytes 196616 | tf_op jit(solution)/shard_map/ppermute | solution.py:402
  16.7 3.4 %collective-permute-start.4 = (bf16[48,256]{1,0:T(8,128)(2,1)S(1)}, bf16[48,256]{1,0:T(8,128)(2,1)S(1)}, u32[]{:S(2)}, u32[]{:S(2)}) collective-permute-start(bf16[48,256]{1,0:T(8,128)(2,1)S(1)} %get-tuple-element.18), channel_id=1, source_target_pairs={{0,16},{8,24},{16,32},{24,40},{32,48},{40,56},{48,64},{56,72},{64,... | collective-permute-start | bytes 73736 | tf_op jit(solution)/shard_map/ppermute | solution.py:404
  20.1 2.4 %collective-permute-start.5 = (bf16[48,256]{1,0:T(8,128)(2,1)S(1)}, bf16[48,256]{1,0:T(8,128)(2,1)S(1)}, u32[]{:S(2)}, u32[]{:S(2)}) collective-permute-start(bf16[48,256]{1,0:T(8,128)(2,1)S(1)} %get-tuple-element.19), channel_id=1, source_target_pairs={{16,0},{24,8},{32,16},{40,24},{48,32},{56,40},{64,48},{72,56},{80,... | collective-permute-start | bytes 73736 | tf_op jit(solution)/shard_map/ppermute | solution.py:405
  22.5 0.0 collective-permute-done.4.low2
  22.6 7.5 %collective-permute-done.5.high2 = bf16[48,256]{1,0:T(8,128)(2,1)S(1)} collective-permute-done((bf16[48,256]{1,0:T(8,128)(2,1)S(1)}, bf16[48,256]{1,0:T(8,128)(2,1)S(1)}, u32[]{:S(2)}, u32[]{:S(2)}) %collective-permute-start.5) | collective-permute-done | bytes 24608 | tf_op jit(solution)/shard_map/ppermute | solution.py:405
  30.0 0.0 collective-permute-done.3.swap_out
  30.0 0.0 collective-permute-done.2.swap_in
  30.0 8.8 %shard_map.75 = f32[16,8,128]{2,1,0:T(8,128)} custom-call(bf16[128,256]{1,0:T(8,128)(2,1)S(1)} %get-tuple-element.17.own, bf16[128,256]{1,0:T(8,128)(2,1)S(1)} %collective-permute-done.2.swap_in, bf16[128,256]{1,0:T(8,128)(2,1)S(1)} %collective-permute-done.3.swap_out, bf16[48,256]{1,0:T(8,128)(2,1)S(1)} %collective-permute-done.4.low2, ...), custom_call_target="tpu_custom_call" | custom-call | flops 6000000000 | bytes 9000000 | tf_op jit(solution)/shard_map/pallas_call | solution.py:407
Async XLA Ops:
  0.0 9.7 %collective-permute-start = (bf16[16,8,128]{2,1,0:T(8,128)(2,1)}, bf16[16,8,128]{2,1,0:T(8,128)(2,1)S(1)}, u32[]{:S(2)}, u32[]{:S(2)}) collective-permute-start(bf16[16,8,128]{2,1,0:T(8,128)(2,1)} %own.1), channel_id=1, source_target_pairs={{1,0},{2,1},{3,2},{4,3},{5,4},{6,5},{7,6},{9,8},{10,9},{11,10},{12... | collective-permute-start | bytes 98312 | tf_op jit(solution)/shard_map/ppermute | solution.py:389
  4.0 6.9 %collective-permute-start.1 = (bf16[16,8,128]{2,1,0:T(8,128)(2,1)}, bf16[16,8,128]{2,1,0:T(8,128)(2,1)S(1)}, u32[]{:S(2)}, u32[]{:S(2)}) collective-permute-start(bf16[16,8,128]{2,1,0:T(8,128)(2,1)} %own.1), channel_id=1, source_target_pairs={{0,1},{1,2},{2,3},{3,4},{4,5},{5,6},{6,7},{8,9},{9,10},{10,11},{11... | collective-permute-start | bytes 98312 | tf_op jit(solution)/shard_map/ppermute | solution.py:388
  5.9 5.0 %copy-start = (bf16[16,8,128]{2,1,0:T(8,128)(2,1)S(1)}, bf16[16,8,128]{2,1,0:T(8,128)(2,1)}, u32[]{:S(2)}) copy-start(bf16[16,8,128]{2,1,0:T(8,128)(2,1)} %own.1) | copy-start | bytes 98308
  11.1 19.0 %collective-permute-start.3 = (bf16[128,256]{1,0:T(8,128)(2,1)S(1)}, bf16[128,256]{1,0:T(8,128)(2,1)S(1)}, u32[]{:S(2)}, u32[]{:S(2)}) collective-permute-start(bf16[128,256]{1,0:T(8,128)(2,1)S(1)} %get-tuple-element.17.own), channel_id=1, source_target_pairs={{8,16},{16,8},{24,32},{32,24},{40,48},{48,40},{56,64},{64,56},{72,... | collective-permute-start | bytes 196616 | tf_op jit(solution)/shard_map/ppermute | solution.py:403
  13.0 17.0 %collective-permute-start.2 = (bf16[128,256]{1,0:T(8,128)(2,1)S(1)}, bf16[128,256]{1,0:T(8,128)(2,1)S(1)}, u32[]{:S(2)}, u32[]{:S(2)}) collective-permute-start(bf16[128,256]{1,0:T(8,128)(2,1)S(1)} %get-tuple-element.17.own), channel_id=1, source_target_pairs={{0,8},{8,0},{16,24},{24,16},{32,40},{40,32},{48,56},{56,48},{64,72... | collective-permute-start | bytes 196616 | tf_op jit(solution)/shard_map/ppermute | solution.py:402
  16.7 5.8 %collective-permute-start.4 = (bf16[48,256]{1,0:T(8,128)(2,1)S(1)}, bf16[48,256]{1,0:T(8,128)(2,1)S(1)}, u32[]{:S(2)}, u32[]{:S(2)}) collective-permute-start(bf16[48,256]{1,0:T(8,128)(2,1)S(1)} %get-tuple-element.18), channel_id=1, source_target_pairs={{0,16},{8,24},{16,32},{24,40},{32,48},{40,56},{48,64},{56,72},{64,... | collective-permute-start | bytes 73736 | tf_op jit(solution)/shard_map/ppermute | solution.py:404
  20.1 9.9 %collective-permute-start.5 = (bf16[48,256]{1,0:T(8,128)(2,1)S(1)}, bf16[48,256]{1,0:T(8,128)(2,1)S(1)}, u32[]{:S(2)}, u32[]{:S(2)}) collective-permute-start(bf16[48,256]{1,0:T(8,128)(2,1)S(1)} %get-tuple-element.19), channel_id=1, source_target_pairs={{16,0},{24,8},{32,16},{40,24},{48,32},{56,40},{64,48},{72,56},{80,... | collective-permute-start | bytes 73736 | tf_op jit(solution)/shard_map/ppermute | solution.py:405

commit v2 on v1

--- a/solution.py
+++ b/solution.py
@@ -59,19 +59,61 @@
 SETS = (((0,), (1, 2)), ((0, 1), (2,)))
 
 
-def weights_kernel(*refs):
-    raw, refs = refs[:6], refs[6:]
-    w_first, w_down, w_coarse, w_mid_skip, w_mid_up, w_fine_skip, w_fine_up, w_head = refs[:8]
-    tiled, sems = refs[8], refs[-1]
-    first, down, coarse, middle, fine, head = refs[9:15]
+def banded(out, taps, channels, row_depths, depth_of):
+    size = channels * len(row_depths)
+    for at, depth in enumerate(row_depths):
+        masks = band_masks(channels, depth, depth_of)
+        for xy in range(9):
+            block = sum(masks[dz] * taps[dz][xy] for dz in range(3))
+            out[pl.ds(xy * size + at * channels, channels), :] = block
+
+
+def folded(out, get, channels, depths, depth_of):
+    size = channels * depths
+    place = depth_of(iota((channels, 256), 1))
+    even = place % 2 == 0
+    masks = [up_masks(channels, depth, depth_of) for depth in range(depths)]
+    for px in range(2):
+        for tx in range(2):
+            by_y = [
+                [sum(get(dz, dx, dy) for dx in SETS[px][tx]) for dy in range(3)]
+                for dz in range(3)
+            ]
+            for py in range(2):
+                for ty in range(2):
+                    w0, w1, w2 = [
+                        sum(by_y[dz][dy] for dy in SETS[py][ty]) for dz in range(3)
+                    ]
+                    inner = jnp.where(even, w1 + w2, w0 + w1).astype(BF)
+                    outer = jnp.where(even, w0, w2).astype(BF)
+                    for depth in range(depths):
+                        block = masks[depth][0] * inner + masks[depth][1] * outer
+                        at = (tx * 2 + ty) * size + depth * channels
+                        out[px * 2 + py, pl.ds(at, channels), :] = block
+
+
+def encoder_weights_kernel(
+    raw_first, raw_down, raw_coarse, raw_middle, raw_fine, raw_head,
+    w_first, w_down, w_coarse, w_head, middle, fine,
+    first, down, coarse, head, sems,
+):
     copies = [
         pltpu.make_async_copy(source, target, sems.at[at])
-        for at, (source, target) in enumerate(zip(raw, refs[9:15]))
+        for at, (source, target) in enumerate(
+            (
+                (raw_first, first),
+                (raw_down, down),
+                (raw_coarse, coarse),
+                (raw_head, head),
+                (raw_middle, middle),
+                (raw_fine, fine),
+            )
+        )
     ]
     for copy in copies:
         copy.start()
     r16, r32, r64 = repeat_matrix(16), repeat_matrix(32), repeat_matrix(64)
-    for copy in copies:
+    for copy in copies[:4]:
         copy.wait()
 
     w_first[...] = jnp.zeros_like(w_first)
@@ -87,37 +129,6 @@
             for even in range(2):
                 w_first[even, pl.ds(dy * 64 + (even + dx) * 16, 16), :] = block
 
-    def banded(out, taps, channels, row_depths, depth_of):
-        size = channels * len(row_depths)
-        for at, depth in enumerate(row_depths):
-            masks = band_masks(channels, depth, depth_of)
-            for xy in range(9):
-                block = sum(masks[dz] * taps[dz][xy] for dz in range(3))
-                out[pl.ds(xy * size + at * channels, channels), :] = block
-
-    def folded(out, get, channels, depths, depth_of):
-        size = channels * depths
-        place = depth_of(iota((channels, 256), 1))
-        even = place % 2 == 0
-        masks = [up_masks(channels, depth, depth_of) for depth in range(depths)]
-        for px in range(2):
-            for tx in range(2):
-                by_y = [
-                    [sum(get(dz, dx, dy) for dx in SETS[px][tx]) for dy in range(3)]
-                    for dz in range(3)
-                ]
-                for py in range(2):
-                    for ty in range(2):
-                        w0, w1, w2 = [
-                            sum(by_y[dz][dy] for dy in SETS[py][ty]) for dz in range(3)
-                        ]
-                        inner = jnp.where(even, w1 + w2, w0 + w1).astype(BF)
-                        outer = jnp.where(even, w0, w2).astype(BF)
-                        for depth in range(depths):
-                            block = masks[depth][0] * inner + masks[depth][1] * outer
-                            at = (tx * 2 + ty) * size + depth * channels
-                            out[px * 2 + py, pl.ds(at, channels), :] = block
-
     flat = down[...].reshape(27 * 16, 32)
     all_taps = (dot(flat, r32) * (1 / 16)).astype(BF)
     taps = [[all_taps[(dz * 9 + xy) * 16 : (dz * 9 + xy + 1) * 16] for xy in range(9)] for dz in range(3)]
@@ -128,6 +139,16 @@
     taps = [[all_taps[(dz * 9 + xy) * 32 : (dz * 9 + xy + 1) * 32] for xy in range(9)] for dz in range(3)]
     banded(w_coarse, taps, 32, list(range(4)), natural(64))
 
+    row = dot(jnp.broadcast_to(head[...], (16, 16)), r16)
+    w_head[...] = jnp.where(iota((16, 256), 1) // 16 == iota((16, 256), 0), row, 0.0).astype(BF)
+    for copy in copies[4:]:
+        copy.wait()
+
+
+def decoder_weights_kernel(
+    middle, fine, after, w_mid_skip, w_mid_up, w_fine_skip, w_fine_up, tiled
+):
+    r16, r32 = repeat_matrix(16), repeat_matrix(32)
     for tap in range(27):
         tiled[tap] = dot_tn(middle[tap], r32) * 0.5
     taps = [[tiled[dz * 9 + xy, 64:96, :].astype(BF) for xy in range(9)] for dz in range(3)]
@@ -140,11 +161,8 @@
     banded(w_fine_skip, taps, 16, list(range(0, 16, 2)) + list(range(1, 16, 2)), natural(16))
     folded(w_fine_up, lambda dz, dx, dy: tiled[dz * 9 + dx * 3 + dy, 0:32, :], 32, 8, natural(16))
 
-    row = dot(jnp.broadcast_to(head[...], (16, 16)), r16)
-    w_head[...] = jnp.where(iota((16, 256), 1) // 16 == iota((16, 256), 0), row, 0.0).astype(BF)
-
-
-def join_kernel(own, high, low, after, out, first_rows, last_rows):
+
+def join_kernel(own, high, low, after, out):
     near = iota((128, 128), 1) < 64
     mine = own[...].astype(F32).reshape(128, 128)
     rim = jnp.where(
@@ -153,10 +171,19 @@
     both = jnp.concatenate([mine, rim], axis=1).astype(BF)
     row, col = iota((128, 128), 0), iota((128, 128), 1)
     swap = (col == (row % 16) * 8 + row // 16).astype(BF)
-    rows = dot(swap, both).astype(BF)
-    out[...] = rows
-    first_rows[...] = rows[:48]
-    last_rows[...] = rows[80:]
+    out[...] = dot(swap, both).astype(BF)
+
+
+def chip_edge_kernel(own, twin, out):
+    odd = lax.axis_index("gx") % 2 == 1
+    for_high = jnp.concatenate([twin[80:], own[...]], axis=0)
+    for_low = jnp.concatenate([own[...], twin[:48]], axis=0)
+    out[...] = jnp.where(odd, for_high, for_low)
+
+
+def twin_edge_kernel(edge, after, out):
+    odd = lax.axis_index("gx") % 2 == 1
+    out[...] = jnp.where(odd, edge[:48], edge[128:])
 
 
 def silu_half(h):
@@ -164,7 +191,7 @@
 
 
 def net_kernel(
-    own, swap_in, swap_out, low2, high2,
+    own, twin, chip_edge, twin_edge,
     w_first, w_down, w_coarse, w_mid_skip, w_mid_up, w_fine_skip, w_fine_up, w_head,
     out,
     fine_s, pool_fine_s, mid_s, pool_mid_s, coarse_s, up_s, last_s,
@@ -182,13 +209,12 @@
     at_y = gy * 32 + cell_of(iota((J, 256), 0))
     y_mask = jnp.where((at_y >= 0) & (at_y < cells_y), 1.0, 0.0)
 
-    odd = gx % 2 == 1
-    inner, outer = swap_in[...], swap_out[...]
-    flag = jnp.where(odd, 1.0, 0.0).astype(BF)
-    keep = jnp.where(odd, 0.0, 1.0).astype(BF)
-    low1 = inner * flag + outer * keep
-    high1 = inner * keep + outer * flag
-    field = jnp.concatenate([low2[...], low1, own[...], high1, high2[...]], axis=0)
+    mine, other, edge, rest = own[...], twin[...], chip_edge[...], twin_edge[...]
+    field = jnp.where(
+        gx % 2 == 1,
+        jnp.concatenate([rest, other, mine, edge], axis=0),
+        jnp.concatenate([edge, mine, other, rest], axis=0),
+    )
     wide = field.astype(F32)
     shifted = [
         pltpu.roll(wide, 1, 1).astype(BF),
@@ -342,34 +368,33 @@
     def shape(*dims, kind=BF):
         return jax.ShapeDtypeStruct(dims, kind)
 
-    weights = pl.pallas_call(
-        weights_kernel,
+    def cost(flops, moved):
+        return pl.CostEstimate(flops=flops, bytes_accessed=moved, transcendentals=0)
+
+    def small(limit):
+        return pltpu.CompilerParams(vmem_limit_bytes=limit * 2**20)
+
+    w_first, w_down, w_coarse, w_head, middle, fine = pl.pallas_call(
+        encoder_weights_kernel,
         out_shape=(
             shape(2, 192, 256),
             shape(1152, 256),
             shape(1152, 256),
-            shape(2304, 256),
-            shape(4, 1024, 256),
-            shape(2304, 256),
-            shape(4, 1024, 256),
             shape(16, 256),
+            shape(27, 32, 96),
+            shape(27, 16, 48),
         ),
         in_specs=[ANY] * 6,
-        out_specs=(VMEM,) * 8,
+        out_specs=(VMEM,) * 6,
         scratch_shapes=[
-            pltpu.VMEM((27, 96, 256), F32),
             pltpu.VMEM((9, 3, 16), BF),
             pltpu.VMEM((27, 16, 32), BF),
             pltpu.VMEM((27, 32, 64), BF),
-            pltpu.VMEM((27, 32, 96), BF),
-            pltpu.VMEM((27, 16, 48), BF),
             pltpu.VMEM((1, 16), BF),
             pltpu.SemaphoreType.DMA((6,)),
         ],
-        compiler_params=pltpu.CompilerParams(vmem_limit_bytes=32 * 2**20),
-        cost_estimate=pl.CostEstimate(
-            flops=2 * 10**9, bytes_accessed=9 * 10**6, transcendentals=0
-        ),
+        compiler_params=small(16),
+        cost_estimate=cost(10**9, 3 * 10**6),
     )(
         *(
             pltpu.with_memory_space_constraint(weight, pltpu.HBM)
@@ -387,27 +412,56 @@
     count = lax.axis_size("gy")
     low = lax.ppermute(noisy_field, "gy", [(i, i + 1) for i in range(count - 1)])
     high = lax.ppermute(noisy_field, "gy", [(i + 1, i) for i in range(count - 1)])
-    own, first_rows, last_rows = pl.pallas_call(
+    own = pl.pallas_call(
         join_kernel,
-        out_shape=(shape(128, 256), shape(48, 256), shape(48, 256)),
+        out_shape=shape(128, 256),
         in_specs=[VMEM] * 3 + [ANY],
-        out_specs=(VMEM,) * 3,
-        compiler_params=pltpu.CompilerParams(vmem_limit_bytes=4 * 2**20),
-        cost_estimate=pl.CostEstimate(flops=10**7, bytes_accessed=2 * 10**5, transcendentals=0),
-    )(noisy_field, high, low, weights[-1])
+        out_specs=VMEM,
+        compiler_params=small(4),
+        cost_estimate=cost(10**7, 2 * 10**5),
+    )(noisy_field, high, low, w_head)
 
     count = lax.axis_size("gx")
-    inner = [(i, i ^ 1) for i in range(count)]
-    outer = [(i, ((i + 1) ^ 1) - 1) for i in range(1, count - 1)]
-    swap_in = lax.ppermute(own, "gx", inner)
-    swap_out = lax.ppermute(own, "gx", outer)
-    low2 = lax.ppermute(last_rows, "gx", [(i, i + 2) for i in range(count - 2)])
-    high2 = lax.ppermute(first_rows, "gx", [(i + 2, i) for i in range(count - 2)])
+    in_chip = [(i, i ^ 1) for i in range(count)]
+    between = [(i, ((i + 1) ^ 1) - 1) for i in range(1, count - 1)]
+    twin = lax.ppermute(own, "gx", in_chip)
+    edge = pl.pallas_call(
+        chip_edge_kernel,
+        out_shape=shape(176, 256),
+        in_specs=[VMEM] * 2,
+        out_specs=VMEM,
+        compiler_params=small(4),
+        cost_estimate=cost(10**5, 3 * 10**5),
+    )(own, twin)
+    chip_edge = lax.ppermute(edge, "gx", between)
+    decoder_weights = pl.pallas_call(
+        decoder_weights_kernel,
+        out_shape=(
+            shape(2304, 256),
+            shape(4, 1024, 256),
+            shape(2304, 256),
+            shape(4, 1024, 256),
+        ),
+        in_specs=[VMEM] * 2 + [ANY],
+        out_specs=(VMEM,) * 4,
+        scratch_shapes=[pltpu.VMEM((27, 96, 256), F32)],
+        compiler_params=small(24),
+        cost_estimate=cost(2 * 10**9, 9 * 10**6),
+    )(middle, fine, edge)
+    rest = pl.pallas_call(
+        twin_edge_kernel,
+        out_shape=shape(48, 256),
+        in_specs=[VMEM, ANY],
+        out_specs=VMEM,
+        compiler_params=small(4),
+        cost_estimate=cost(10**5, 10**5),
+    )(chip_edge, decoder_weights[0])
+    twin_edge = lax.ppermute(rest, "gx", in_chip)
 
     return pl.pallas_call(
         net_kernel,
         out_shape=shape(16, 8, 128, kind=F32),
-        in_specs=[VMEM] * 13,
+        in_specs=[VMEM] * 12,
         out_specs=VMEM,
         scratch_shapes=[
             pltpu.VMEM((6, 10, 32, 256), BF),
@@ -418,11 +472,11 @@
             pltpu.VMEM((4, 6, 32, 256), BF),
             pltpu.VMEM((8, 128, 256), BF),
         ],
-        compiler_params=pltpu.CompilerParams(vmem_limit_bytes=40 * 2**20),
+        compiler_params=small(40),
         cost_estimate=pl.CostEstimate(
             flops=6 * 10**9, bytes_accessed=9 * 10**6, transcendentals=10**6
         ),
-    )(own, swap_in, swap_out, low2, high2, *weights)
+    )(own, twin, chip_edge, twin_edge, w_first, w_down, w_coarse, *decoder_weights, w_head)
 
 
 def solution(mesh):

time: 39 us -> 33.2 us (0.85)
  the two profiles are of different devices: /device:TPU:94 before, /device:TPU:79 now
where the time goes in v2:
time: 33.2 us; the launch traced here: 33 us
  starting transfers between devices  13.1 us (39%)
  Pallas kernels  12.7 us (38%)
  waiting for transfers between devices  7.08 us (21%)
    pallas_call x1, Pallas kernels, body(): pl.pallas_call(net_kernel, out_shape=shape(16, 8, 128, kind=F32), in_spec...  8.79 us
    ppermute x1, starting transfers between devices, body(): chip_edge = lax.ppermute(edge, 'gx', between)  5.36 us
    ppermute x1, starting transfers between devices, body(): lax.ppermute(noisy_field, 'gy', [(i + 1, i) for i in range(count - 1)])  3.55 us
    ppermute x1, waiting for transfers between devices, body(): chip_edge = lax.ppermute(edge, 'gx', between)  2.88 us
    ppermute x1, starting transfers between devices, body(): twin = lax.ppermute(own, 'gx', in_chip)  2.19 us
    pallas_call x1, Pallas kernels, body(): pl.pallas_call(decoder_weights_kernel, out_shape=(shape(2304, 256), shape...  2.14 us
    ppermute x1, waiting for transfers between devices, body(): lax.ppermute(noisy_field, 'gy', [(i, i + 1) for i in range(count - 1)])  2.11 us
    ppermute x1, starting transfers between devices, body(): lax.ppermute(noisy_field, 'gy', [(i, i + 1) for i in range(count - 1)])  2.03 us
  transfers between devices with their start and end apart: 5, of which 4 were waited for; matrix products, arithmetic and copies ran while one was open for 0% of the time, Pallas kernels for 11%

profile of v2, /device:TPU:79, one launch (start us, length us, event | category | flops | bytes accessed | tf_op | source)
XLA Modules:
  0.0 33.0 jit_solution(4558088220190368408)
XLA Ops:
  0.0 0.0 copy-start
  0.0 3.6 %collective-permute-start = (bf16[16,8,128]{2,1,0:T(8,128)(2,1)}, bf16[16,8,128]{2,1,0:T(8,128)(2,1)S(1)}, u32[]{:S(2)}, u32[]{:S(2)}) collective-permute-start(bf16[16,8,128]{2,1,0:T(8,128)(2,1)} %own.1), channel_id=1, source_target_pairs={{1,0},{2,1},{3,2},{4,3},{5,4},{6,5},{7,6},{9,8},{10,9},{11,10},{12... | collective-permute-start | bytes 98312 | tf_op jit(solution)/shard_map/ppermute | solution.py:414
  3.6 2.0 %collective-permute-start.1 = (bf16[16,8,128]{2,1,0:T(8,128)(2,1)}, bf16[16,8,128]{2,1,0:T(8,128)(2,1)S(1)}, u32[]{:S(2)}, u32[]{:S(2)}) collective-permute-start(bf16[16,8,128]{2,1,0:T(8,128)(2,1)} %own.1), channel_id=1, source_target_pairs={{0,1},{1,2},{2,3},{3,4},{4,5},{5,6},{6,7},{8,9},{9,10},{10,11},{11... | collective-permute-start | bytes 98312 | tf_op jit(solution)/shard_map/ppermute | solution.py:413
  5.6 1.6 %shard_map.73 = (bf16[2,192,256]{2,1,0:T(8,128)(2,1)S(1)}, bf16[1152,256]{1,0:T(8,128)(2,1)S(1)}, bf16[1152,256]{1,0:T(8,128)(2,1)S(1)}, bf16[16,256]{1,0:T(8,12...) custom-call(bf16[9,3,16]{2,1,0:T(4,128)(2,1)} %bitcast.20, bf16[27,16,32]{2,1,0:T(8,128)(2,1)} %bitcast.18, ...), custom_call_target="tpu_custom_call" | custom-call | flops 1000000000 | bytes 3000000 | tf_op jit(solution)/shard_map/pallas_call | solution.py:377
  7.2 0.0 collective-permute-done.high
  7.2 2.1 %collective-permute-done.1.low = bf16[16,8,128]{2,1,0:T(8,128)(2,1)S(1)} collective-permute-done((bf16[16,8,128]{2,1,0:T(8,128)(2,1)}, bf16[16,8,128]{2,1,0:T(8,128)(2,1)S(1)}, u32[]{:S(2)}, u32[]{:S(2)}) %collective-permute-start.1) | collective-permute-done | bytes 32800 | tf_op jit(solution)/shard_map/ppermute | solution.py:413
  9.3 0.0 copy-done
  9.3 0.1 shard_map.74.own
  9.5 2.2 %collective-permute-start.2 = (bf16[128,256]{1,0:T(8,128)(2,1)S(1)}, bf16[128,256]{1,0:T(8,128)(2,1)S(1)}, u32[]{:S(2)}, u32[]{:S(2)}) collective-permute-start(bf16[128,256]{1,0:T(8,128)(2,1)S(1)} %shard_map.74.own), channel_id=1, source_target_pairs={{0,8},{8,0},{16,24},{24,16},{32,40},{40,32},{48,56},{56,48},{64,72... | collective-permute-start | bytes 196616 | tf_op jit(solution)/shard_map/ppermute | solution.py:427
  11.7 0.9 %collective-permute-done.2.twin = bf16[128,256]{1,0:T(8,128)(2,1)S(1)} collective-permute-done((bf16[128,256]{1,0:T(8,128)(2,1)S(1)}, bf16[128,256]{1,0:T(8,128)(2,1)S(1)}, u32[]{:S(2)}, u32[]{:S(2)}) %collective-permute-start.2) | collective-permute-done | bytes 65568 | tf_op jit(solution)/shard_map/ppermute | solution.py:427
  12.6 5.4 %collective-permute-start.3 = (bf16[176,256]{1,0:T(8,128)(2,1)S(1)}, bf16[176,256]{1,0:T(8,128)(2,1)S(1)}, u32[]{:S(2)}, u32[]{:S(2)}) collective-permute-start(bf16[176,256]{1,0:T(8,128)(2,1)S(1)} %shard_map.75.after), channel_id=1, source_target_pairs={{8,16},{16,8},{24,32},{32,24},{40,48},{48,40},{56,64},{64,56},{72,... | collective-permute-start | bytes 270344 | tf_op jit(solution)/shard_map/ppermute | solution.py:436
  18.0 2.1 %shard_map.76 = (bf16[2304,256]{1,0:T(8,128)(2,1)S(1)}, bf16[4,1024,256]{2,1,0:T(8,128)(2,1)S(1)}, bf16[2304,256]{1,0:T(8,128)(2,1)S(1)}, bf16[4,1024,256]{2,1,0:T(8,128)(2,1)S(1)}) custom-call(bf16[27,32,96]{2,1,0:T(8,128)(2,1)S(1)} %get-tuple-element.16.middle, bf16[27,16,48]{2,1,0:T(8,128)(2,1)S(1)} %get-tuple-element.17.fine, ...), custom_call_target="tpu_custom_call" | custom-call | flops 2000000000 | bytes 9000000 | tf_op jit(solution)/shard_map/pallas_call | solution.py:437
  20.1 2.9 %collective-permute-done.3.edge.chip_edge = bf16[176,256]{1,0:T(8,128)(2,1)S(1)} collective-permute-done((bf16[176,256]{1,0:T(8,128)(2,1)S(1)}, bf16[176,256]{1,0:T(8,128)(2,1)S(1)}, u32[]{:S(2)}, u32[]{:S(2)}) %collective-permute-start.3) | collective-permute-done | bytes 90144 | tf_op jit(solution)/shard_map/ppermute | solution.py:436
  23.0 0.0 collective-permute-start.4
  23.0 1.2 %collective-permute-done.4.twin_edge = bf16[48,256]{1,0:T(8,128)(2,1)S(1)} collective-permute-done((bf16[48,256]{1,0:T(8,128)(2,1)S(1)}, bf16[48,256]{1,0:T(8,128)(2,1)S(1)}, u32[]{:S(2)}, u32[]{:S(2)}) %collective-permute-start.4) | collective-permute-done | bytes 24608 | tf_op jit(solution)/shard_map/ppermute | solution.py:459
  24.2 8.8 %shard_map.78 = f32[16,8,128]{2,1,0:T(8,128)} custom-call(bf16[128,256]{1,0:T(8,128)(2,1)S(1)} %shard_map.74.own, bf16[128,256]{1,0:T(8,128)(2,1)S(1)} %collective-permute-done.2.twin, bf16[176,256]{1,0:T(8,128)(2,1)S(1)} %collective-permute-done.3.edge.chip_edge, bf16[48,256]{1,0:T(8,128)(2,1)S(1)} %collective-permute-done.4.twin_edge, ...), custom_call_target="tpu_custom_call" | custom-call | flops 6000000000 | bytes 9000000 | tf_op jit(solution)/shard_map/pallas_call | solution.py:461
  (2 shorter events, 0.0 us)
Async XLA Ops:
  0.0 9.3 %copy-start = (bf16[16,8,128]{2,1,0:T(8,128)(2,1)S(1)}, bf16[16,8,128]{2,1,0:T(8,128)(2,1)}, u32[]{:S(2)}) copy-start(bf16[16,8,128]{2,1,0:T(8,128)(2,1)} %own.1) | copy-start | bytes 98308
  0.0 7.2 %collective-permute-start = (bf16[16,8,128]{2,1,0:T(8,128)(2,1)}, bf16[16,8,128]{2,1,0:T(8,128)(2,1)S(1)}, u32[]{:S(2)}, u32[]{:S(2)}) collective-permute-start(bf16[16,8,128]{2,1,0:T(8,128)(2,1)} %own.1), channel_id=1, source_target_pairs={{1,0},{2,1},{3,2},{4,3},{5,4},{6,5},{7,6},{9,8},{10,9},{11,10},{12... | collective-permute-start | bytes 98312 | tf_op jit(solution)/shard_map/ppermute | solution.py:414
  3.6 5.8 %collective-permute-start.1 = (bf16[16,8,128]{2,1,0:T(8,128)(2,1)}, bf16[16,8,128]{2,1,0:T(8,128)(2,1)S(1)}, u32[]{:S(2)}, u32[]{:S(2)}) collective-permute-start(bf16[16,8,128]{2,1,0:T(8,128)(2,1)} %own.1), channel_id=1, source_target_pairs={{0,1},{1,2},{2,3},{3,4},{4,5},{5,6},{6,7},{8,9},{9,10},{10,11},{11... | collective-permute-start | bytes 98312 | tf_op jit(solution)/shard_map/ppermute | solution.py:413
  9.5 3.1 %collective-permute-start.2 = (bf16[128,256]{1,0:T(8,128)(2,1)S(1)}, bf16[128,256]{1,0:T(8,128)(2,1)S(1)}, u32[]{:S(2)}, u32[]{:S(2)}) collective-permute-start(bf16[128,256]{1,0:T(8,128)(2,1)S(1)} %shard_map.74.own), channel_id=1, source_target_pairs={{0,8},{8,0},{16,24},{24,16},{32,40},{40,32},{48,56},{56,48},{64,72... | collective-permute-start | bytes 196616 | tf_op jit(solution)/shard_map/ppermute | solution.py:427
  12.6 10.4 %collective-permute-start.3 = (bf16[176,256]{1,0:T(8,128)(2,1)S(1)}, bf16[176,256]{1,0:T(8,128)(2,1)S(1)}, u32[]{:S(2)}, u32[]{:S(2)}) collective-permute-start(bf16[176,256]{1,0:T(8,128)(2,1)S(1)} %shard_map.75.after), channel_id=1, source_target_pairs={{8,16},{16,8},{24,32},{32,24},{40,48},{48,40},{56,64},{64,56},{72,... | collective-permute-start | bytes 270344 | tf_op jit(solution)/shard_map/ppermute | solution.py:436
  23.0 1.2 %collective-permute-start.4 = (bf16[48,256]{1,0:T(8,128)(2,1)S(1)}, bf16[48,256]{1,0:T(8,128)(2,1)S(1)}, u32[]{:S(2)}, u32[]{:S(2)}) collective-permute-start(bf16[48,256]{1,0:T(8,128)(2,1)S(1)} %shard_map.77), channel_id=1, source_target_pairs={{0,8},{8,0},{16,24},{24,16},{32,40},{40,32},{48,56},{56,48},{64,72... | collective-permute-start | bytes 73736 | tf_op jit(solution)/shard_map/ppermute | solution.py:459

commit v3 on v2

--- a/solution.py
+++ b/solution.py
@@ -54,6 +54,15 @@
     inner = (place == 2 * depth) | (place == 2 * depth + 1)
     outer = (place == 2 * depth + 2) | (place == 2 * depth - 1)
     return ones_where(inner), ones_where(outer)
+
+
+def cell_of(j):
+    return jnp.where(j < 40, j, j - J)
+
+
+def cell_inside(axis, held, cell):
+    at = lax.axis_index(axis) * held + cell
+    return (at >= 0) & (at < lax.axis_size(axis) * held)
 
 
 SETS = (((0,), (1, 2)), ((0, 1), (2,)))
@@ -94,7 +103,7 @@
 
 def encoder_weights_kernel(
     raw_first, raw_down, raw_coarse, raw_middle, raw_fine, raw_head,
-    w_first, w_down, w_coarse, w_head, middle, fine,
+    w_first, w_down, w_coarse, w_head, middle, fine, pick,
     first, down, coarse, head, sems,
 ):
     copies = [
@@ -113,6 +122,10 @@
     for copy in copies:
         copy.start()
     r16, r32, r64 = repeat_matrix(16), repeat_matrix(32), repeat_matrix(64)
+    row = iota((4 * J, 256), 0)
+    cell = cell_of(row % J)
+    inside = cell_inside("gy", 32, cell)
+    pick[...] = ((iota((4 * J, 256), 1) == (4 * cell + row // J + 256) % 256) & inside).astype(BF)
     for copy in copies[:4]:
         copy.wait()
 
@@ -145,18 +158,19 @@
         copy.wait()
 
 
-def decoder_weights_kernel(
-    middle, fine, after, w_mid_skip, w_mid_up, w_fine_skip, w_fine_up, tiled
-):
-    r16, r32 = repeat_matrix(16), repeat_matrix(32)
+def mid_weights_kernel(middle, after, w_mid_skip, w_mid_up, tiled):
+    r32 = repeat_matrix(32)
     for tap in range(27):
         tiled[tap] = dot_tn(middle[tap], r32) * 0.5
     taps = [[tiled[dz * 9 + xy, 64:96, :].astype(BF) for xy in range(9)] for dz in range(3)]
     banded(w_mid_skip, taps, 32, [0, 2, 4, 6, 1, 3, 5, 7], natural(32))
     folded(w_mid_up, lambda dz, dx, dy: tiled[dz * 9 + dx * 3 + dy, 0:64, :], 64, 4, natural(32))
 
+
+def fine_weights_kernel(fine, after, w_fine_skip, w_fine_up, tiled):
+    r16 = repeat_matrix(16)
     for tap in range(27):
-        tiled[tap, 0:48, :] = dot_tn(fine[tap], r16) * 0.5
+        tiled[tap] = dot_tn(fine[tap], r16) * 0.5
     taps = [[tiled[dz * 9 + xy, 32:48, :].astype(BF) for xy in range(9)] for dz in range(3)]
     banded(w_fine_skip, taps, 16, list(range(0, 16, 2)) + list(range(1, 16, 2)), natural(16))
     folded(w_fine_up, lambda dz, dx, dy: tiled[dz * 9 + dx * 3 + dy, 0:32, :], 32, 8, natural(16))
@@ -174,14 +188,14 @@
     out[...] = dot(swap, both).astype(BF)
 
 
-def chip_edge_kernel(own, twin, out):
+def chip_edge_kernel(own, twin, after, out):
     odd = lax.axis_index("gx") % 2 == 1
     for_high = jnp.concatenate([twin[80:], own[...]], axis=0)
     for_low = jnp.concatenate([own[...], twin[:48]], axis=0)
     out[...] = jnp.where(odd, for_high, for_low)
 
 
-def twin_edge_kernel(edge, after, out):
+def twin_edge_kernel(edge, after, also_after, out):
     odd = lax.axis_index("gx") % 2 == 1
     out[...] = jnp.where(odd, edge[:48], edge[128:])
 
@@ -190,65 +204,105 @@
     return h + h * jnp.tanh(h)
 
 
+def row_flag(cell):
+    return jnp.where(cell_inside("gx", 2, cell), 1.0, 0.0)
+
+
+def encode(field, pick, w_first, first_pair, pairs, put_fine, put_pooled):
+    wide = field.astype(F32)
+    shifted = [pltpu.roll(wide, 1, 1).astype(BF), field, pltpu.roll(wide, 255, 1).astype(BF)]
+    for at in range(pairs):
+        m = first_pair + at
+        window = jnp.concatenate([part[at * 32 : at * 32 + 64] for part in shifted], axis=0)
+        flag = row_flag(lax.shift_right_arithmetic(m, 1) if put_fine is None else m // 2)
+        lhs = (dot_nt(pick[...], window) * flag).astype(BF)
+        pooled = [jnp.zeros((J, 128), F32) for _ in range(2)]
+        for even in range(2):
+            value = silu_half(dot(lhs, w_first[even])).reshape(4, J, 256)
+            for part in range(2):
+                both = value[2 * part] + value[2 * part + 1]
+                pooled[part] = pooled[part] + both[:, :128] + both[:, 128:]
+            if put_fine is not None and -1 <= 2 * m + even <= 8:
+                for group in range(4):
+                    put_fine(group + 1, 2 * m + even, value[group, :32])
+                put_fine(0, 2 * m + even, pltpu.roll(value[3], 1, 0)[:32])
+                put_fine(5, 2 * m + even, pltpu.roll(value[0], J - 1, 0)[:32])
+        put_pooled(0, at, pltpu.roll(pooled[1], 1, 0))
+        put_pooled(1, at, pooled[0])
+        put_pooled(2, at, pooled[1])
+        put_pooled(3, at, pltpu.roll(pooled[0], J - 1, 0))
+
+
+def for_each_core(work):
+    odd = lax.axis_index("gx") % 2
+
+    @pl.when(odd == 0)
+    def _():
+        work(0)
+
+    @pl.when(odd == 1)
+    def _():
+        work(1)
+
+
+def encode_part(field, pick, w_first, first_pair, first_x, fine, pooled):
+    def put_fine(group, x, value):
+        fine[group, x - first_x] = value.astype(BF)
+
+    def put_pooled(group, at, value):
+        pooled[group, at] = value.astype(BF)
+
+    encode(field, pick, w_first, first_pair, 6, put_fine, put_pooled)
+
+
+def encode_near_kernel(own, twin, pick, w_first, after, fine, pooled):
+    def work(core):
+        first, second = (twin, own) if core else (own, twin)
+        field = jnp.concatenate([first[16:], second[:112]], axis=0)
+        encode_part(field, pick, w_first, -3 if core else 1, -1 if core else 2, fine, pooled)
+
+    for_each_core(work)
+
+
+def encode_far_kernel(own, edge, pick, w_first, after, fine, pooled):
+    def work(core):
+        parts = [own[80:], edge[...]] if core else [edge[...], own[:48]]
+        field = jnp.concatenate(parts, axis=0)
+        encode_part(field, pick, w_first, 3 if core else -5, 6 if core else -1, fine, pooled)
+
+    for_each_core(work)
+
+
 def net_kernel(
-    own, twin, chip_edge, twin_edge,
+    twin, twin_edge, pick, fine_near, pool_near, fine_far, pool_far,
     w_first, w_down, w_coarse, w_mid_skip, w_mid_up, w_fine_skip, w_fine_up, w_head,
     out,
     fine_s, pool_fine_s, mid_s, pool_mid_s, coarse_s, up_s, last_s,
 ):
-    gx, gy = lax.axis_index("gx"), lax.axis_index("gy")
-    cells_x, cells_y = lax.axis_size("gx") * 2, lax.axis_size("gy") * 32
-
-    def row_flag(cell):
-        at = gx * 2 + cell
-        return jnp.where((at >= 0) & (at < cells_x), 1.0, 0.0)
-
-    def cell_of(j):
-        return jnp.where(j < 40, j, j - J)
-
-    at_y = gy * 32 + cell_of(iota((J, 256), 0))
-    y_mask = jnp.where((at_y >= 0) & (at_y < cells_y), 1.0, 0.0)
-
-    mine, other, edge, rest = own[...], twin[...], chip_edge[...], twin_edge[...]
+    y_mask = jnp.where(cell_inside("gy", 32, cell_of(iota((J, 256), 0))), 1.0, 0.0)
+
+    def gather(core):
+        if core:
+            fine_s[:, 0:7], fine_s[:, 7:10] = fine_near[...], fine_far[...]
+            pool_fine_s[:, 2:8], pool_fine_s[:, 8:14] = pool_near[...], pool_far[...]
+        else:
+            fine_s[:, 0:3], fine_s[:, 3:10] = fine_far[...], fine_near[...]
+            pool_fine_s[:, 0:6], pool_fine_s[:, 6:12] = pool_far[...], pool_near[...]
+
+    for_each_core(gather)
+    odd = lax.axis_index("gx") % 2 == 1
+    rest, other = twin_edge[...], twin[...]
     field = jnp.where(
-        gx % 2 == 1,
-        jnp.concatenate([rest, other, mine, edge], axis=0),
-        jnp.concatenate([edge, mine, other, rest], axis=0),
-    )
-    wide = field.astype(F32)
-    shifted = [
-        pltpu.roll(wide, 1, 1).astype(BF),
-        field,
-        pltpu.roll(wide, 255, 1).astype(BF),
-    ]
-    row = iota((4 * J, 256), 0)
-    cell = cell_of(row % J)
-    y = 4 * cell + row // J
-    at_row = gy * 32 + cell
-    pick = (
-        (iota((4 * J, 256), 1) == (y + 256) % 256) & (at_row >= 0) & (at_row < cells_y)
-    ).astype(BF)
-
-    for m in range(-5, 9):
-        at = (2 * m + 10) * 16
-        window = jnp.concatenate([part[at : at + 64] for part in shifted], axis=0)
-        lhs = (dot_nt(pick, window) * row_flag(m // 2)).astype(BF)
-        pooled = [jnp.zeros((J, 128), F32) for _ in range(2)]
-        for even in range(2):
-            x = 2 * m + even
-            value = silu_half(dot(lhs, w_first[even])).reshape(4, J, 256)
-            for part in range(2):
-                both = value[2 * part] + value[2 * part + 1]
-                pooled[part] = pooled[part] + both[:, :128] + both[:, 128:]
-            if -1 <= x <= 8:
-                for group in range(4):
-                    fine_s[group + 1, x + 1] = value[group, :32].astype(BF)
-                fine_s[0, x + 1] = pltpu.roll(value[3], 1, 0)[:32].astype(BF)
-                fine_s[5, x + 1] = pltpu.roll(value[0], J - 1, 0)[:32].astype(BF)
-        pool_fine_s[0, m + 5] = pltpu.roll(pooled[1], 1, 0).astype(BF)
-        pool_fine_s[1, m + 5] = pooled[0].astype(BF)
-        pool_fine_s[2, m + 5] = pooled[1].astype(BF)
-        pool_fine_s[3, m + 5] = pltpu.roll(pooled[0], J - 1, 0).astype(BF)
+        odd,
+        jnp.concatenate([rest, other[:48]], axis=0),
+        jnp.concatenate([other[80:], rest], axis=0),
+    )
+    first_at = jnp.where(odd, 0, 12)
+
+    def put_pooled(group, at, value):
+        pool_fine_s[group, first_at + at] = value.astype(BF)
+
+    encode(field, pick, w_first, first_at - 5, 2, None, put_pooled)
 
     sums = [jnp.zeros((J, 128), F32) for _ in range(6)]
     for py in range(2):
@@ -317,19 +371,16 @@
                 shift = 1 if py else J - 1
                 up_s[0 if py else 3, at] = pltpu.roll(masked, shift, 0)[:32].astype(BF)
 
+    lhs = jnp.concatenate(
+        [
+            fine_s[dy : dy + 4, dx : dx + 8].reshape(1024, 256)
+            for dx in range(3)
+            for dy in range(3)
+        ],
+        axis=1,
+    )
+    skip = dot(lhs, w_fine_skip[...]).reshape(4, 8, 32, 256)
     for py in range(2):
-        skip = []
-        for half in range(2):
-            group = 2 * half + py
-            lhs = jnp.concatenate(
-                [
-                    fine_s[group + dy, dx : dx + 8].reshape(256, 256)
-                    for dx in range(3)
-                    for dy in range(3)
-                ],
-                axis=1,
-            )
-            skip.append(dot(lhs, w_fine_skip[...]).reshape(8, 32, 256))
         for px in range(2):
             lhs = jnp.concatenate(
                 [
@@ -344,7 +395,7 @@
                 group = 2 * half + py
                 for k in range(4):
                     x = 2 * k + px
-                    value = silu_half(skip[half][x] + up[half, k])
+                    value = silu_half(skip[group, x] + up[half, k])
                     last_s[x, pl.ds(group * 32, 32), :] = value.astype(BF)
 
     heads = jnp.concatenate([dot_nt(w_head[...], last_s[x]) for x in range(8)], axis=0)
@@ -374,7 +425,7 @@
     def small(limit):
         return pltpu.CompilerParams(vmem_limit_bytes=limit * 2**20)
 
-    w_first, w_down, w_coarse, w_head, middle, fine = pl.pallas_call(
+    w_first, w_down, w_coarse, w_head, middle, fine, pick = pl.pallas_call(
         encoder_weights_kernel,
         out_shape=(
             shape(2, 192, 256),
@@ -383,9 +434,10 @@
             shape(16, 256),
             shape(27, 32, 96),
             shape(27, 16, 48),
+            shape(4 * J, 256),
         ),
         in_specs=[ANY] * 6,
-        out_specs=(VMEM,) * 6,
+        out_specs=(VMEM,) * 7,
         scratch_shapes=[
             pltpu.VMEM((9, 3, 16), BF),
             pltpu.VMEM((27, 16, 32), BF),
@@ -425,43 +477,60 @@
     in_chip = [(i, i ^ 1) for i in range(count)]
     between = [(i, ((i + 1) ^ 1) - 1) for i in range(1, count - 1)]
     twin = lax.ppermute(own, "gx", in_chip)
+    w_mid_skip, w_mid_up = pl.pallas_call(
+        mid_weights_kernel,
+        out_shape=(shape(2304, 256), shape(4, 1024, 256)),
+        in_specs=[VMEM, ANY],
+        out_specs=(VMEM,) * 2,
+        scratch_shapes=[pltpu.VMEM((27, 96, 256), F32)],
+        compiler_params=small(24),
+        cost_estimate=cost(10**9, 4 * 10**6),
+    )(middle, own)
     edge = pl.pallas_call(
         chip_edge_kernel,
         out_shape=shape(176, 256),
-        in_specs=[VMEM] * 2,
+        in_specs=[VMEM] * 2 + [ANY],
         out_specs=VMEM,
         compiler_params=small(4),
         cost_estimate=cost(10**5, 3 * 10**5),
-    )(own, twin)
+    )(own, twin, w_mid_skip)
     chip_edge = lax.ppermute(edge, "gx", between)
-    decoder_weights = pl.pallas_call(
-        decoder_weights_kernel,
-        out_shape=(
-            shape(2304, 256),
-            shape(4, 1024, 256),
-            shape(2304, 256),
-            shape(4, 1024, 256),
-        ),
-        in_specs=[VMEM] * 2 + [ANY],
-        out_specs=(VMEM,) * 4,
-        scratch_shapes=[pltpu.VMEM((27, 96, 256), F32)],
-        compiler_params=small(24),
-        cost_estimate=cost(2 * 10**9, 9 * 10**6),
-    )(middle, fine, edge)
+
+    def encoder(kernel, x_rows, *operands):
+        return pl.pallas_call(
+            kernel,
+            out_shape=(shape(6, x_rows, 32, 256), shape(4, 6, J, 128)),
+            in_specs=[VMEM] * 4 + [ANY],
+            out_specs=(VMEM,) * 2,
+            compiler_params=small(16),
+            cost_estimate=cost(2 * 10**9, 3 * 10**6),
+        )(*operands)
+
+    fine_near, pool_near = encoder(encode_near_kernel, 7, own, twin, pick, w_first, edge)
+    w_fine_skip, w_fine_up = pl.pallas_call(
+        fine_weights_kernel,
+        out_shape=(shape(2304, 256), shape(4, 1024, 256)),
+        in_specs=[VMEM, ANY],
+        out_specs=(VMEM,) * 2,
+        scratch_shapes=[pltpu.VMEM((27, 48, 256), F32)],
+        compiler_params=small(16),
+        cost_estimate=cost(10**9, 4 * 10**6),
+    )(fine, edge)
     rest = pl.pallas_call(
         twin_edge_kernel,
         out_shape=shape(48, 256),
-        in_specs=[VMEM, ANY],
+        in_specs=[VMEM, ANY, ANY],
         out_specs=VMEM,
         compiler_params=small(4),
         cost_estimate=cost(10**5, 10**5),
-    )(chip_edge, decoder_weights[0])
+    )(chip_edge, w_fine_skip, pool_near)
     twin_edge = lax.ppermute(rest, "gx", in_chip)
+    fine_far, pool_far = encoder(encode_far_kernel, 3, own, chip_edge, pick, w_first, rest)
 
     return pl.pallas_call(
         net_kernel,
         out_shape=shape(16, 8, 128, kind=F32),
-        in_specs=[VMEM] * 12,
+        in_specs=[VMEM] * 15,
         out_specs=VMEM,
         scratch_shapes=[
             pltpu.VMEM((6, 10, 32, 256), BF),
@@ -476,7 +545,10 @@
         cost_estimate=pl.CostEstimate(
             flops=6 * 10**9, bytes_accessed=9 * 10**6, transcendentals=10**6
         ),
-    )(own, twin, chip_edge, twin_edge, w_first, w_down, w_coarse, *decoder_weights, w_head)
+    )(
+        twin, twin_edge, pick, fine_near, pool_near, fine_far, pool_far,
+        w_first, w_down, w_coarse, w_mid_skip, w_mid_up, w_fine_skip, w_fine_up, w_head,
+    )
 
 
 def solution(mesh):

time: 33.2 us -> 31.2 us (0.940)
  waiting for transfers between devices: 7.08 us -> 5.11 us
    pallas_call x1 -> x4, Pallas kernels: 2.14 us -> 4.98 us  [the longest x2 2.71 us: encoder(): pl.pallas_call(kernel, out_shape=(shape(6, x_rows, 32, 256), shape(4, 6,...]
    pallas_call x1, Pallas kernels: 8.79 us -> 6.16 us  [body(): pl.pallas_call(net_kernel, out_shape=shape(16, 8, 128, kind=F32), in_spec...]
    ppermute x1, waiting for transfers between devices: 1.19 us -> 0.01 us  [body(): twin_edge = lax.ppermute(rest, 'gx', in_chip)]
    ppermute x1, waiting for transfers between devices: 0.9 us -> 0.01 us  [body(): twin = lax.ppermute(own, 'gx', in_chip)]
    ppermute x1, starting transfers between devices: 5.36 us -> 5.03 us  [body(): chip_edge = lax.ppermute(edge, 'gx', between)]
  transfers between devices with their start and end apart: 5 -> 5, of which waited for: 4 -> 2; matrix products, arithmetic and copies ran while one was open for 0% -> 0% of each run, Pallas kernels for 11% -> 21%
where the time goes in v3:
time: 31.2 us; the launch traced here: 30.9 us
  Pallas kernels  12.9 us (41%)
  starting transfers between devices  12.8 us (41%)
  waiting for transfers between devices  5.11 us (16%)
    pallas_call x1, Pallas kernels, body(): pl.pallas_call(net_kernel, out_shape=shape(16, 8, 128, kind=F32), in_spec...  6.16 us
    ppermute x1, starting transfers between devices, body(): chip_edge = lax.ppermute(edge, 'gx', between)  5.03 us
    ppermute x1, starting transfers between devices, body(): lax.ppermute(noisy_field, 'gy', [(i + 1, i) for i in range(count - 1)])  3.55 us
    ppermute x1, waiting for transfers between devices, body(): chip_edge = lax.ppermute(edge, 'gx', between)  2.99 us
    pallas_call x2, Pallas kernels, encoder(): pl.pallas_call(kernel, out_shape=(shape(6, x_rows, 32, 256), shape(4, 6,...  2.71 us
    ppermute x1, starting transfers between devices, body(): twin = lax.ppermute(own, 'gx', in_chip)  2.19 us
    ppermute x1, waiting for transfers between devices, body(): lax.ppermute(noisy_field, 'gy', [(i, i + 1) for i in range(count - 1)])  2.11 us
    ppermute x1, starting transfers between devices, body(): lax.ppermute(noisy_field, 'gy', [(i, i + 1) for i in range(count - 1)])  2.03 us
  transfers between devices with their start and end apart: 5, of which 2 were waited for; matrix products, arithmetic and copies ran while one was open for 0% of the time, Pallas kernels for 21%

profile of v3, /device:TPU:79, one launch (start us, length us, event | category | flops | bytes accessed | tf_op | source)
XLA Modules:
  0.0 30.9 jit_solution(5868933374727223962)
XLA Ops:
  0.0 0.0 copy-start
  0.0 3.6 %collective-permute-start = (bf16[16,8,128]{2,1,0:T(8,128)(2,1)}, bf16[16,8,128]{2,1,0:T(8,128)(2,1)S(1)}, u32[]{:S(2)}, u32[]{:S(2)}) collective-permute-start(bf16[16,8,128]{2,1,0:T(8,128)(2,1)} %own.1), channel_id=1, source_target_pairs={{1,0},{2,1},{3,2},{4,3},{5,4},{6,5},{7,6},{9,8},{10,9},{11,10},{12... | collective-permute-start | bytes 98312 | tf_op jit(solution)/shard_map/ppermute | solution.py:466
  3.6 2.0 %collective-permute-start.1 = (bf16[16,8,128]{2,1,0:T(8,128)(2,1)}, bf16[16,8,128]{2,1,0:T(8,128)(2,1)S(1)}, u32[]{:S(2)}, u32[]{:S(2)}) collective-permute-start(bf16[16,8,128]{2,1,0:T(8,128)(2,1)} %own.1), channel_id=1, source_target_pairs={{0,1},{1,2},{2,3},{3,4},{4,5},{5,6},{6,7},{8,9},{9,10},{10,11},{11... | collective-permute-start | bytes 98312 | tf_op jit(solution)/shard_map/ppermute | solution.py:465
  5.6 1.6 %shard_map.73 = (bf16[2,192,256]{2,1,0:T(8,128)(2,1)S(1)}, bf16[1152,256]{1,0:T(8,128)(2,1)S(1)}, bf16[1152,256]{1,0:T(8,128)(2,1)S(1)}, bf16[16,256]{1,0:T(8,12...) custom-call(bf16[9,3,16]{2,1,0:T(4,128)(2,1)} %bitcast.20, ...), custom_call_target="tpu_custom_call" | custom-call | flops 1000000000 | bytes 3000000 | tf_op jit(solution)/shard_map/pallas_call | solution.py:428
  7.2 0.0 collective-permute-done.high
  7.2 2.1 %collective-permute-done.1.low = bf16[16,8,128]{2,1,0:T(8,128)(2,1)S(1)} collective-permute-done((bf16[16,8,128]{2,1,0:T(8,128)(2,1)}, bf16[16,8,128]{2,1,0:T(8,128)(2,1)S(1)}, u32[]{:S(2)}, u32[]{:S(2)}) %collective-permute-start.1) | collective-permute-done | bytes 32800 | tf_op jit(solution)/shard_map/ppermute | solution.py:465
  9.3 0.0 copy-done
  9.3 0.1 shard_map.74.after.own
  9.5 2.2 %collective-permute-start.2 = (bf16[128,256]{1,0:T(8,128)(2,1)S(1)}, bf16[128,256]{1,0:T(8,128)(2,1)S(1)}, u32[]{:S(2)}, u32[]{:S(2)}) collective-permute-start(bf16[128,256]{1,0:T(8,128)(2,1)S(1)} %shard_map.74.after.own), channel_id=1, source_target_pairs={{0,8},{8,0},{16,24},{24,16},{32,40},{40,32},{48,56},{56,48},{64,72... | collective-permute-start | bytes 196616 | tf_op jit(solution)/shard_map/ppermute | solution.py:479
  11.7 1.3 %shard_map.75 = (bf16[2304,256]{1,0:T(8,128)(2,1)S(1)}, bf16[4,1024,256]{2,1,0:T(8,128)(2,1)S(1)}) custom-call(bf16[27,32,96]{2,1,0:T(8,128)(2,1)S(1)} %get-tuple-element.21.middle, bf16[128,256]{1,0:T(8,128)(2,1)S(1)} %shard_map.74.after.own), custom_call_target="tpu_custom_call" | custom-call | flops 1000000000 | bytes 4000000 | tf_op jit(solution)/shard_map/pallas_call | solution.py:480
  13.0 0.0 collective-permute-done.2.twin
  13.0 5.0 %collective-permute-start.3 = (bf16[176,256]{1,0:T(8,128)(2,1)S(1)}, bf16[176,256]{1,0:T(8,128)(2,1)S(1)}, u32[]{:S(2)}, u32[]{:S(2)}) collective-permute-start(bf16[176,256]{1,0:T(8,128)(2,1)S(1)} %shard_map.76.after), channel_id=1, source_target_pairs={{8,16},{16,8},{24,32},{32,24},{40,48},{48,40},{56,64},{64,56},{72,... | collective-permute-start | bytes 270344 | tf_op jit(solution)/shard_map/ppermute | solution.py:497
  18.0 1.4 %shard_map.78 = (bf16[6,7,32,256]{3,2,1,0:T(8,128)(2,1)S(1)}, bf16[4,6,48,128]{3,2,1,0:T(8,128)(2,1)S(1)}) custom-call(bf16[128,256]{1,0:T(8,128)(2,1)S(1)} %shard_map.74.after.own, bf16[128,256]{1,0:T(8,128)(2,1)S(1)} %collective-permute-done.2.twin, bf16[192,256]{1,0:T(8,128)(2,1)S(1)} %get-tuple-element.25.pick, ...), custom_call_target="tpu_custom_call" | custom-call | flops 2000000000 | bytes 3000000 | tf_op jit(solution)/shard_map/pallas_call | solution.py:500
  19.4 1.0 %shard_map.77 = (bf16[2304,256]{1,0:T(8,128)(2,1)S(1)}, bf16[4,1024,256]{2,1,0:T(8,128)(2,1)S(1)}) custom-call(bf16[27,16,48]{2,1,0:T(8,128)(2,1)S(1)} %get-tuple-element.23.fine, bf16[176,256]{1,0:T(8,128)(2,1)S(1)} %shard_map.76.after), custom_call_target="tpu_custom_call" | custom-call | flops 1000000000 | bytes 4000000 | tf_op jit(solution)/shard_map/pallas_call | solution.py:510
  20.4 3.0 %collective-permute-done.3.edge = bf16[176,256]{1,0:T(8,128)(2,1)S(1)} collective-permute-done((bf16[176,256]{1,0:T(8,128)(2,1)S(1)}, bf16[176,256]{1,0:T(8,128)(2,1)S(1)}, u32[]{:S(2)}, u32[]{:S(2)}) %collective-permute-start.3) | collective-permute-done | bytes 90144 | tf_op jit(solution)/shard_map/ppermute | solution.py:497
  23.4 0.0 collective-permute-start.4
  23.4 1.3 %shard_map.80 = (bf16[6,3,32,256]{3,2,1,0:T(8,128)(2,1)S(1)}, bf16[4,6,48,128]{3,2,1,0:T(8,128)(2,1)S(1)}) custom-call(bf16[128,256]{1,0:T(8,128)(2,1)S(1)} %shard_map.74.after.own, bf16[176,256]{1,0:T(8,128)(2,1)S(1)} %collective-permute-done.3.edge, bf16[192,256]{1,0:T(8,128)(2,1)S(1)} %get-tuple-element.25.pick, ...), custom_call_target="tpu_custom_call" | custom-call | flops 2000000000 | bytes 3000000 | tf_op jit(solution)/shard_map/pallas_call | solution.py:500
  24.8 0.0 collective-permute-done.4.twin_edge
  24.8 6.2 %shard_map.81 = f32[16,8,128]{2,1,0:T(8,128)} custom-call(bf16[128,256]{1,0:T(8,128)(2,1)S(1)} %collective-permute-done.2.twin, bf16[48,256]{1,0:T(8,128)(2,1)S(1)} %collective-permute-done.4.twin_edge, bf16[192,256]{1,0:T(8,128)(2,1)S(1)} %get-tuple-element.25.pick, bf16[6,7,32,256]{3,2,1,0:T(8,128)(2,1)S(1)} %get-tuple-element.28.fine_near, ...), custom_call_target="tpu_custom_call" | custom-call | flops 6000000000 | bytes 9000000 | tf_op jit(solution)/shard_map/pallas_call | solution.py:530
  (2 shorter events, 0.0 us)
Async XLA Ops:
  0.0 9.3 %copy-start = (bf16[16,8,128]{2,1,0:T(8,128)(2,1)S(1)}, bf16[16,8,128]{2,1,0:T(8,128)(2,1)}, u32[]{:S(2)}) copy-start(bf16[16,8,128]{2,1,0:T(8,128)(2,1)} %own.1) | copy-start | bytes 98308
  0.0 7.2 %collective-permute-start = (bf16[16,8,128]{2,1,0:T(8,128)(2,1)}, bf16[16,8,128]{2,1,0:T(8,128)(2,1)S(1)}, u32[]{:S(2)}, u32[]{:S(2)}) collective-permute-start(bf16[16,8,128]{2,1,0:T(8,128)(2,1)} %own.1), channel_id=1, source_target_pairs={{1,0},{2,1},{3,2},{4,3},{5,4},{6,5},{7,6},{9,8},{10,9},{11,10},{12... | collective-permute-start | bytes 98312 | tf_op jit(solution)/shard_map/ppermute | solution.py:466
  3.6 5.8 %collective-permute-start.1 = (bf16[16,8,128]{2,1,0:T(8,128)(2,1)}, bf16[16,8,128]{2,1,0:T(8,128)(2,1)S(1)}, u32[]{:S(2)}, u32[]{:S(2)}) collective-permute-start(bf16[16,8,128]{2,1,0:T(8,128)(2,1)} %own.1), channel_id=1, source_target_pairs={{0,1},{1,2},{2,3},{3,4},{4,5},{5,6},{6,7},{8,9},{9,10},{10,11},{11... | collective-permute-start | bytes 98312 | tf_op jit(solution)/shard_map/ppermute | solution.py:465
  9.5 3.5 %collective-permute-start.2 = (bf16[128,256]{1,0:T(8,128)(2,1)S(1)}, bf16[128,256]{1,0:T(8,128)(2,1)S(1)}, u32[]{:S(2)}, u32[]{:S(2)}) collective-permute-start(bf16[128,256]{1,0:T(8,128)(2,1)S(1)} %shard_map.74.after.own), channel_id=1, source_target_pairs={{0,8},{8,0},{16,24},{24,16},{32,40},{40,32},{48,56},{56,48},{64,72... | collective-permute-start | bytes 196616 | tf_op jit(solution)/shard_map/ppermute | solution.py:479
  13.0 10.4 %collective-permute-start.3 = (bf16[176,256]{1,0:T(8,128)(2,1)S(1)}, bf16[176,256]{1,0:T(8,128)(2,1)S(1)}, u32[]{:S(2)}, u32[]{:S(2)}) collective-permute-start(bf16[176,256]{1,0:T(8,128)(2,1)S(1)} %shard_map.76.after), channel_id=1, source_target_pairs={{8,16},{16,8},{24,32},{32,24},{40,48},{48,40},{56,64},{64,56},{72,... | collective-permute-start | bytes 270344 | tf_op jit(solution)/shard_map/ppermute | solution.py:497
  23.4 1.4 %collective-permute-start.4 = (bf16[48,256]{1,0:T(8,128)(2,1)S(1)}, bf16[48,256]{1,0:T(8,128)(2,1)S(1)}, u32[]{:S(2)}, u32[]{:S(2)}) collective-permute-start(bf16[48,256]{1,0:T(8,128)(2,1)S(1)} %shard_map.79.after), channel_id=1, source_target_pairs={{0,8},{8,0},{16,24},{24,16},{32,40},{40,32},{48,56},{56,48},{64,72... | collective-permute-start | bytes 73736 | tf_op jit(solution)/shard_map/ppermute | solution.py:527

commit v4 on v3

--- a/solution.py
+++ b/solution.py
@@ -44,16 +44,26 @@
     return jnp.where(cond, 1.0, 0.0).astype(BF)
 
 
-def band_masks(rows, depth, depth_of):
-    place = depth_of(iota((rows, 256), 1))
-    return [ones_where(place == depth + 1 - tap) for tap in range(3)]
-
-
-def up_masks(rows, depth, depth_of):
-    place = depth_of(iota((rows, 256), 1))
-    inner = (place == 2 * depth) | (place == 2 * depth + 1)
-    outer = (place == 2 * depth + 2) | (place == 2 * depth - 1)
-    return ones_where(inner), ones_where(outer)
+def tiles(depth_of):
+    return [
+        (slice(at, at + 128), {depth_of(lane) for lane in range(at, at + 128)})
+        for at in (0, 128)
+    ]
+
+
+def place_block(out, index, row, rows, terms, places, held, lanes):
+    total = None
+    for depths, value in terms:
+        depths = [depth for depth in depths if depth in held]
+        if depths:
+            mask = places[:, lanes] == depths[0]
+            for depth in depths[1:]:
+                mask = mask | (places[:, lanes] == depth)
+            part = ones_where(mask) * value[:, lanes]
+            total = part if total is None else total + part
+    if total is None:
+        total = jnp.zeros((rows, 128), BF)
+    out[(*index, pl.ds(row, rows), lanes)] = total
 
 
 def cell_of(j):
@@ -70,18 +80,19 @@
 
 def banded(out, taps, channels, row_depths, depth_of):
     size = channels * len(row_depths)
-    for at, depth in enumerate(row_depths):
-        masks = band_masks(channels, depth, depth_of)
-        for xy in range(9):
-            block = sum(masks[dz] * taps[dz][xy] for dz in range(3))
-            out[pl.ds(xy * size + at * channels, channels), :] = block
+    places = depth_of(iota((channels, 256), 1))
+    for lanes, held in tiles(depth_of):
+        for at, depth in enumerate(row_depths):
+            for xy in range(9):
+                terms = [((depth + 1 - dz,), taps[dz][xy]) for dz in range(3)]
+                row = xy * size + at * channels
+                place_block(out, (), row, channels, terms, places, held, lanes)
 
 
 def folded(out, get, channels, depths, depth_of):
     size = channels * depths
-    place = depth_of(iota((channels, 256), 1))
-    even = place % 2 == 0
-    masks = [up_masks(channels, depth, depth_of) for depth in range(depths)]
+    places = depth_of(iota((channels, 256), 1))
+    even = places % 2 == 0
     for px in range(2):
         for tx in range(2):
             by_y = [
@@ -95,10 +106,15 @@
                     ]
                     inner = jnp.where(even, w1 + w2, w0 + w1).astype(BF)
                     outer = jnp.where(even, w0, w2).astype(BF)
-                    for depth in range(depths):
-                        block = masks[depth][0] * inner + masks[depth][1] * outer
-                        at = (tx * 2 + ty) * size + depth * channels
-                        out[px * 2 + py, pl.ds(at, channels), :] = block
+                    for lanes, held in tiles(depth_of):
+                        for depth in range(depths):
+                            terms = [
+                                ((2 * depth, 2 * depth + 1), inner),
+                                ((2 * depth + 2, 2 * depth - 1), outer),
+                            ]
+                            row = (tx * 2 + ty) * size + depth * channels
+                            index = (px * 2 + py,)
+                            place_block(out, index, row, channels, terms, places, held, lanes)
 
 
 def encoder_weights_kernel(
@@ -176,11 +192,13 @@
     folded(w_fine_up, lambda dz, dx, dy: tiled[dz * 9 + dx * 3 + dy, 0:32, :], 32, 8, natural(16))
 
 
-def join_kernel(own, high, low, after, out):
-    near = iota((128, 128), 1) < 64
+def join_kernel(own, inner, outer, after, out):
+    from_inner = (iota((128, 128), 1) < 64) == (lax.axis_index("gy") % 2 == 0)
     mine = own[...].astype(F32).reshape(128, 128)
     rim = jnp.where(
-        near, high[...].astype(F32).reshape(128, 128), low[...].astype(F32).reshape(128, 128)
+        from_inner,
+        inner[...].astype(F32).reshape(128, 128),
+        outer[...].astype(F32).reshape(128, 128),
     )
     both = jnp.concatenate([mine, rim], axis=1).astype(BF)
     row, col = iota((128, 128), 0), iota((128, 128), 1)
@@ -461,9 +479,14 @@
         )
     )
 
-    count = lax.axis_size("gy")
-    low = lax.ppermute(noisy_field, "gy", [(i, i + 1) for i in range(count - 1)])
-    high = lax.ppermute(noisy_field, "gy", [(i + 1, i) for i in range(count - 1)])
+    def pairs(axis):
+        count = lax.axis_size(axis)
+        inner = [(i, i ^ 1) for i in range(count)]
+        return inner, [(i, ((i + 1) ^ 1) - 1) for i in range(1, count - 1)]
+
+    swap_in, swap_out = pairs("gy")
+    y_inner = lax.ppermute(noisy_field, "gy", swap_in)
+    y_outer = lax.ppermute(noisy_field, "gy", swap_out)
     own = pl.pallas_call(
         join_kernel,
         out_shape=shape(128, 256),
@@ -471,11 +494,9 @@
         out_specs=VMEM,
         compiler_params=small(4),
         cost_estimate=cost(10**7, 2 * 10**5),
-    )(noisy_field, high, low, w_head)
-
-    count = lax.axis_size("gx")
-    in_chip = [(i, i ^ 1) for i in range(count)]
-    between = [(i, ((i + 1) ^ 1) - 1) for i in range(1, count - 1)]
+    )(noisy_field, y_inner, y_outer, w_head)
+
+    in_chip, between = pairs("gx")
     twin = lax.ppermute(own, "gx", in_chip)
     w_mid_skip, w_mid_up = pl.pallas_call(
         mid_weights_kernel,

time: 31.2 us -> 29.4 us (0.942)
  starting transfers between devices: 12.8 us -> 10.8 us
  waiting for transfers between devices: 5.11 us -> 5.52 us
    ppermute x2, starting transfers between devices: 5.58 us -> 3.56 us  [the longest x1 1.92 us: body(): y_outer = lax.ppermute(noisy_field, 'gy', swap_out)]
  transfers between devices with their start and end apart: 5 -> 5, of which waited for: 2 -> 2; matrix products, arithmetic and copies ran while one was open for 0% -> 0% of each run, Pallas kernels for 21% -> 22%
where the time goes in v4:
time: 29.4 us; the launch traced here: 29.2 us
  Pallas kernels  12.8 us (44%)
  starting transfers between devices  10.8 us (37%)
  waiting for transfers between devices  5.52 us (19%)
    pallas_call x1, Pallas kernels, body(): pl.pallas_call(net_kernel, out_shape=shape(16, 8, 128, kind=F32), in_spec...  6.15 us
    ppermute x1, starting transfers between devices, body(): chip_edge = lax.ppermute(edge, 'gx', between)  5.03 us
    ppermute x1, waiting for transfers between devices, body(): chip_edge = lax.ppermute(edge, 'gx', between)  3.2 us
    pallas_call x2, Pallas kernels, encoder(): pl.pallas_call(kernel, out_shape=(shape(6, x_rows, 32, 256), shape(4, 6,...  2.72 us
    ppermute x1, waiting for transfers between devices, body(): y_outer = lax.ppermute(noisy_field, 'gy', swap_out)  2.31 us
    ppermute x1, starting transfers between devices, body(): twin = lax.ppermute(own, 'gx', in_chip)  2.19 us
    ppermute x1, starting transfers between devices, body(): y_outer = lax.ppermute(noisy_field, 'gy', swap_out)  1.92 us
    ppermute x1, starting transfers between devices, body(): y_inner = lax.ppermute(noisy_field, 'gy', swap_in)  1.64 us
  transfers between devices with their start and end apart: 5, of which 2 were waited for; matrix products, arithmetic and copies ran while one was open for 0% of the time, Pallas kernels for 22%

profile of v4, /device:TPU:79, one launch (start us, length us, event | category | flops | bytes accessed | tf_op | source)
XLA Modules:
  0.0 29.2 jit_solution(7640039765603992104)
XLA Ops:
  0.0 0.0 copy-start
  0.0 1.6 %collective-permute-start = (bf16[16,8,128]{2,1,0:T(8,128)(2,1)}, bf16[16,8,128]{2,1,0:T(8,128)(2,1)S(1)}, u32[]{:S(2)}, u32[]{:S(2)}) collective-permute-start(bf16[16,8,128]{2,1,0:T(8,128)(2,1)} %own.1), channel_id=1, source_target_pairs={{0,1},{1,0},{2,3},{3,2},{4,5},{5,4},{6,7},{7,6},{8,9},{9,8},{10,11... | collective-permute-start | bytes 98312 | tf_op jit(solution)/shard_map/ppermute | solution.py:488
  1.6 1.9 %collective-permute-start.1 = (bf16[16,8,128]{2,1,0:T(8,128)(2,1)}, bf16[16,8,128]{2,1,0:T(8,128)(2,1)S(1)}, u32[]{:S(2)}, u32[]{:S(2)}) collective-permute-start(bf16[16,8,128]{2,1,0:T(8,128)(2,1)} %own.1), channel_id=1, source_target_pairs={{1,2},{2,1},{3,4},{4,3},{5,6},{6,5},{9,10},{10,9},{11,12},{12,11},... | collective-permute-start | bytes 98312 | tf_op jit(solution)/shard_map/ppermute | solution.py:489
  3.6 1.5 %shard_map.73 = (bf16[2,192,256]{2,1,0:T(8,128)(2,1)S(1)}, bf16[1152,256]{1,0:T(8,128)(2,1)S(1)}, bf16[1152,256]{1,0:T(8,128)(2,1)S(1)}, bf16[16,256]{1,0:T(8,12...) custom-call(bf16[9,3,16]{2,1,0:T(4,128)(2,1)} %bitcast.20, ...), custom_call_target="tpu_custom_call" | custom-call | flops 1000000000 | bytes 3000000 | tf_op jit(solution)/shard_map/pallas_call | solution.py:446
  5.1 0.0 collective-permute-done.inner
  5.1 2.3 %collective-permute-done.1.outer = bf16[16,8,128]{2,1,0:T(8,128)(2,1)S(1)} collective-permute-done((bf16[16,8,128]{2,1,0:T(8,128)(2,1)}, bf16[16,8,128]{2,1,0:T(8,128)(2,1)S(1)}, u32[]{:S(2)}, u32[]{:S(2)}) %collective-permute-start.1) | collective-permute-done | bytes 32800 | tf_op jit(solution)/shard_map/ppermute | solution.py:489
  7.4 0.0 copy-done
  7.4 0.2 shard_map.74.after.own
  7.6 2.2 %collective-permute-start.2 = (bf16[128,256]{1,0:T(8,128)(2,1)S(1)}, bf16[128,256]{1,0:T(8,128)(2,1)S(1)}, u32[]{:S(2)}, u32[]{:S(2)}) collective-permute-start(bf16[128,256]{1,0:T(8,128)(2,1)S(1)} %shard_map.74.after.own), channel_id=1, source_target_pairs={{0,8},{8,0},{16,24},{24,16},{32,40},{40,32},{48,56},{56,48},{64,72... | collective-permute-start | bytes 196616 | tf_op jit(solution)/shard_map/ppermute | solution.py:500
  9.8 1.3 %shard_map.75 = (bf16[2304,256]{1,0:T(8,128)(2,1)S(1)}, bf16[4,1024,256]{2,1,0:T(8,128)(2,1)S(1)}) custom-call(bf16[27,32,96]{2,1,0:T(8,128)(2,1)S(1)} %get-tuple-element.21.middle, bf16[128,256]{1,0:T(8,128)(2,1)S(1)} %shard_map.74.after.own), custom_call_target="tpu_custom_call" | custom-call | flops 1000000000 | bytes 4000000 | tf_op jit(solution)/shard_map/pallas_call | solution.py:501
  11.0 0.0 collective-permute-done.2.twin
  11.1 5.0 %collective-permute-start.3 = (bf16[176,256]{1,0:T(8,128)(2,1)S(1)}, bf16[176,256]{1,0:T(8,128)(2,1)S(1)}, u32[]{:S(2)}, u32[]{:S(2)}) collective-permute-start(bf16[176,256]{1,0:T(8,128)(2,1)S(1)} %shard_map.76.after), channel_id=1, source_target_pairs={{8,16},{16,8},{24,32},{32,24},{40,48},{48,40},{56,64},{64,56},{72,... | collective-permute-start | bytes 270344 | tf_op jit(solution)/shard_map/ppermute | solution.py:518
  16.1 1.4 %shard_map.78 = (bf16[6,7,32,256]{3,2,1,0:T(8,128)(2,1)S(1)}, bf16[4,6,48,128]{3,2,1,0:T(8,128)(2,1)S(1)}) custom-call(bf16[128,256]{1,0:T(8,128)(2,1)S(1)} %shard_map.74.after.own, bf16[128,256]{1,0:T(8,128)(2,1)S(1)} %collective-permute-done.2.twin, bf16[192,256]{1,0:T(8,128)(2,1)S(1)} %get-tuple-element.25.pick, ...), custom_call_target="tpu_custom_call" | custom-call | flops 2000000000 | bytes 3000000 | tf_op jit(solution)/shard_map/pallas_call | solution.py:521
  17.5 1.0 %shard_map.77 = (bf16[2304,256]{1,0:T(8,128)(2,1)S(1)}, bf16[4,1024,256]{2,1,0:T(8,128)(2,1)S(1)}) custom-call(bf16[27,16,48]{2,1,0:T(8,128)(2,1)S(1)} %get-tuple-element.23.fine, bf16[176,256]{1,0:T(8,128)(2,1)S(1)} %shard_map.76.after), custom_call_target="tpu_custom_call" | custom-call | flops 1000000000 | bytes 4000000 | tf_op jit(solution)/shard_map/pallas_call | solution.py:531
  18.4 3.2 %collective-permute-done.3.edge = bf16[176,256]{1,0:T(8,128)(2,1)S(1)} collective-permute-done((bf16[176,256]{1,0:T(8,128)(2,1)S(1)}, bf16[176,256]{1,0:T(8,128)(2,1)S(1)}, u32[]{:S(2)}, u32[]{:S(2)}) %collective-permute-start.3) | collective-permute-done | bytes 90144 | tf_op jit(solution)/shard_map/ppermute | solution.py:518
  21.7 0.0 collective-permute-start.4
  21.7 1.3 %shard_map.80 = (bf16[6,3,32,256]{3,2,1,0:T(8,128)(2,1)S(1)}, bf16[4,6,48,128]{3,2,1,0:T(8,128)(2,1)S(1)}) custom-call(bf16[128,256]{1,0:T(8,128)(2,1)S(1)} %shard_map.74.after.own, bf16[176,256]{1,0:T(8,128)(2,1)S(1)} %collective-permute-done.3.edge, bf16[192,256]{1,0:T(8,128)(2,1)S(1)} %get-tuple-element.25.pick, ...), custom_call_target="tpu_custom_call" | custom-call | flops 2000000000 | bytes 3000000 | tf_op jit(solution)/shard_map/pallas_call | solution.py:521
  23.0 0.0 collective-permute-done.4.twin_edge
  23.0 6.2 %shard_map.81 = f32[16,8,128]{2,1,0:T(8,128)} custom-call(bf16[128,256]{1,0:T(8,128)(2,1)S(1)} %collective-permute-done.2.twin, bf16[48,256]{1,0:T(8,128)(2,1)S(1)} %collective-permute-done.4.twin_edge, bf16[192,256]{1,0:T(8,128)(2,1)S(1)} %get-tuple-element.25.pick, bf16[6,7,32,256]{3,2,1,0:T(8,128)(2,1)S(1)} %get-tuple-element.28.fine_near, ...), custom_call_target="tpu_custom_call" | custom-call | flops 6000000000 | bytes 9000000 | tf_op jit(solution)/shard_map/pallas_call | solution.py:551
  (2 shorter events, 0.0 us)
Async XLA Ops:
  0.0 7.4 %copy-start = (bf16[16,8,128]{2,1,0:T(8,128)(2,1)S(1)}, bf16[16,8,128]{2,1,0:T(8,128)(2,1)}, u32[]{:S(2)}) copy-start(bf16[16,8,128]{2,1,0:T(8,128)(2,1)} %own.1) | copy-start | bytes 98308
  0.0 5.1 %collective-permute-start = (bf16[16,8,128]{2,1,0:T(8,128)(2,1)}, bf16[16,8,128]{2,1,0:T(8,128)(2,1)S(1)}, u32[]{:S(2)}, u32[]{:S(2)}) collective-permute-start(bf16[16,8,128]{2,1,0:T(8,128)(2,1)} %own.1), channel_id=1, source_target_pairs={{0,1},{1,0},{2,3},{3,2},{4,5},{5,4},{6,7},{7,6},{8,9},{9,8},{10,11... | collective-permute-start | bytes 98312 | tf_op jit(solution)/shard_map/ppermute | solution.py:488
  1.6 5.8 %collective-permute-start.1 = (bf16[16,8,128]{2,1,0:T(8,128)(2,1)}, bf16[16,8,128]{2,1,0:T(8,128)(2,1)S(1)}, u32[]{:S(2)}, u32[]{:S(2)}) collective-permute-start(bf16[16,8,128]{2,1,0:T(8,128)(2,1)} %own.1), channel_id=1, source_target_pairs={{1,2},{2,1},{3,4},{4,3},{5,6},{6,5},{9,10},{10,9},{11,12},{12,11},... | collective-permute-start | bytes 98312 | tf_op jit(solution)/shard_map/ppermute | solution.py:489
  7.6 3.5 %collective-permute-start.2 = (bf16[128,256]{1,0:T(8,128)(2,1)S(1)}, bf16[128,256]{1,0:T(8,128)(2,1)S(1)}, u32[]{:S(2)}, u32[]{:S(2)}) collective-permute-start(bf16[128,256]{1,0:T(8,128)(2,1)S(1)} %shard_map.74.after.own), channel_id=1, source_target_pairs={{0,8},{8,0},{16,24},{24,16},{32,40},{40,32},{48,56},{56,48},{64,72... | collective-permute-start | bytes 196616 | tf_op jit(solution)/shard_map/ppermute | solution.py:500
  11.1 10.6 %collective-permute-start.3 = (bf16[176,256]{1,0:T(8,128)(2,1)S(1)}, bf16[176,256]{1,0:T(8,128)(2,1)S(1)}, u32[]{:S(2)}, u32[]{:S(2)}) collective-permute-start(bf16[176,256]{1,0:T(8,128)(2,1)S(1)} %shard_map.76.after), channel_id=1, source_target_pairs={{8,16},{16,8},{24,32},{32,24},{40,48},{48,40},{56,64},{64,56},{72,... | collective-permute-start | bytes 270344 | tf_op jit(solution)/shard_map/ppermute | solution.py:518
  21.7 1.4 %collective-permute-start.4 = (bf16[48,256]{1,0:T(8,128)(2,1)S(1)}, bf16[48,256]{1,0:T(8,128)(2,1)S(1)}, u32[]{:S(2)}, u32[]{:S(2)}) collective-permute-start(bf16[48,256]{1,0:T(8,128)(2,1)S(1)} %shard_map.79.after), channel_id=1, source_target_pairs={{0,8},{8,0},{16,24},{24,16},{32,40},{40,32},{48,56},{56,48},{64,72... | collective-permute-start | bytes 73736 | tf_op jit(solution)/shard_map/ppermute | solution.py:548

commit v5 on v4

--- a/solution.py
+++ b/solution.py
@@ -213,11 +213,6 @@
     out[...] = jnp.where(odd, for_high, for_low)
 
 
-def twin_edge_kernel(edge, after, also_after, out):
-    odd = lax.axis_index("gx") % 2 == 1
-    out[...] = jnp.where(odd, edge[:48], edge[128:])
-
-
 def silu_half(h):
     return h + h * jnp.tanh(h)
 
@@ -226,29 +221,37 @@
     return jnp.where(cell_inside("gx", 2, cell), 1.0, 0.0)
 
 
-def encode(field, pick, w_first, first_pair, pairs, put_fine, put_pooled):
+def put_shifts(out, at, group, value):
+    out[group + 1, at] = value.astype(BF)
+    out[0 if group else 3, at] = pltpu.roll(value, 1 if group else J - 1, 0).astype(BF)
+
+
+def put_three(out, at, value):
+    out[0, at] = pltpu.roll(value, 1, 0).astype(BF)
+    out[1, at] = value.astype(BF)
+    out[2, at] = pltpu.roll(value, J - 1, 0).astype(BF)
+
+
+def encode(field, pick, w_first, pairs, fine, first_x, pooled, pooled_at):
     wide = field.astype(F32)
     shifted = [pltpu.roll(wide, 1, 1).astype(BF), field, pltpu.roll(wide, 255, 1).astype(BF)]
-    for at in range(pairs):
-        m = first_pair + at
+    for at, m in enumerate(pairs):
         window = jnp.concatenate([part[at * 32 : at * 32 + 64] for part in shifted], axis=0)
-        flag = row_flag(lax.shift_right_arithmetic(m, 1) if put_fine is None else m // 2)
-        lhs = (dot_nt(pick[...], window) * flag).astype(BF)
-        pooled = [jnp.zeros((J, 128), F32) for _ in range(2)]
+        lhs = (dot_nt(pick[...], window) * row_flag(m // 2)).astype(BF)
+        sums = [jnp.zeros((J, 128), F32) for _ in range(2)]
         for even in range(2):
             value = silu_half(dot(lhs, w_first[even])).reshape(4, J, 256)
             for part in range(2):
                 both = value[2 * part] + value[2 * part + 1]
-                pooled[part] = pooled[part] + both[:, :128] + both[:, 128:]
-            if put_fine is not None and -1 <= 2 * m + even <= 8:
+                sums[part] = sums[part] + both[:, :128] + both[:, 128:]
+            x = 2 * m + even
+            if fine is not None and -1 <= x <= 8:
                 for group in range(4):
-                    put_fine(group + 1, 2 * m + even, value[group, :32])
-                put_fine(0, 2 * m + even, pltpu.roll(value[3], 1, 0)[:32])
-                put_fine(5, 2 * m + even, pltpu.roll(value[0], J - 1, 0)[:32])
-        put_pooled(0, at, pltpu.roll(pooled[1], 1, 0))
-        put_pooled(1, at, pooled[0])
-        put_pooled(2, at, pooled[1])
-        put_pooled(3, at, pltpu.roll(pooled[0], J - 1, 0))
+                    fine[group + 1, x - first_x] = value[group, :32].astype(BF)
+                fine[0, x - first_x] = pltpu.roll(value[3], 1, 0)[:32].astype(BF)
+                fine[5, x - first_x] = pltpu.roll(value[0], J - 1, 0)[:32].astype(BF)
+        for part in range(2):
+            put_shifts(pooled, pooled_at + at, part, sums[part])
 
 
 def for_each_core(work):
@@ -263,88 +266,140 @@
         work(1)
 
 
-def encode_part(field, pick, w_first, first_pair, first_x, fine, pooled):
-    def put_fine(group, x, value):
-        fine[group, x - first_x] = value.astype(BF)
-
-    def put_pooled(group, at, value):
-        pooled[group, at] = value.astype(BF)
-
-    encode(field, pick, w_first, first_pair, 6, put_fine, put_pooled)
+def middle_rows(pool_s, w_down, first):
+    lhs = jnp.concatenate(
+        [
+            pool_s[dy : dy + 2, dx : dx + 4].reshape(8 * J, 128)
+            for dx in range(3)
+            for dy in range(3)
+        ],
+        axis=1,
+    )
+    value = silu_half(dot(lhs, w_down[...])).reshape(2, 4, J, 256)
+    mask = y_mask()
+    rows = [
+        [value[py, at] * (mask * row_flag((first + at) // 2)) for at in range(4)]
+        for py in range(2)
+    ]
+    pooled = []
+    for at in (0, 2):
+        cells = rows[0][at] + rows[0][at + 1] + rows[1][at] + rows[1][at + 1]
+        pooled.append(cells[:, :128] + cells[:, 128:])
+    return rows, pooled
+
+
+def y_mask():
+    return jnp.where(cell_inside("gy", 32, cell_of(iota((J, 256), 0))), 1.0, 0.0)
 
 
 def encode_near_kernel(own, twin, pick, w_first, after, fine, pooled):
     def work(core):
-        first, second = (twin, own) if core else (own, twin)
-        field = jnp.concatenate([first[16:], second[:112]], axis=0)
-        encode_part(field, pick, w_first, -3 if core else 1, -1 if core else 2, fine, pooled)
+        if core:
+            field = jnp.concatenate([twin[80:], own[:112]], axis=0)
+        else:
+            field = jnp.concatenate([own[16:], twin[:48]], axis=0)
+        pairs = range(-1, 3) if core else range(1, 5)
+        encode(field, pick, w_first, pairs, fine, -1 if core else 2, pooled, 0)
 
     for_each_core(work)
 
 
-def encode_far_kernel(own, edge, pick, w_first, after, fine, pooled):
+def skip_near_kernel(fine, w_fine_skip, out):
+    lhs = jnp.concatenate(
+        [
+            fine[dy : dy + 4, dx : dx + 5].reshape(640, 256)
+            for dx in range(3)
+            for dy in range(3)
+        ],
+        axis=1,
+    )
+    out[...] = dot(lhs, w_fine_skip[...]).reshape(4, 5, 32, 256)
+
+
+def encode_inner_kernel(
+    own, edge, pick, w_first, w_down, pool_near, after,
+    fine, pool_far, mid, pool_mid, for_twin, pool_s,
+):
     def work(core):
-        parts = [own[80:], edge[...]] if core else [edge[...], own[:48]]
-        field = jnp.concatenate(parts, axis=0)
-        encode_part(field, pick, w_first, 3 if core else -5, 6 if core else -1, fine, pooled)
+        if core:
+            field = jnp.concatenate([own[80:], edge[:48]], axis=0)
+        else:
+            field = jnp.concatenate([edge[128:], own[:48]], axis=0)
+        near, far = (0, 4) if core else (2, 0)
+        pairs = (3, 4) if core else (-1, 0)
+        encode(field, pick, w_first, pairs, fine, 6 if core else -1, pool_s, far)
+        pool_far[...] = pool_s[:, far : far + 2]
+        pool_s[:, near : near + 4] = pool_near[...]
+        rows, pooled = middle_rows(pool_s, w_down, 0)
+        for at in range(4):
+            for py in range(2):
+                put_shifts(mid, at, py, rows[py][at])
+        for at in range(2):
+            put_three(pool_mid, at, pooled[at])
+            for py in range(2):
+                sent = rows[py][at if core else at + 2].astype(BF)
+                for_twin[pl.ds((at * 2 + py) * J, J), :] = sent
+        for_twin[pl.ds(4 * J, J), :] = jnp.concatenate(pooled, axis=1).astype(BF)
 
     for_each_core(work)
 
 
+def encode_outer_kernel(
+    edge, pick, w_first, w_down, pool_far, after, mid, pool_mid, pool_s
+):
+    def work(core):
+        field = edge[16:] if core else edge[:160]
+        far, outer = (0, 2) if core else (4, 0)
+        pairs = range(5, 9) if core else range(-5, -1)
+        pool_s[:, far : far + 2] = pool_far[...]
+        encode(field, pick, w_first, pairs, None, 0, pool_s, outer)
+        rows, pooled = middle_rows(pool_s, w_down, 4 if core else -4)
+        for at in range(2):
+            put_three(pool_mid, at, pooled[at])
+            for py in range(2):
+                put_shifts(mid, at, py, rows[py][at if core else at + 2])
+
+    for_each_core(work)
+
+
 def net_kernel(
-    twin, twin_edge, pick, fine_near, pool_near, fine_far, pool_far,
-    w_first, w_down, w_coarse, w_mid_skip, w_mid_up, w_fine_skip, w_fine_up, w_head,
+    from_twin, fine_near, fine_far, skip_near, mid_in, mid_out, pool_mid_in, pool_mid_out,
+    w_coarse, w_mid_skip, w_mid_up, w_fine_skip, w_fine_up, w_head,
     out,
-    fine_s, pool_fine_s, mid_s, pool_mid_s, coarse_s, up_s, last_s,
+    fine_s, mid_s, pool_mid_s, coarse_s, up_s, skip_s, last_s,
 ):
-    y_mask = jnp.where(cell_inside("gy", 32, cell_of(iota((J, 256), 0))), 1.0, 0.0)
+    mask = y_mask()
 
     def gather(core):
+        first, last = (6, 0) if core else (0, 6)
+        mid_s[:, first : first + 2], mid_s[:, 2:6] = mid_out[...], mid_in[...]
+        cell = 4 if core else 0
+        pool_mid_s[:, cell : cell + 2], pool_mid_s[:, 2:4] = pool_mid_out[...], pool_mid_in[...]
+        for at in range(2):
+            for py in range(2):
+                row = (at * 2 + py) * J
+                put_shifts(mid_s, last + at, py, from_twin[row : row + J].astype(F32))
+            lanes = slice(at * 128, at * 128 + 128)
+            put_three(pool_mid_s, 4 - cell + at, from_twin[4 * J :, lanes].astype(F32))
         if core:
-            fine_s[:, 0:7], fine_s[:, 7:10] = fine_near[...], fine_far[...]
-            pool_fine_s[:, 2:8], pool_fine_s[:, 8:14] = pool_near[...], pool_far[...]
+            fine_s[:, 0:2], fine_s[:, 2:5] = fine_near[:, 5:7], fine_far[...]
         else:
-            fine_s[:, 0:3], fine_s[:, 3:10] = fine_far[...], fine_near[...]
-            pool_fine_s[:, 0:6], pool_fine_s[:, 6:12] = pool_far[...], pool_near[...]
-
-    for_each_core(gather)
-    odd = lax.axis_index("gx") % 2 == 1
-    rest, other = twin_edge[...], twin[...]
-    field = jnp.where(
-        odd,
-        jnp.concatenate([rest, other[:48]], axis=0),
-        jnp.concatenate([other[80:], rest], axis=0),
-    )
-    first_at = jnp.where(odd, 0, 12)
-
-    def put_pooled(group, at, value):
-        pool_fine_s[group, first_at + at] = value.astype(BF)
-
-    encode(field, pick, w_first, first_at - 5, 2, None, put_pooled)
-
-    sums = [jnp.zeros((J, 128), F32) for _ in range(6)]
-    for py in range(2):
+            fine_s[:, 0:3], fine_s[:, 3:5] = fine_far[...], fine_near[:, 0:2]
         lhs = jnp.concatenate(
             [
-                pool_fine_s[py + dy, dx : dx + 12].reshape(12 * J, 128)
+                fine_s[dy : dy + 4, dx : dx + 3].reshape(384, 256)
                 for dx in range(3)
                 for dy in range(3)
             ],
             axis=1,
         )
-        value = silu_half(dot(lhs, w_down[...])).reshape(12, J, 256)
-        for at in range(12):
-            m = at - 4
-            masked = value[at] * (y_mask * row_flag(m // 2))
-            sums[at // 2] = sums[at // 2] + masked[:, :128] + masked[:, 128:]
-            if -2 <= m <= 5:
-                mid_s[py + 1, m + 2] = masked.astype(BF)
-                shift = 1 if py else J - 1
-                mid_s[0 if py else 3, m + 2] = pltpu.roll(masked, shift, 0).astype(BF)
-    for at in range(6):
-        pool_mid_s[0, at] = pltpu.roll(sums[at], 1, 0).astype(BF)
-        pool_mid_s[1, at] = sums[at].astype(BF)
-        pool_mid_s[2, at] = pltpu.roll(sums[at], J - 1, 0).astype(BF)
+        skip = dot(lhs, w_fine_skip[...]).reshape(4, 3, 32, 256)
+        if core:
+            skip_s[:, 0:5], skip_s[:, 5:8] = skip_near[...], skip
+        else:
+            skip_s[:, 0:3], skip_s[:, 3:8] = skip, skip_near[...]
+
+    for_each_core(gather)
 
     lhs = jnp.concatenate(
         [
@@ -356,10 +411,7 @@
     )
     value = silu_half(dot(lhs, w_coarse[...])).reshape(4, J, 256)
     for at in range(4):
-        masked = value[at] * (y_mask * row_flag(at - 1))
-        coarse_s[0, at] = pltpu.roll(masked, 1, 0).astype(BF)
-        coarse_s[1, at] = masked.astype(BF)
-        coarse_s[2, at] = pltpu.roll(masked, J - 1, 0).astype(BF)
+        put_three(coarse_s, at, value[at] * (mask * row_flag(at - 1)))
 
     lhs = jnp.concatenate(
         [
@@ -384,20 +436,11 @@
             for k in range(3):
                 at = 2 * k if px else 2 * k + 1
                 value = silu_half(skip[py, at] + up[k])
-                masked = value * (y_mask * row_flag((at - 1) // 2))
+                masked = value * (mask * row_flag((at - 1) // 2))
                 up_s[py + 1, at] = masked[:32].astype(BF)
                 shift = 1 if py else J - 1
                 up_s[0 if py else 3, at] = pltpu.roll(masked, shift, 0)[:32].astype(BF)
 
-    lhs = jnp.concatenate(
-        [
-            fine_s[dy : dy + 4, dx : dx + 8].reshape(1024, 256)
-            for dx in range(3)
-            for dy in range(3)
-        ],
-        axis=1,
-    )
-    skip = dot(lhs, w_fine_skip[...]).reshape(4, 8, 32, 256)
     for py in range(2):
         for px in range(2):
             lhs = jnp.concatenate(
@@ -413,7 +456,7 @@
                 group = 2 * half + py
                 for k in range(4):
                     x = 2 * k + px
-                    value = silu_half(skip[group, x] + up[half, k])
+                    value = silu_half(skip_s[group, x] + up[half, k])
                     last_s[x, pl.ds(group * 32, 32), :] = value.astype(BF)
 
     heads = jnp.concatenate([dot_nt(w_head[...], last_s[x]) for x in range(8)], axis=0)
@@ -517,17 +560,14 @@
     )(own, twin, w_mid_skip)
     chip_edge = lax.ppermute(edge, "gx", between)
 
-    def encoder(kernel, x_rows, *operands):
-        return pl.pallas_call(
-            kernel,
-            out_shape=(shape(6, x_rows, 32, 256), shape(4, 6, J, 128)),
-            in_specs=[VMEM] * 4 + [ANY],
-            out_specs=(VMEM,) * 2,
-            compiler_params=small(16),
-            cost_estimate=cost(2 * 10**9, 3 * 10**6),
-        )(*operands)
-
-    fine_near, pool_near = encoder(encode_near_kernel, 7, own, twin, pick, w_first, edge)
+    fine_near, pool_near = pl.pallas_call(
+        encode_near_kernel,
+        out_shape=(shape(6, 7, 32, 256), shape(4, 4, J, 128)),
+        in_specs=[VMEM] * 4 + [ANY],
+        out_specs=(VMEM,) * 2,
+        compiler_params=small(16),
+        cost_estimate=cost(10**9, 3 * 10**6),
+    )(own, twin, pick, w_first, edge)
     w_fine_skip, w_fine_up = pl.pallas_call(
         fine_weights_kernel,
         out_shape=(shape(2304, 256), shape(4, 1024, 256)),
@@ -537,38 +577,62 @@
         compiler_params=small(16),
         cost_estimate=cost(10**9, 4 * 10**6),
     )(fine, edge)
-    rest = pl.pallas_call(
-        twin_edge_kernel,
-        out_shape=shape(48, 256),
-        in_specs=[VMEM, ANY, ANY],
+    skip_near = pl.pallas_call(
+        skip_near_kernel,
+        out_shape=shape(4, 5, 32, 256, kind=F32),
+        in_specs=[VMEM] * 2,
         out_specs=VMEM,
-        compiler_params=small(4),
-        cost_estimate=cost(10**5, 10**5),
-    )(chip_edge, w_fine_skip, pool_near)
-    twin_edge = lax.ppermute(rest, "gx", in_chip)
-    fine_far, pool_far = encoder(encode_far_kernel, 3, own, chip_edge, pick, w_first, rest)
+        compiler_params=small(16),
+        cost_estimate=cost(10**9, 2 * 10**6),
+    )(fine_near, w_fine_skip)
+
+    fine_far, pool_far, mid_in, pool_mid_in, for_twin = pl.pallas_call(
+        encode_inner_kernel,
+        out_shape=(
+            shape(6, 3, 32, 256),
+            shape(4, 2, J, 128),
+            shape(4, 4, J, 256),
+            shape(3, 2, J, 128),
+            shape(5 * J, 256),
+        ),
+        in_specs=[VMEM] * 6 + [ANY],
+        out_specs=(VMEM,) * 5,
+        scratch_shapes=[pltpu.VMEM((4, 6, J, 128), BF)],
+        compiler_params=small(16),
+        cost_estimate=cost(10**9, 3 * 10**6),
+    )(own, chip_edge, pick, w_first, w_down, pool_near, skip_near)
+    from_twin = lax.ppermute(for_twin, "gx", in_chip)
+    mid_out, pool_mid_out = pl.pallas_call(
+        encode_outer_kernel,
+        out_shape=(shape(4, 2, J, 256), shape(3, 2, J, 128)),
+        in_specs=[VMEM] * 5 + [ANY],
+        out_specs=(VMEM,) * 2,
+        scratch_shapes=[pltpu.VMEM((4, 6, J, 128), BF)],
+        compiler_params=small(16),
+        cost_estimate=cost(2 * 10**9, 3 * 10**6),
+    )(chip_edge, pick, w_first, w_down, pool_far, for_twin)
 
     return pl.pallas_call(
         net_kernel,
         out_shape=shape(16, 8, 128, kind=F32),
-        in_specs=[VMEM] * 15,
+        in_specs=[VMEM] * 14,
         out_specs=VMEM,
         scratch_shapes=[
-            pltpu.VMEM((6, 10, 32, 256), BF),
-            pltpu.VMEM((4, 14, J, 128), BF),
+            pltpu.VMEM((6, 5, 32, 256), BF),
             pltpu.VMEM((4, 8, J, 256), BF),
             pltpu.VMEM((3, 6, J, 128), BF),
             pltpu.VMEM((3, 4, J, 256), BF),
             pltpu.VMEM((4, 6, 32, 256), BF),
+            pltpu.VMEM((4, 8, 32, 256), F32),
             pltpu.VMEM((8, 128, 256), BF),
         ],
-        compiler_params=small(40),
+        compiler_params=small(32),
         cost_estimate=pl.CostEstimate(
             flops=6 * 10**9, bytes_accessed=9 * 10**6, transcendentals=10**6
         ),
     )(
-        twin, twin_edge, pick, fine_near, pool_near, fine_far, pool_far,
-        w_first, w_down, w_coarse, w_mid_skip, w_mid_up, w_fine_skip, w_fine_up, w_head,
+        from_twin, fine_near, fine_far, skip_near, mid_in, mid_out, pool_mid_in, pool_mid_out,
+        w_coarse, w_mid_skip, w_mid_up, w_fine_skip, w_fine_up, w_head,
     )
 
 

time: 29.4 us -> 29.2 us (level)
  waiting for transfers between devices: 5.52 us -> 5.03 us
    pallas_call x3 -> x4, Pallas kernels: 2.72 us -> 4.09 us  [the longest x1 1.26 us: body(): pl.pallas_call(encode_outer_kernel, out_shape=(shape(4, 2, J, 256), shape...]
    pallas_call x1, Pallas kernels: 6.15 us -> 5.01 us  [body(): pl.pallas_call(net_kernel, out_shape=shape(16, 8, 128, kind=F32), in_spec...]
    ppermute x1, waiting for transfers between devices: 3.2 us -> 2.66 us  [body(): chip_edge = lax.ppermute(edge, 'gx', between)]
  transfers between devices with their start and end apart: 5 -> 5, of which waited for: 2 -> 3; matrix products, arithmetic and copies ran while one was open for 0% -> 0% of each run, Pallas kernels for 22% -> 24%
where the time goes in v5:
time: 29.2 us; the launch traced here: 29 us
  Pallas kernels  13 us (45%)
  starting transfers between devices  10.9 us (37%)
  waiting for transfers between devices  5.03 us (17%)
    ppermute x1, starting transfers between devices, body(): chip_edge = lax.ppermute(edge, 'gx', between)  5.03 us
    pallas_call x1, Pallas kernels, body(): pl.pallas_call(net_kernel, out_shape=shape(16, 8, 128, kind=F32), in_spec...  5.01 us
    ppermute x1, waiting for transfers between devices, body(): chip_edge = lax.ppermute(edge, 'gx', between)  2.66 us
    ppermute x1, waiting for transfers between devices, body(): y_outer = lax.ppermute(noisy_field, 'gy', swap_out)  2.31 us
    ppermute x1, starting transfers between devices, body(): twin = lax.ppermute(own, 'gx', in_chip)  2.19 us
    ppermute x1, starting transfers between devices, body(): y_outer = lax.ppermute(noisy_field, 'gy', swap_out)  1.92 us
    ppermute x1, starting transfers between devices, body(): y_inner = lax.ppermute(noisy_field, 'gy', swap_in)  1.64 us
    pallas_call x1, Pallas kernels, body(): pl.pallas_call(encoder_weights_kernel, out_shape=(shape(2, 192, 256), sha...  1.49 us
  transfers between devices with their start and end apart: 5, of which 3 were waited for; matrix products, arithmetic and copies ran while one was open for 0% of the time, Pallas kernels for 24%

profile of v5, /device:TPU:79, one launch (start us, length us, event | category | flops | bytes accessed | tf_op | source)
XLA Modules:
  0.0 29.0 jit_solution(3145051266502337357)
XLA Ops:
  0.0 0.0 copy-start
  0.0 1.6 %collective-permute-start = (bf16[16,8,128]{2,1,0:T(8,128)(2,1)}, bf16[16,8,128]{2,1,0:T(8,128)(2,1)S(1)}, u32[]{:S(2)}, u32[]{:S(2)}) collective-permute-start(bf16[16,8,128]{2,1,0:T(8,128)(2,1)} %own.1), channel_id=1, source_target_pairs={{0,1},{1,0},{2,3},{3,2},{4,5},{5,4},{6,7},{7,6},{8,9},{9,8},{10,11... | collective-permute-start | bytes 98312 | tf_op jit(solution)/shard_map/ppermute | solution.py:531
  1.6 1.9 %collective-permute-start.1 = (bf16[16,8,128]{2,1,0:T(8,128)(2,1)}, bf16[16,8,128]{2,1,0:T(8,128)(2,1)S(1)}, u32[]{:S(2)}, u32[]{:S(2)}) collective-permute-start(bf16[16,8,128]{2,1,0:T(8,128)(2,1)} %own.1), channel_id=1, source_target_pairs={{1,2},{2,1},{3,4},{4,3},{5,6},{6,5},{9,10},{10,9},{11,12},{12,11},... | collective-permute-start | bytes 98312 | tf_op jit(solution)/shard_map/ppermute | solution.py:532
  3.6 1.5 %shard_map.73 = (bf16[2,192,256]{2,1,0:T(8,128)(2,1)S(1)}, bf16[1152,256]{1,0:T(8,128)(2,1)S(1)}, bf16[1152,256]{1,0:T(8,128)(2,1)S(1)}, bf16[16,256]{1,0:T(8,12...) custom-call(bf16[9,3,16]{2,1,0:T(4,128)(2,1)} %bitcast.20, ...), custom_call_target="tpu_custom_call" | custom-call | flops 1000000000 | bytes 3000000 | tf_op jit(solution)/shard_map/pallas_call | solution.py:489
  5.1 0.0 collective-permute-done.inner
  5.1 2.3 %collective-permute-done.1.outer = bf16[16,8,128]{2,1,0:T(8,128)(2,1)S(1)} collective-permute-done((bf16[16,8,128]{2,1,0:T(8,128)(2,1)}, bf16[16,8,128]{2,1,0:T(8,128)(2,1)S(1)}, u32[]{:S(2)}, u32[]{:S(2)}) %collective-permute-start.1) | collective-permute-done | bytes 32800 | tf_op jit(solution)/shard_map/ppermute | solution.py:532
  7.4 0.0 copy-done
  7.4 0.2 shard_map.74.after.own
  7.6 2.2 %collective-permute-start.2 = (bf16[128,256]{1,0:T(8,128)(2,1)S(1)}, bf16[128,256]{1,0:T(8,128)(2,1)S(1)}, u32[]{:S(2)}, u32[]{:S(2)}) collective-permute-start(bf16[128,256]{1,0:T(8,128)(2,1)S(1)} %shard_map.74.after.own), channel_id=1, source_target_pairs={{0,8},{8,0},{16,24},{24,16},{32,40},{40,32},{48,56},{56,48},{64,72... | collective-permute-start | bytes 196616 | tf_op jit(solution)/shard_map/ppermute | solution.py:543
  9.8 1.3 %shard_map.75 = (bf16[2304,256]{1,0:T(8,128)(2,1)S(1)}, bf16[4,1024,256]{2,1,0:T(8,128)(2,1)S(1)}) custom-call(bf16[27,32,96]{2,1,0:T(8,128)(2,1)S(1)} %get-tuple-element.26.middle, bf16[128,256]{1,0:T(8,128)(2,1)S(1)} %shard_map.74.after.own), custom_call_target="tpu_custom_call" | custom-call | flops 1000000000 | bytes 4000000 | tf_op jit(solution)/shard_map/pallas_call | solution.py:544
  11.0 0.0 collective-permute-done.2.twin
  11.1 5.0 %collective-permute-start.3 = (bf16[176,256]{1,0:T(8,128)(2,1)S(1)}, bf16[176,256]{1,0:T(8,128)(2,1)S(1)}, u32[]{:S(2)}, u32[]{:S(2)}) collective-permute-start(bf16[176,256]{1,0:T(8,128)(2,1)S(1)} %shard_map.76.after), channel_id=1, source_target_pairs={{8,16},{16,8},{24,32},{32,24},{40,48},{48,40},{56,64},{64,56},{72,... | collective-permute-start | bytes 270344 | tf_op jit(solution)/shard_map/ppermute | solution.py:561
  16.1 1.0 %shard_map.78 = (bf16[2304,256]{1,0:T(8,128)(2,1)S(1)}, bf16[4,1024,256]{2,1,0:T(8,128)(2,1)S(1)}) custom-call(bf16[27,16,48]{2,1,0:T(8,128)(2,1)S(1)} %get-tuple-element.33.fine, bf16[176,256]{1,0:T(8,128)(2,1)S(1)} %shard_map.76.after), custom_call_target="tpu_custom_call" | custom-call | flops 1000000000 | bytes 4000000 | tf_op jit(solution)/shard_map/pallas_call | solution.py:571
  17.1 1.0 %shard_map.77 = (bf16[6,7,32,256]{3,2,1,0:T(8,128)(2,1)S(1)}, bf16[4,4,48,128]{3,2,1,0:T(8,128)(2,1)S(1)}) custom-call(bf16[128,256]{1,0:T(8,128)(2,1)S(1)} %shard_map.74.after.own, bf16[128,256]{1,0:T(8,128)(2,1)S(1)} %collective-permute-done.2.twin, bf16[192,256]{1,0:T(8,128)(2,1)S(1)} %get-tuple-element.28.pick, ...), custom_call_target="tpu_custom_call" | custom-call | flops 1000000000 | bytes 3000000 | tf_op jit(solution)/shard_map/pallas_call | solution.py:563
  18.0 0.9 %shard_map.79.after.skip_near = f32[4,5,32,256]{3,2,1,0:T(8,128)S(1)} custom-call(bf16[6,7,32,256]{3,2,1,0:T(8,128)(2,1)S(1)} %get-tuple-element.32.fine.fine_near, bf16[2304,256]{1,0:T(8,128)(2,1)S(1)} %get-tuple-element.34.w_fine_skip), custom_call_target="tpu_custom_call" | custom-call | flops 1000000000 | bytes 2000000 | tf_op jit(solution)/shard_map/pallas_call | solution.py:580
  19.0 2.7 %collective-permute-done.3.edge = bf16[176,256]{1,0:T(8,128)(2,1)S(1)} collective-permute-done((bf16[176,256]{1,0:T(8,128)(2,1)S(1)}, bf16[176,256]{1,0:T(8,128)(2,1)S(1)}, u32[]{:S(2)}, u32[]{:S(2)}) %collective-permute-start.3) | collective-permute-done | bytes 90144 | tf_op jit(solution)/shard_map/ppermute | solution.py:561
  21.6 0.9 %shard_map.80 = (bf16[6,3,32,256]{3,2,1,0:T(8,128)(2,1)S(1)}, bf16[4,2,48,128]{3,2,1,0:T(8,128)(2,1)S(1)}, bf16[4,4,48,256]{3,2,1,0:T(8,128)(2,1)S(1)}, bf16[3,2...) custom-call(bf16[128,256]{1,0:T(8,128)(2,1)S(1)} %shard_map.74.after.own, ...), custom_call_target="tpu_custom_call" | custom-call | flops 1000000000 | bytes 3000000 | tf_op jit(solution)/shard_map/pallas_call | solution.py:589
  22.6 0.1 collective-permute-start.4
  22.7 1.3 %shard_map.81 = (bf16[4,2,48,256]{3,2,1,0:T(8,128)(2,1)S(1)}, bf16[3,2,48,128]{3,2,1,0:T(8,128)(2,1)S(1)}) custom-call(bf16[176,256]{1,0:T(8,128)(2,1)S(1)} %collective-permute-done.3.edge, bf16[192,256]{1,0:T(8,128)(2,1)S(1)} %get-tuple-element.28.pick, bf16[2,192,256]{2,1,0:T(8,128)(2,1)S(1)} %get-tuple-element.29.w_first, ...), custom_call_target="tpu_custom_call" | custom-call | flops 2000000000 | bytes 3000000 | tf_op jit(solution)/shard_map/pallas_call | solution.py:605
  24.0 0.1 collective-permute-done.4.from_twin
  24.0 5.0 %shard_map.82 = f32[16,8,128]{2,1,0:T(8,128)} custom-call(bf16[240,256]{1,0:T(8,128)(2,1)S(1)} %collective-permute-done.4.from_twin, bf16[6,7,32,256]{3,2,1,0:T(8,128)(2,1)S(1)} %get-tuple-element.32.fine.fine_near, bf16[6,3,32,256]{3,2,1,0:T(8,128)(2,1)S(1)} %get-tuple-element.36.fine_far, f32[4,5,32,256]{3,2,1,0:T(8,128)S(1)} %shard_map.79.after.skip_near, ...), custom_call_target="tpu_custom_call" | custom-call | flops 6000000000 | bytes 9000000 | tf_op jit(solution)/shard_map/pallas_call | solution.py:615
  (1 shorter events, 0.0 us)
Async XLA Ops:
  0.0 7.4 %copy-start = (bf16[16,8,128]{2,1,0:T(8,128)(2,1)S(1)}, bf16[16,8,128]{2,1,0:T(8,128)(2,1)}, u32[]{:S(2)}) copy-start(bf16[16,8,128]{2,1,0:T(8,128)(2,1)} %own.1) | copy-start | bytes 98308
  0.0 5.1 %collective-permute-start = (bf16[16,8,128]{2,1,0:T(8,128)(2,1)}, bf16[16,8,128]{2,1,0:T(8,128)(2,1)S(1)}, u32[]{:S(2)}, u32[]{:S(2)}) collective-permute-start(bf16[16,8,128]{2,1,0:T(8,128)(2,1)} %own.1), channel_id=1, source_target_pairs={{0,1},{1,0},{2,3},{3,2},{4,5},{5,4},{6,7},{7,6},{8,9},{9,8},{10,11... | collective-permute-start | bytes 98312 | tf_op jit(solution)/shard_map/ppermute | solution.py:531
  1.6 5.8 %collective-permute-start.1 = (bf16[16,8,128]{2,1,0:T(8,128)(2,1)}, bf16[16,8,128]{2,1,0:T(8,128)(2,1)S(1)}, u32[]{:S(2)}, u32[]{:S(2)}) collective-permute-start(bf16[16,8,128]{2,1,0:T(8,128)(2,1)} %own.1), channel_id=1, source_target_pairs={{1,2},{2,1},{3,4},{4,3},{5,6},{6,5},{9,10},{10,9},{11,12},{12,11},... | collective-permute-start | bytes 98312 | tf_op jit(solution)/shard_map/ppermute | solution.py:532
  7.6 3.5 %collective-permute-start.2 = (bf16[128,256]{1,0:T(8,128)(2,1)S(1)}, bf16[128,256]{1,0:T(8,128)(2,1)S(1)}, u32[]{:S(2)}, u32[]{:S(2)}) collective-permute-start(bf16[128,256]{1,0:T(8,128)(2,1)S(1)} %shard_map.74.after.own), channel_id=1, source_target_pairs={{0,8},{8,0},{16,24},{24,16},{32,40},{40,32},{48,56},{56,48},{64,72... | collective-permute-start | bytes 196616 | tf_op jit(solution)/shard_map/ppermute | solution.py:543
  11.1 10.6 %collective-permute-start.3 = (bf16[176,256]{1,0:T(8,128)(2,1)S(1)}, bf16[176,256]{1,0:T(8,128)(2,1)S(1)}, u32[]{:S(2)}, u32[]{:S(2)}) collective-permute-start(bf16[176,256]{1,0:T(8,128)(2,1)S(1)} %shard_map.76.after), channel_id=1, source_target_pairs={{8,16},{16,8},{24,32},{32,24},{40,48},{48,40},{56,64},{64,56},{72,... | collective-permute-start | bytes 270344 | tf_op jit(solution)/shard_map/ppermute | solution.py:561
  22.6 1.4 %collective-permute-start.4 = (bf16[240,256]{1,0:T(8,128)(2,1)S(1)}, bf16[240,256]{1,0:T(8,128)(2,1)S(1)}, u32[]{:S(2)}, u32[]{:S(2)}) collective-permute-start(bf16[240,256]{1,0:T(8,128)(2,1)S(1)} %get-tuple-element.35.after), channel_id=1, source_target_pairs={{0,8},{8,0},{16,24},{24,16},{32,40},{40,32},{48,56},{56,48},{64,72... | collective-permute-start | bytes 368648 | tf_op jit(solution)/shard_map/ppermute | solution.py:604

commit v6 on v5

--- a/solution.py
+++ b/solution.py
@@ -183,13 +183,11 @@
     folded(w_mid_up, lambda dz, dx, dy: tiled[dz * 9 + dx * 3 + dy, 0:64, :], 64, 4, natural(32))
 
 
-def fine_weights_kernel(fine, after, w_fine_skip, w_fine_up, tiled):
+def fine_weights_kernel(fine, after, w_fine_skip):
     r16 = repeat_matrix(16)
-    for tap in range(27):
-        tiled[tap] = dot_tn(fine[tap], r16) * 0.5
-    taps = [[tiled[dz * 9 + xy, 32:48, :].astype(BF) for xy in range(9)] for dz in range(3)]
+    tiled = [(dot_tn(fine[tap], r16)[32:] * 0.5).astype(BF) for tap in range(27)]
+    taps = [tiled[dz * 9 : dz * 9 + 9] for dz in range(3)]
     banded(w_fine_skip, taps, 16, list(range(0, 16, 2)) + list(range(1, 16, 2)), natural(16))
-    folded(w_fine_up, lambda dz, dx, dy: tiled[dz * 9 + dx * 3 + dy, 0:32, :], 32, 8, natural(16))
 
 
 def join_kernel(own, inner, outer, after, out):
@@ -235,23 +233,28 @@
 def encode(field, pick, w_first, pairs, fine, first_x, pooled, pooled_at):
     wide = field.astype(F32)
     shifted = [pltpu.roll(wide, 1, 1).astype(BF), field, pltpu.roll(wide, 255, 1).astype(BF)]
+    windows = []
     for at, m in enumerate(pairs):
         window = jnp.concatenate([part[at * 32 : at * 32 + 64] for part in shifted], axis=0)
-        lhs = (dot_nt(pick[...], window) * row_flag(m // 2)).astype(BF)
-        sums = [jnp.zeros((J, 128), F32) for _ in range(2)]
-        for even in range(2):
-            value = silu_half(dot(lhs, w_first[even])).reshape(4, J, 256)
+        windows.append((dot_nt(pick[...], window) * row_flag(m // 2)).astype(BF))
+    lhs = jnp.concatenate(windows, axis=0)
+    sums = [[jnp.zeros((J, 128), F32) for _ in range(2)] for _ in pairs]
+    for even in range(2):
+        values = silu_half(dot(lhs, w_first[even])).reshape(len(pairs), 4, J, 256)
+        for at, m in enumerate(pairs):
+            value = values[at]
             for part in range(2):
                 both = value[2 * part] + value[2 * part + 1]
-                sums[part] = sums[part] + both[:, :128] + both[:, 128:]
+                sums[at][part] = sums[at][part] + both[:, :128] + both[:, 128:]
             x = 2 * m + even
             if fine is not None and -1 <= x <= 8:
                 for group in range(4):
                     fine[group + 1, x - first_x] = value[group, :32].astype(BF)
                 fine[0, x - first_x] = pltpu.roll(value[3], 1, 0)[:32].astype(BF)
                 fine[5, x - first_x] = pltpu.roll(value[0], J - 1, 0)[:32].astype(BF)
+    for at in range(len(pairs)):
         for part in range(2):
-            put_shifts(pooled, pooled_at + at, part, sums[part])
+            put_shifts(pooled, pooled_at + at, part, sums[at][part])
 
 
 def for_each_core(work):
@@ -266,23 +269,23 @@
         work(1)
 
 
-def middle_rows(pool_s, w_down, first):
+def middle_rows(pool_s, w_down, first, count):
     lhs = jnp.concatenate(
         [
-            pool_s[dy : dy + 2, dx : dx + 4].reshape(8 * J, 128)
+            pool_s[dy : dy + 2, dx : dx + count].reshape(2 * count * J, 128)
             for dx in range(3)
             for dy in range(3)
         ],
         axis=1,
     )
-    value = silu_half(dot(lhs, w_down[...])).reshape(2, 4, J, 256)
+    value = silu_half(dot(lhs, w_down[...])).reshape(2, count, J, 256)
     mask = y_mask()
     rows = [
-        [value[py, at] * (mask * row_flag((first + at) // 2)) for at in range(4)]
+        [value[py, at] * (mask * row_flag((first + at) // 2)) for at in range(count)]
         for py in range(2)
     ]
     pooled = []
-    for at in (0, 2):
+    for at in range(0, count, 2):
         cells = rows[0][at] + rows[0][at + 1] + rows[1][at] + rows[1][at + 1]
         pooled.append(cells[:, :128] + cells[:, 128:])
     return rows, pooled
@@ -292,7 +295,9 @@
     return jnp.where(cell_inside("gy", 32, cell_of(iota((J, 256), 0))), 1.0, 0.0)
 
 
-def encode_near_kernel(own, twin, pick, w_first, after, fine, pooled):
+def encode_near_kernel(
+    own, twin, pick, w_first, w_down, after, fine, pooled, mid, pool_mid, for_twin
+):
     def work(core):
         if core:
             field = jnp.concatenate([twin[80:], own[:112]], axis=0)
@@ -300,46 +305,56 @@
             field = jnp.concatenate([own[16:], twin[:48]], axis=0)
         pairs = range(-1, 3) if core else range(1, 5)
         encode(field, pick, w_first, pairs, fine, -1 if core else 2, pooled, 0)
+        rows, cells = middle_rows(pooled, w_down, 0 if core else 2, 2)
+        for at in range(2):
+            for py in range(2):
+                put_shifts(mid, at, py, rows[py][at])
+                for_twin[pl.ds((at * 2 + py) * J, J), :] = rows[py][at].astype(BF)
+        pool_mid[...] = cells[0].astype(BF)
 
     for_each_core(work)
 
 
-def skip_near_kernel(fine, w_fine_skip, out):
+def skip_near_kernel(fine_near, fine, w_fine_skip, out, w_fine_up, tiled):
     lhs = jnp.concatenate(
         [
-            fine[dy : dy + 4, dx : dx + 5].reshape(640, 256)
+            fine_near[dy : dy + 4, dx : dx + 5].reshape(640, 256)
             for dx in range(3)
             for dy in range(3)
         ],
         axis=1,
     )
     out[...] = dot(lhs, w_fine_skip[...]).reshape(4, 5, 32, 256)
+    r16 = repeat_matrix(16)
+    for tap in range(27):
+        tiled[tap] = dot_tn(fine[tap], r16)[:32] * 0.5
+    folded(w_fine_up, lambda dz, dx, dy: tiled[dz * 9 + dx * 3 + dy], 32, 8, natural(16))
 
 
 def encode_inner_kernel(
-    own, edge, pick, w_first, w_down, pool_near, after,
+    own, edge, pick, w_first, w_down, pool_near, pool_mid_near, for_twin_near, after,
     fine, pool_far, mid, pool_mid, for_twin, pool_s,
 ):
     def work(core):
         if core:
             field = jnp.concatenate([own[80:], edge[:48]], axis=0)
+            pool_s[:, 0:2] = pool_near[:, 2:4]
         else:
             field = jnp.concatenate([edge[128:], own[:48]], axis=0)
-        near, far = (0, 4) if core else (2, 0)
-        pairs = (3, 4) if core else (-1, 0)
+            pool_s[:, 2:4] = pool_near[:, 0:2]
+        pairs, far = ((3, 4), 2) if core else ((-1, 0), 0)
         encode(field, pick, w_first, pairs, fine, 6 if core else -1, pool_s, far)
         pool_far[...] = pool_s[:, far : far + 2]
-        pool_s[:, near : near + 4] = pool_near[...]
-        rows, pooled = middle_rows(pool_s, w_down, 0)
-        for at in range(4):
+        rows, pooled = middle_rows(pool_s, w_down, 2 if core else 0, 2)
+        for at in range(2):
             for py in range(2):
                 put_shifts(mid, at, py, rows[py][at])
+        near = pool_mid_near[...].astype(F32)
+        cells = (near, pooled[0]) if core else (pooled[0], near)
         for at in range(2):
-            put_three(pool_mid, at, pooled[at])
-            for py in range(2):
-                sent = rows[py][at if core else at + 2].astype(BF)
-                for_twin[pl.ds((at * 2 + py) * J, J), :] = sent
-        for_twin[pl.ds(4 * J, J), :] = jnp.concatenate(pooled, axis=1).astype(BF)
+            put_three(pool_mid, at, cells[at])
+        for_twin[pl.ds(0, 4 * J), :] = for_twin_near[...]
+        for_twin[pl.ds(4 * J, J), :] = jnp.concatenate(cells, axis=1).astype(BF)
 
     for_each_core(work)
 
@@ -353,7 +368,7 @@
         pairs = range(5, 9) if core else range(-5, -1)
         pool_s[:, far : far + 2] = pool_far[...]
         encode(field, pick, w_first, pairs, None, 0, pool_s, outer)
-        rows, pooled = middle_rows(pool_s, w_down, 4 if core else -4)
+        rows, pooled = middle_rows(pool_s, w_down, 4 if core else -4, 4)
         for at in range(2):
             put_three(pool_mid, at, pooled[at])
             for py in range(2):
@@ -363,7 +378,8 @@
 
 
 def net_kernel(
-    from_twin, fine_near, fine_far, skip_near, mid_in, mid_out, pool_mid_in, pool_mid_out,
+    from_twin, fine_near, fine_far, skip_near, mid_near, mid_far, mid_out,
+    pool_mid_in, pool_mid_out,
     w_coarse, w_mid_skip, w_mid_up, w_fine_skip, w_fine_up, w_head,
     out,
     fine_s, mid_s, pool_mid_s, coarse_s, up_s, skip_s, last_s,
@@ -372,7 +388,9 @@
 
     def gather(core):
         first, last = (6, 0) if core else (0, 6)
-        mid_s[:, first : first + 2], mid_s[:, 2:6] = mid_out[...], mid_in[...]
+        near, far = (2, 4) if core else (4, 2)
+        mid_s[:, first : first + 2] = mid_out[...]
+        mid_s[:, near : near + 2], mid_s[:, far : far + 2] = mid_near[...], mid_far[...]
         cell = 4 if core else 0
         pool_mid_s[:, cell : cell + 2], pool_mid_s[:, 2:4] = pool_mid_out[...], pool_mid_in[...]
         for at in range(2):
@@ -383,23 +401,22 @@
             put_three(pool_mid_s, 4 - cell + at, from_twin[4 * J :, lanes].astype(F32))
         if core:
             fine_s[:, 0:2], fine_s[:, 2:5] = fine_near[:, 5:7], fine_far[...]
+            skip_s[:, 0:5] = skip_near[...]
         else:
             fine_s[:, 0:3], fine_s[:, 3:5] = fine_far[...], fine_near[:, 0:2]
-        lhs = jnp.concatenate(
-            [
-                fine_s[dy : dy + 4, dx : dx + 3].reshape(384, 256)
-                for dx in range(3)
-                for dy in range(3)
-            ],
-            axis=1,
-        )
-        skip = dot(lhs, w_fine_skip[...]).reshape(4, 3, 32, 256)
-        if core:
-            skip_s[:, 0:5], skip_s[:, 5:8] = skip_near[...], skip
-        else:
-            skip_s[:, 0:3], skip_s[:, 3:8] = skip, skip_near[...]
+            skip_s[:, 3:8] = skip_near[...]
 
     for_each_core(gather)
+    lhs = jnp.concatenate(
+        [
+            fine_s[dy : dy + 4, dx : dx + 3].reshape(384, 256)
+            for dx in range(3)
+            for dy in range(3)
+        ],
+        axis=1,
+    )
+    skip_far = dot(lhs, w_fine_skip[...]).reshape(4, 3, 32, 256)
+    skip_s[:, pl.ds(lax.axis_index("gx") % 2 * 5, 3)] = skip_far
 
     lhs = jnp.concatenate(
         [
@@ -441,8 +458,11 @@
                 shift = 1 if py else J - 1
                 up_s[0 if py else 3, at] = pltpu.roll(masked, shift, 0)[:32].astype(BF)
 
-    for py in range(2):
-        for px in range(2):
+    row, col = iota((128, 128), 0), iota((128, 128), 1)
+    order = (col == 4 * (row % 32) + row // 32).astype(BF)
+    orders = jnp.concatenate([order, order, order], axis=0)
+    for px in range(2):
+        for py in range(2):
             lhs = jnp.concatenate(
                 [
                     up_s[py + ty : py + ty + 2, px + tx : px + tx + 4].reshape(256, 256)
@@ -455,23 +475,18 @@
             for half in range(2):
                 group = 2 * half + py
                 for k in range(4):
-                    x = 2 * k + px
-                    value = silu_half(skip_s[group, x] + up[half, k])
-                    last_s[x, pl.ds(group * 32, 32), :] = value.astype(BF)
-
-    heads = jnp.concatenate([dot_nt(w_head[...], last_s[x]) for x in range(8)], axis=0)
-    high = heads.astype(BF)
-    rest = heads - high.astype(F32)
-    low = rest.astype(BF)
-    lowest = (rest - low.astype(F32)).astype(BF)
-    row, col = iota((128, 128), 0), iota((128, 128), 1)
-    order = (col == 4 * (row % 32) + row // 32).astype(BF)
-    noise = dot(
-        jnp.concatenate([high, low, lowest], axis=1),
-        jnp.concatenate([order, order, order], axis=0),
-    ).reshape(8, 16, 128)
-    for x in range(8):
-        out[:, x, :] = noise[x]
+                    value = silu_half(skip_s[group, 2 * k + px] + up[half, k])
+                    last_s[2 * k + px, pl.ds(group * 32, 32), :] = value.astype(BF)
+        heads = jnp.concatenate(
+            [dot_nt(w_head[...], last_s[2 * k + px]) for k in range(4)], axis=0
+        )
+        high = heads.astype(BF)
+        rest = heads - high.astype(F32)
+        low = rest.astype(BF)
+        lowest = (rest - low.astype(F32)).astype(BF)
+        noise = dot(jnp.concatenate([high, low, lowest], axis=1), orders).reshape(4, 16, 128)
+        for k in range(4):
+            out[:, 2 * k + px, :] = noise[k]
 
 
 def body(
@@ -560,47 +575,56 @@
     )(own, twin, w_mid_skip)
     chip_edge = lax.ppermute(edge, "gx", between)
 
-    fine_near, pool_near = pl.pallas_call(
+    fine_near, pool_near, mid_near, pool_mid_near, for_twin_near = pl.pallas_call(
         encode_near_kernel,
-        out_shape=(shape(6, 7, 32, 256), shape(4, 4, J, 128)),
-        in_specs=[VMEM] * 4 + [ANY],
-        out_specs=(VMEM,) * 2,
+        out_shape=(
+            shape(6, 7, 32, 256),
+            shape(4, 4, J, 128),
+            shape(4, 2, J, 256),
+            shape(J, 128),
+            shape(4 * J, 256),
+        ),
+        in_specs=[VMEM] * 5 + [ANY],
+        out_specs=(VMEM,) * 5,
         compiler_params=small(16),
         cost_estimate=cost(10**9, 3 * 10**6),
-    )(own, twin, pick, w_first, edge)
-    w_fine_skip, w_fine_up = pl.pallas_call(
+    )(own, twin, pick, w_first, w_down, edge)
+    w_fine_skip = pl.pallas_call(
         fine_weights_kernel,
-        out_shape=(shape(2304, 256), shape(4, 1024, 256)),
+        out_shape=shape(2304, 256),
         in_specs=[VMEM, ANY],
-        out_specs=(VMEM,) * 2,
-        scratch_shapes=[pltpu.VMEM((27, 48, 256), F32)],
-        compiler_params=small(16),
-        cost_estimate=cost(10**9, 4 * 10**6),
-    )(fine, edge)
-    skip_near = pl.pallas_call(
-        skip_near_kernel,
-        out_shape=shape(4, 5, 32, 256, kind=F32),
-        in_specs=[VMEM] * 2,
         out_specs=VMEM,
         compiler_params=small(16),
         cost_estimate=cost(10**9, 2 * 10**6),
-    )(fine_near, w_fine_skip)
-
-    fine_far, pool_far, mid_in, pool_mid_in, for_twin = pl.pallas_call(
+    )(fine, edge)
+    skip_near, w_fine_up = pl.pallas_call(
+        skip_near_kernel,
+        out_shape=(shape(4, 5, 32, 256, kind=F32), shape(4, 1024, 256)),
+        in_specs=[VMEM] * 3,
+        out_specs=(VMEM,) * 2,
+        scratch_shapes=[pltpu.VMEM((27, 32, 256), F32)],
+        compiler_params=small(16),
+        cost_estimate=cost(10**9, 4 * 10**6),
+    )(fine_near, fine, w_fine_skip)
+
+    fine_far, pool_far, mid_far, pool_mid_in, for_twin = pl.pallas_call(
         encode_inner_kernel,
         out_shape=(
             shape(6, 3, 32, 256),
             shape(4, 2, J, 128),
-            shape(4, 4, J, 256),
+            shape(4, 2, J, 256),
             shape(3, 2, J, 128),
             shape(5 * J, 256),
         ),
-        in_specs=[VMEM] * 6 + [ANY],
+        in_specs=[VMEM] * 8 + [ANY],
         out_specs=(VMEM,) * 5,
-        scratch_shapes=[pltpu.VMEM((4, 6, J, 128), BF)],
+        scratch_shapes=[pltpu.VMEM((4, 4, J, 128), BF)],
         compiler_params=small(16),
         cost_estimate=cost(10**9, 3 * 10**6),
-    )(own, chip_edge, pick, w_first, w_down, pool_near, skip_near)
+    )(
+        own, chip_edge, pick, w_first, w_down, pool_near, pool_mid_near, for_twin_near,
+        skip_near,
+    )
     from_twin = lax.ppermute(for_twin, "gx", in_chip)
     mid_out, pool_mid_out = pl.pallas_call(
         encode_outer_kernel,
@@ -615,7 +639,7 @@
     return pl.pallas_call(
         net_kernel,
         out_shape=shape(16, 8, 128, kind=F32),
-        in_specs=[VMEM] * 14,
+        in_specs=[VMEM] * 15,
         out_specs=VMEM,
         scratch_shapes=[
             pltpu.VMEM((6, 5, 32, 256), BF),
@@ -631,7 +655,8 @@
             flops=6 * 10**9, bytes_accessed=9 * 10**6, transcendentals=10**6
         ),
     )(
-        from_twin, fine_near, fine_far, skip_near, mid_in, mid_out, pool_mid_in, pool_mid_out,
+        from_twin, fine_near, fine_far, skip_near, mid_near, mid_far, mid_out,
+        pool_mid_in, pool_mid_out,
         w_coarse, w_mid_skip, w_mid_up, w_fine_skip, w_fine_up, w_head,
     )
 

time: 29.2 us -> 29.5 us (1.010)
  Pallas kernels: 13 us -> 13.4 us
  transfers between devices with their start and end apart: 5 -> 5, of which waited for: 3 -> 2; matrix products, arithmetic and copies ran while one was open for 0% -> 0% of each run, Pallas kernels for 24% -> 24%
where the time goes in v6:
time: 29.5 us; the launch traced here: 29.3 us
  Pallas kernels  13.4 us (45%)
  starting transfers between devices  10.9 us (37%)
  waiting for transfers between devices  4.91 us (17%)
    pallas_call x1, Pallas kernels, body(): pl.pallas_call(net_kernel, out_shape=shape(16, 8, 128, kind=F32), in_spec...  5.24 us
    ppermute x1, starting transfers between devices, body(): chip_edge = lax.ppermute(edge, 'gx', between)  5.03 us
    ppermute x1, waiting for transfers between devices, body(): chip_edge = lax.ppermute(edge, 'gx', between)  2.59 us
    ppermute x1, waiting for transfers between devices, body(): y_outer = lax.ppermute(noisy_field, 'gy', swap_out)  2.31 us
    ppermute x1, starting transfers between devices, body(): twin = lax.ppermute(own, 'gx', in_chip)  2.19 us
    ppermute x1, starting transfers between devices, body(): y_outer = lax.ppermute(noisy_field, 'gy', swap_out)  1.92 us
    ppermute x1, starting transfers between devices, body(): y_inner = lax.ppermute(noisy_field, 'gy', swap_in)  1.64 us
    pallas_call x1, Pallas kernels, body(): pl.pallas_call(encoder_weights_kernel, out_shape=(shape(2, 192, 256), sha...  1.49 us
  transfers between devices with their start and end apart: 5, of which 2 were waited for; matrix products, arithmetic and copies ran while one was open for 0% of the time, Pallas kernels for 24%

profile of v6, /device:TPU:79, one launch (start us, length us, event | category | flops | bytes accessed | tf_op | source)
XLA Modules:
  0.0 29.3 jit_solution(14031905348854054969)
XLA Ops:
  0.0 0.0 copy-start
  0.0 1.6 %collective-permute-start = (bf16[16,8,128]{2,1,0:T(8,128)(2,1)}, bf16[16,8,128]{2,1,0:T(8,128)(2,1)S(1)}, u32[]{:S(2)}, u32[]{:S(2)}) collective-permute-start(bf16[16,8,128]{2,1,0:T(8,128)(2,1)} %own.1), channel_id=1, source_target_pairs={{0,1},{1,0},{2,3},{3,2},{4,5},{5,4},{6,7},{7,6},{8,9},{9,8},{10,11... | collective-permute-start | bytes 98312 | tf_op jit(solution)/shard_map/ppermute | solution.py:546
  1.6 1.9 %collective-permute-start.1 = (bf16[16,8,128]{2,1,0:T(8,128)(2,1)}, bf16[16,8,128]{2,1,0:T(8,128)(2,1)S(1)}, u32[]{:S(2)}, u32[]{:S(2)}) collective-permute-start(bf16[16,8,128]{2,1,0:T(8,128)(2,1)} %own.1), channel_id=1, source_target_pairs={{1,2},{2,1},{3,4},{4,3},{5,6},{6,5},{9,10},{10,9},{11,12},{12,11},... | collective-permute-start | bytes 98312 | tf_op jit(solution)/shard_map/ppermute | solution.py:547
  3.6 1.5 %shard_map.73 = (bf16[2,192,256]{2,1,0:T(8,128)(2,1)S(1)}, bf16[1152,256]{1,0:T(8,128)(2,1)S(1)}, bf16[1152,256]{1,0:T(8,128)(2,1)S(1)}, bf16[16,256]{1,0:T(8,12...) custom-call(bf16[9,3,16]{2,1,0:T(4,128)(2,1)} %bitcast.20, ...), custom_call_target="tpu_custom_call" | custom-call | flops 1000000000 | bytes 3000000 | tf_op jit(solution)/shard_map/pallas_call | solution.py:504
  5.1 0.0 collective-permute-done.inner
  5.1 2.3 %collective-permute-done.1.outer = bf16[16,8,128]{2,1,0:T(8,128)(2,1)S(1)} collective-permute-done((bf16[16,8,128]{2,1,0:T(8,128)(2,1)}, bf16[16,8,128]{2,1,0:T(8,128)(2,1)S(1)}, u32[]{:S(2)}, u32[]{:S(2)}) %collective-permute-start.1) | collective-permute-done | bytes 32800 | tf_op jit(solution)/shard_map/ppermute | solution.py:547
  7.4 0.0 copy-done
  7.4 0.2 shard_map.74.after.own
  7.6 2.2 %collective-permute-start.2 = (bf16[128,256]{1,0:T(8,128)(2,1)S(1)}, bf16[128,256]{1,0:T(8,128)(2,1)S(1)}, u32[]{:S(2)}, u32[]{:S(2)}) collective-permute-start(bf16[128,256]{1,0:T(8,128)(2,1)S(1)} %shard_map.74.after.own), channel_id=1, source_target_pairs={{0,8},{8,0},{16,24},{24,16},{32,40},{40,32},{48,56},{56,48},{64,72... | collective-permute-start | bytes 196616 | tf_op jit(solution)/shard_map/ppermute | solution.py:558
  9.8 1.3 %shard_map.75 = (bf16[2304,256]{1,0:T(8,128)(2,1)S(1)}, bf16[4,1024,256]{2,1,0:T(8,128)(2,1)S(1)}) custom-call(bf16[27,32,96]{2,1,0:T(8,128)(2,1)S(1)} %get-tuple-element.29.middle, bf16[128,256]{1,0:T(8,128)(2,1)S(1)} %shard_map.74.after.own), custom_call_target="tpu_custom_call" | custom-call | flops 1000000000 | bytes 4000000 | tf_op jit(solution)/shard_map/pallas_call | solution.py:559
  11.0 0.0 collective-permute-done.2.twin
  11.1 5.0 %collective-permute-start.3 = (bf16[176,256]{1,0:T(8,128)(2,1)S(1)}, bf16[176,256]{1,0:T(8,128)(2,1)S(1)}, u32[]{:S(2)}, u32[]{:S(2)}) collective-permute-start(bf16[176,256]{1,0:T(8,128)(2,1)S(1)} %shard_map.76.after), channel_id=1, source_target_pairs={{8,16},{16,8},{24,32},{32,24},{40,48},{48,40},{56,64},{64,56},{72,... | collective-permute-start | bytes 270344 | tf_op jit(solution)/shard_map/ppermute | solution.py:576
  16.1 0.4 %shard_map.78.w_fine_skip = bf16[2304,256]{1,0:T(8,128)(2,1)S(1)} custom-call(bf16[27,16,48]{2,1,0:T(8,128)(2,1)S(1)} %get-tuple-element.38.fine, bf16[176,256]{1,0:T(8,128)(2,1)S(1)} %shard_map.76.after), custom_call_target="tpu_custom_call" | custom-call | flops 1000000000 | bytes 2000000 | tf_op jit(solution)/shard_map/pallas_call | solution.py:592
  16.5 1.1 %shard_map.77 = (bf16[6,7,32,256]{3,2,1,0:T(8,128)(2,1)S(1)}, bf16[4,4,48,128]{3,2,1,0:T(8,128)(2,1)S(1)}, bf16[4,2,48,256]{3,2,1,0:T(8,128)(2,1)S(1)}, bf16[48,128]{1,0:T(8,128)(2,1)S(1)}, bf16[192,256]{1,0:T(8,128)(2,1)S(1)}) custom-call(bf16[128,256]{1,0:T(8,128)(2,1)S(1)} %shard_map.74.after.own, bf16[128,256]{1,0:T(8,128)(2,1)S(1)} %collective-permute-done.2.twin, ...), custom_call_target="tpu_custom_call" | custom-call | flops 1000000000 | bytes 3000000 | tf_op jit(solution)/shard_map/pallas_call | solution.py:578
  17.6 1.4 %shard_map.79 = (f32[4,5,32,256]{3,2,1,0:T(8,128)S(1)}, bf16[4,1024,256]{2,1,0:T(8,128)(2,1)S(1)}) custom-call(bf16[6,7,32,256]{3,2,1,0:T(8,128)(2,1)S(1)} %get-tuple-element.37.fine_near, bf16[27,16,48]{2,1,0:T(8,128)(2,1)S(1)} %get-tuple-element.38.fine, bf16[2304,256]{1,0:T(8,128)(2,1)S(1)} %shard_map.78.w_fine_skip), custom_call_target="tpu_custom_call" | custom-call | flops 1000000000 | bytes 4000000 | tf_op jit(solution)/shard_map/pallas_call | solution.py:600
  19.1 2.6 %collective-permute-done.3.edge = bf16[176,256]{1,0:T(8,128)(2,1)S(1)} collective-permute-done((bf16[176,256]{1,0:T(8,128)(2,1)S(1)}, bf16[176,256]{1,0:T(8,128)(2,1)S(1)}, u32[]{:S(2)}, u32[]{:S(2)}) %collective-permute-start.3) | collective-permute-done | bytes 90144 | tf_op jit(solution)/shard_map/ppermute | solution.py:576
  21.6 0.9 %shard_map.80 = (bf16[6,3,32,256]{3,2,1,0:T(8,128)(2,1)S(1)}, bf16[4,2,48,128]{3,2,1,0:T(8,128)(2,1)S(1)}, bf16[4,2,48,256]{3,2,1,0:T(8,128)(2,1)S(1)}, bf16[3,2...) custom-call(bf16[128,256]{1,0:T(8,128)(2,1)S(1)} %shard_map.74.after.own, ...), custom_call_target="tpu_custom_call" | custom-call | flops 1000000000 | bytes 3000000 | tf_op jit(solution)/shard_map/pallas_call | solution.py:610
  22.5 0.1 collective-permute-start.4
  22.6 1.4 %shard_map.81 = (bf16[4,2,48,256]{3,2,1,0:T(8,128)(2,1)S(1)}, bf16[3,2,48,128]{3,2,1,0:T(8,128)(2,1)S(1)}) custom-call(bf16[176,256]{1,0:T(8,128)(2,1)S(1)} %collective-permute-done.3.edge, bf16[192,256]{1,0:T(8,128)(2,1)S(1)} %get-tuple-element.31.pick, bf16[2,192,256]{2,1,0:T(8,128)(2,1)S(1)} %get-tuple-element.32.w_first, ...), custom_call_target="tpu_custom_call" | custom-call | flops 2000000000 | bytes 3000000 | tf_op jit(solution)/shard_map/pallas_call | solution.py:629
  24.0 0.0 collective-permute-done.4.from_twin
  24.0 5.2 %shard_map.82 = f32[16,8,128]{2,1,0:T(8,128)} custom-call(bf16[240,256]{1,0:T(8,128)(2,1)S(1)} %collective-permute-done.4.from_twin, bf16[6,7,32,256]{3,2,1,0:T(8,128)(2,1)S(1)} %get-tuple-element.37.fine_near, bf16[6,3,32,256]{3,2,1,0:T(8,128)(2,1)S(1)} %get-tuple-element.41.fine_far, f32[4,5,32,256]{3,2,1,0:T(8,128)S(1)} %get-tuple-element.39.after.skip_near, ...), custom_call_target="tpu_custom_call" | custom-call | flops 6000000000 | bytes 9000000 | tf_op jit(solution)/shard_map/pallas_call | solution.py:639
  (1 shorter events, 0.0 us)
Async XLA Ops:
  0.0 7.4 %copy-start = (bf16[16,8,128]{2,1,0:T(8,128)(2,1)S(1)}, bf16[16,8,128]{2,1,0:T(8,128)(2,1)}, u32[]{:S(2)}) copy-start(bf16[16,8,128]{2,1,0:T(8,128)(2,1)} %own.1) | copy-start | bytes 98308
  0.0 5.1 %collective-permute-start = (bf16[16,8,128]{2,1,0:T(8,128)(2,1)}, bf16[16,8,128]{2,1,0:T(8,128)(2,1)S(1)}, u32[]{:S(2)}, u32[]{:S(2)}) collective-permute-start(bf16[16,8,128]{2,1,0:T(8,128)(2,1)} %own.1), channel_id=1, source_target_pairs={{0,1},{1,0},{2,3},{3,2},{4,5},{5,4},{6,7},{7,6},{8,9},{9,8},{10,11... | collective-permute-start | bytes 98312 | tf_op jit(solution)/shard_map/ppermute | solution.py:546
  1.6 5.8 %collective-permute-start.1 = (bf16[16,8,128]{2,1,0:T(8,128)(2,1)}, bf16[16,8,128]{2,1,0:T(8,128)(2,1)S(1)}, u32[]{:S(2)}, u32[]{:S(2)}) collective-permute-start(bf16[16,8,128]{2,1,0:T(8,128)(2,1)} %own.1), channel_id=1, source_target_pairs={{1,2},{2,1},{3,4},{4,3},{5,6},{6,5},{9,10},{10,9},{11,12},{12,11},... | collective-permute-start | bytes 98312 | tf_op jit(solution)/shard_map/ppermute | solution.py:547
  7.6 3.5 %collective-permute-start.2 = (bf16[128,256]{1,0:T(8,128)(2,1)S(1)}, bf16[128,256]{1,0:T(8,128)(2,1)S(1)}, u32[]{:S(2)}, u32[]{:S(2)}) collective-permute-start(bf16[128,256]{1,0:T(8,128)(2,1)S(1)} %shard_map.74.after.own), channel_id=1, source_target_pairs={{0,8},{8,0},{16,24},{24,16},{32,40},{40,32},{48,56},{56,48},{64,72... | collective-permute-start | bytes 196616 | tf_op jit(solution)/shard_map/ppermute | solution.py:558
  11.1 10.6 %collective-permute-start.3 = (bf16[176,256]{1,0:T(8,128)(2,1)S(1)}, bf16[176,256]{1,0:T(8,128)(2,1)S(1)}, u32[]{:S(2)}, u32[]{:S(2)}) collective-permute-start(bf16[176,256]{1,0:T(8,128)(2,1)S(1)} %shard_map.76.after), channel_id=1, source_target_pairs={{8,16},{16,8},{24,32},{32,24},{40,48},{48,40},{56,64},{64,56},{72,... | collective-permute-start | bytes 270344 | tf_op jit(solution)/shard_map/ppermute | solution.py:576
  22.5 1.5 %collective-permute-start.4 = (bf16[240,256]{1,0:T(8,128)(2,1)S(1)}, bf16[240,256]{1,0:T(8,128)(2,1)S(1)}, u32[]{:S(2)}, u32[]{:S(2)}) collective-permute-start(bf16[240,256]{1,0:T(8,128)(2,1)S(1)} %get-tuple-element.40.after), channel_id=1, source_target_pairs={{0,8},{8,0},{16,24},{24,16},{32,40},{40,32},{48,56},{56,48},{64,72... | collective-permute-start | bytes 368648 | tf_op jit(solution)/shard_map/ppermute | solution.py:628

commit v7 on v6

--- a/solution.py
+++ b/solution.py
@@ -147,7 +147,7 @@
 
     w_first[...] = jnp.zeros_like(w_first)
     for dx in range(3):
-        rows = [dot(first[dz * 3 + dx], r16) * 0.5 for dz in range(3)]
+        rows = [dot(first[dz * 3 + dx], r16) for dz in range(3)]
         place = halves(16)(iota((16, 256), 1))
         depth = iota((16, 256), 0)
         for dy in range(3):
@@ -159,12 +159,12 @@
                 w_first[even, pl.ds(dy * 64 + (even + dx) * 16, 16), :] = block
 
     flat = down[...].reshape(27 * 16, 32)
-    all_taps = (dot(flat, r32) * (1 / 16)).astype(BF)
+    all_taps = (dot(flat, r32) * (1 / 8)).astype(BF)
     taps = [[all_taps[(dz * 9 + xy) * 16 : (dz * 9 + xy + 1) * 16] for xy in range(9)] for dz in range(3)]
     banded(w_down, taps, 16, list(range(8)), halves(32))
 
     flat = coarse[...].reshape(27 * 32, 64)
-    all_taps = (dot(flat, r64) * (1 / 16)).astype(BF)
+    all_taps = (dot(flat, r64) * (1 / 8)).astype(BF)
     taps = [[all_taps[(dz * 9 + xy) * 32 : (dz * 9 + xy + 1) * 32] for xy in range(9)] for dz in range(3)]
     banded(w_coarse, taps, 32, list(range(4)), natural(64))
 
@@ -177,7 +177,7 @@
 def mid_weights_kernel(middle, after, w_mid_skip, w_mid_up, tiled):
     r32 = repeat_matrix(32)
     for tap in range(27):
-        tiled[tap] = dot_tn(middle[tap], r32) * 0.5
+        tiled[tap] = dot_tn(middle[tap], r32)
     taps = [[tiled[dz * 9 + xy, 64:96, :].astype(BF) for xy in range(9)] for dz in range(3)]
     banded(w_mid_skip, taps, 32, [0, 2, 4, 6, 1, 3, 5, 7], natural(32))
     folded(w_mid_up, lambda dz, dx, dy: tiled[dz * 9 + dx * 3 + dy, 0:64, :], 64, 4, natural(32))
@@ -185,7 +185,7 @@
 
 def fine_weights_kernel(fine, after, w_fine_skip):
     r16 = repeat_matrix(16)
-    tiled = [(dot_tn(fine[tap], r16)[32:] * 0.5).astype(BF) for tap in range(27)]
+    tiled = [dot_tn(fine[tap], r16)[32:].astype(BF) for tap in range(27)]
     taps = [tiled[dz * 9 : dz * 9 + 9] for dz in range(3)]
     banded(w_fine_skip, taps, 16, list(range(0, 16, 2)) + list(range(1, 16, 2)), natural(16))
 
@@ -211,8 +211,8 @@
     out[...] = jnp.where(odd, for_high, for_low)
 
 
-def silu_half(h):
-    return h + h * jnp.tanh(h)
+def silu(u):
+    return u * (1.0 / (1.0 + jnp.exp(-u)))
 
 
 def row_flag(cell):
@@ -233,28 +233,23 @@
 def encode(field, pick, w_first, pairs, fine, first_x, pooled, pooled_at):
     wide = field.astype(F32)
     shifted = [pltpu.roll(wide, 1, 1).astype(BF), field, pltpu.roll(wide, 255, 1).astype(BF)]
-    windows = []
     for at, m in enumerate(pairs):
         window = jnp.concatenate([part[at * 32 : at * 32 + 64] for part in shifted], axis=0)
-        windows.append((dot_nt(pick[...], window) * row_flag(m // 2)).astype(BF))
-    lhs = jnp.concatenate(windows, axis=0)
-    sums = [[jnp.zeros((J, 128), F32) for _ in range(2)] for _ in pairs]
-    for even in range(2):
-        values = silu_half(dot(lhs, w_first[even])).reshape(len(pairs), 4, J, 256)
-        for at, m in enumerate(pairs):
-            value = values[at]
+        lhs = (dot_nt(pick[...], window) * row_flag(m // 2)).astype(BF)
+        sums = [jnp.zeros((J, 128), F32) for _ in range(2)]
+        for even in range(2):
+            value = silu(dot(lhs, w_first[even])).reshape(4, J, 256)
             for part in range(2):
                 both = value[2 * part] + value[2 * part + 1]
-                sums[at][part] = sums[at][part] + both[:, :128] + both[:, 128:]
+                sums[part] = sums[part] + both[:, :128] + both[:, 128:]
             x = 2 * m + even
             if fine is not None and -1 <= x <= 8:
                 for group in range(4):
                     fine[group + 1, x - first_x] = value[group, :32].astype(BF)
                 fine[0, x - first_x] = pltpu.roll(value[3], 1, 0)[:32].astype(BF)
                 fine[5, x - first_x] = pltpu.roll(value[0], J - 1, 0)[:32].astype(BF)
-    for at in range(len(pairs)):
         for part in range(2):
-            put_shifts(pooled, pooled_at + at, part, sums[at][part])
+            put_shifts(pooled, pooled_at + at, part, sums[part])
 
 
 def for_each_core(work):
@@ -278,7 +273,7 @@
         ],
         axis=1,
     )
-    value = silu_half(dot(lhs, w_down[...])).reshape(2, count, J, 256)
+    value = silu(dot(lhs, w_down[...])).reshape(2, count, J, 256)
     mask = y_mask()
     rows = [
         [value[py, at] * (mask * row_flag((first + at) // 2)) for at in range(count)]
@@ -327,7 +322,7 @@
     out[...] = dot(lhs, w_fine_skip[...]).reshape(4, 5, 32, 256)
     r16 = repeat_matrix(16)
     for tap in range(27):
-        tiled[tap] = dot_tn(fine[tap], r16)[:32] * 0.5
+        tiled[tap] = dot_tn(fine[tap], r16)[:32]
     folded(w_fine_up, lambda dz, dx, dy: tiled[dz * 9 + dx * 3 + dy], 32, 8, natural(16))
 
 
@@ -401,22 +396,23 @@
             put_three(pool_mid_s, 4 - cell + at, from_twin[4 * J :, lanes].astype(F32))
         if core:
             fine_s[:, 0:2], fine_s[:, 2:5] = fine_near[:, 5:7], fine_far[...]
-            skip_s[:, 0:5] = skip_near[...]
         else:
             fine_s[:, 0:3], fine_s[:, 3:5] = fine_far[...], fine_near[:, 0:2]
-            skip_s[:, 3:8] = skip_near[...]
+        lhs = jnp.concatenate(
+            [
+                fine_s[dy : dy + 4, dx : dx + 3].reshape(384, 256)
+                for dx in range(3)
+                for dy in range(3)
+            ],
+            axis=1,
+        )
+        skip = dot(lhs, w_fine_skip[...]).reshape(4, 3, 32, 256)
+        if core:
+            skip_s[:, 0:5], skip_s[:, 5:8] = skip_near[...], skip
+        else:
+            skip_s[:, 0:3], skip_s[:, 3:8] = skip, skip_near[...]
 
     for_each_core(gather)
-    lhs = jnp.concatenate(
-        [
-            fine_s[dy : dy + 4, dx : dx + 3].reshape(384, 256)
-            for dx in range(3)
-            for dy in range(3)
-        ],
-        axis=1,
-    )
-    skip_far = dot(lhs, w_fine_skip[...]).reshape(4, 3, 32, 256)
-    skip_s[:, pl.ds(lax.axis_index("gx") % 2 * 5, 3)] = skip_far
 
     lhs = jnp.concatenate(
         [
@@ -426,7 +422,7 @@
         ],
         axis=1,
     )
-    value = silu_half(dot(lhs, w_coarse[...])).reshape(4, J, 256)
+    value = silu(dot(lhs, w_coarse[...])).reshape(4, J, 256)
     for at in range(4):
         put_three(coarse_s, at, value[at] * (mask * row_flag(at - 1)))
 
@@ -452,17 +448,14 @@
             up = dot(lhs, w_mid_up[px * 2 + py]).reshape(3, J, 256)
             for k in range(3):
                 at = 2 * k if px else 2 * k + 1
-                value = silu_half(skip[py, at] + up[k])
+                value = silu(skip[py, at] + up[k])
                 masked = value * (mask * row_flag((at - 1) // 2))
                 up_s[py + 1, at] = masked[:32].astype(BF)
                 shift = 1 if py else J - 1
                 up_s[0 if py else 3, at] = pltpu.roll(masked, shift, 0)[:32].astype(BF)
 
-    row, col = iota((128, 128), 0), iota((128, 128), 1)
-    order = (col == 4 * (row % 32) + row // 32).astype(BF)
-    orders = jnp.concatenate([order, order, order], axis=0)
-    for px in range(2):
-        for py in range(2):
+    for py in range(2):
+        for px in range(2):
             lhs = jnp.concatenate(
                 [
                     up_s[py + ty : py + ty + 2, px + tx : px + tx + 4].reshape(256, 256)
@@ -475,18 +468,23 @@
             for half in range(2):
                 group = 2 * half + py
                 for k in range(4):
-                    value = silu_half(skip_s[group, 2 * k + px] + up[half, k])
-                    last_s[2 * k + px, pl.ds(group * 32, 32), :] = value.astype(BF)
-        heads = jnp.concatenate(
-            [dot_nt(w_head[...], last_s[2 * k + px]) for k in range(4)], axis=0
-        )
-        high = heads.astype(BF)
-        rest = heads - high.astype(F32)
-        low = rest.astype(BF)
-        lowest = (rest - low.astype(F32)).astype(BF)
-        noise = dot(jnp.concatenate([high, low, lowest], axis=1), orders).reshape(4, 16, 128)
-        for k in range(4):
-            out[:, 2 * k + px, :] = noise[k]
+                    x = 2 * k + px
+                    value = silu(skip_s[group, x] + up[half, k])
+                    last_s[x, pl.ds(group * 32, 32), :] = value.astype(BF)
+
+    heads = jnp.concatenate([dot_nt(w_head[...], last_s[x]) for x in range(8)], axis=0)
+    high = heads.astype(BF)
+    rest = heads - high.astype(F32)
+    low = rest.astype(BF)
+    lowest = (rest - low.astype(F32)).astype(BF)
+    row, col = iota((128, 128), 0), iota((128, 128), 1)
+    order = (col == 4 * (row % 32) + row // 32).astype(BF)
+    noise = dot(
+        jnp.concatenate([high, low, lowest], axis=1),
+        jnp.concatenate([order, order, order], axis=0),
+    ).reshape(8, 16, 128)
+    for x in range(8):
+        out[:, x, :] = noise[x]
 
 
 def body(

time: 29.5 us -> 29.3 us (level)
  waiting for transfers between devices: 4.91 us -> 4.51 us
    pallas_call x1, Pallas kernels: 1.06 us -> 1.47 us  [body(): pl.pallas_call(encode_near_kernel, out_shape=(shape(6, 7, 32, 256), shape...]
    ppermute x1, waiting for transfers between devices: 2.59 us -> 2.19 us  [body(): chip_edge = lax.ppermute(edge, 'gx', between)]
  transfers between devices with their start and end apart: 5 -> 5, of which waited for: 2 -> 2; matrix products, arithmetic and copies ran while one was open for 0% -> 0% of each run, Pallas kernels for 24% -> 25%
where the time goes in v7:
time: 29.3 us; the launch traced here: 29.1 us
  Pallas kernels  13.6 us (46%)
  starting transfers between devices  10.9 us (37%)
  waiting for transfers between devices  4.51 us (15%)
    ppermute x1, starting transfers between devices, body(): chip_edge = lax.ppermute(edge, 'gx', between)  5.09 us
    pallas_call x1, Pallas kernels, body(): pl.pallas_call(net_kernel, out_shape=shape(16, 8, 128, kind=F32), in_spec...  5.04 us
    ppermute x1, waiting for transfers between devices, body(): y_outer = lax.ppermute(noisy_field, 'gy', swap_out)  2.31 us
    ppermute x1, waiting for transfers between devices, body(): chip_edge = lax.ppermute(edge, 'gx', between)  2.19 us
    ppermute x1, starting transfers between devices, body(): twin = lax.ppermute(own, 'gx', in_chip)  2.19 us
    ppermute x1, starting transfers between devices, body(): y_outer = lax.ppermute(noisy_field, 'gy', swap_out)  1.92 us
    ppermute x1, starting transfers between devices, body(): y_inner = lax.ppermute(noisy_field, 'gy', swap_in)  1.64 us
    pallas_call x1, Pallas kernels, body(): pl.pallas_call(encoder_weights_kernel, out_shape=(shape(2, 192, 256), sha...  1.5 us
  transfers between devices with their start and end apart: 5, of which 2 were waited for; matrix products, arithmetic and copies ran while one was open for 0% of the time, Pallas kernels for 25%

profile of v7, /device:TPU:79, one launch (start us, length us, event | category | flops | bytes accessed | tf_op | source)
XLA Modules:
  0.0 29.1 jit_solution(1278437593138085726)
XLA Ops:
  0.0 0.0 copy-start
  0.0 1.6 %collective-permute-start = (bf16[16,8,128]{2,1,0:T(8,128)(2,1)}, bf16[16,8,128]{2,1,0:T(8,128)(2,1)S(1)}, u32[]{:S(2)}, u32[]{:S(2)}) collective-permute-start(bf16[16,8,128]{2,1,0:T(8,128)(2,1)} %own.1), channel_id=1, source_target_pairs={{0,1},{1,0},{2,3},{3,2},{4,5},{5,4},{6,7},{7,6},{8,9},{9,8},{10,11... | collective-permute-start | bytes 98312 | tf_op jit(solution)/shard_map/ppermute | solution.py:544
  1.6 1.9 %collective-permute-start.1 = (bf16[16,8,128]{2,1,0:T(8,128)(2,1)}, bf16[16,8,128]{2,1,0:T(8,128)(2,1)S(1)}, u32[]{:S(2)}, u32[]{:S(2)}) collective-permute-start(bf16[16,8,128]{2,1,0:T(8,128)(2,1)} %own.1), channel_id=1, source_target_pairs={{1,2},{2,1},{3,4},{4,3},{5,6},{6,5},{9,10},{10,9},{11,12},{12,11},... | collective-permute-start | bytes 98312 | tf_op jit(solution)/shard_map/ppermute | solution.py:545
  3.6 1.5 %shard_map.73 = (bf16[2,192,256]{2,1,0:T(8,128)(2,1)S(1)}, bf16[1152,256]{1,0:T(8,128)(2,1)S(1)}, bf16[1152,256]{1,0:T(8,128)(2,1)S(1)}, bf16[16,256]{1,0:T(8,12...) custom-call(bf16[9,3,16]{2,1,0:T(4,128)(2,1)} %bitcast.20, ...), custom_call_target="tpu_custom_call" | custom-call | flops 1000000000 | bytes 3000000 | tf_op jit(solution)/shard_map/pallas_call | solution.py:502
  5.1 0.0 collective-permute-done.inner
  5.1 2.3 %collective-permute-done.1.outer = bf16[16,8,128]{2,1,0:T(8,128)(2,1)S(1)} collective-permute-done((bf16[16,8,128]{2,1,0:T(8,128)(2,1)}, bf16[16,8,128]{2,1,0:T(8,128)(2,1)S(1)}, u32[]{:S(2)}, u32[]{:S(2)}) %collective-permute-start.1) | collective-permute-done | bytes 32800 | tf_op jit(solution)/shard_map/ppermute | solution.py:545
  7.4 0.0 copy-done
  7.4 0.2 shard_map.74.after.own
  7.6 2.2 %collective-permute-start.2 = (bf16[128,256]{1,0:T(8,128)(2,1)S(1)}, bf16[128,256]{1,0:T(8,128)(2,1)S(1)}, u32[]{:S(2)}, u32[]{:S(2)}) collective-permute-start(bf16[128,256]{1,0:T(8,128)(2,1)S(1)} %shard_map.74.after.own), channel_id=1, source_target_pairs={{0,8},{8,0},{16,24},{24,16},{32,40},{40,32},{48,56},{56,48},{64,72... | collective-permute-start | bytes 196616 | tf_op jit(solution)/shard_map/ppermute | solution.py:556
  9.8 1.1 %shard_map.75 = (bf16[2304,256]{1,0:T(8,128)(2,1)S(1)}, bf16[4,1024,256]{2,1,0:T(8,128)(2,1)S(1)}) custom-call(bf16[27,32,96]{2,1,0:T(8,128)(2,1)S(1)} %get-tuple-element.29.middle, bf16[128,256]{1,0:T(8,128)(2,1)S(1)} %shard_map.74.after.own), custom_call_target="tpu_custom_call" | custom-call | flops 1000000000 | bytes 4000000 | tf_op jit(solution)/shard_map/pallas_call | solution.py:557
  10.9 0.0 collective-permute-done.2.twin
  10.9 5.1 %collective-permute-start.3 = (bf16[176,256]{1,0:T(8,128)(2,1)S(1)}, bf16[176,256]{1,0:T(8,128)(2,1)S(1)}, u32[]{:S(2)}, u32[]{:S(2)}) collective-permute-start(bf16[176,256]{1,0:T(8,128)(2,1)S(1)} %shard_map.76.after), channel_id=1, source_target_pairs={{8,16},{16,8},{24,32},{32,24},{40,48},{48,40},{56,64},{64,56},{72,... | collective-permute-start | bytes 270344 | tf_op jit(solution)/shard_map/ppermute | solution.py:574
  16.0 0.4 %shard_map.78.w_fine_skip = bf16[2304,256]{1,0:T(8,128)(2,1)S(1)} custom-call(bf16[27,16,48]{2,1,0:T(8,128)(2,1)S(1)} %get-tuple-element.38.fine, bf16[176,256]{1,0:T(8,128)(2,1)S(1)} %shard_map.76.after), custom_call_target="tpu_custom_call" | custom-call | flops 1000000000 | bytes 2000000 | tf_op jit(solution)/shard_map/pallas_call | solution.py:590
  16.5 1.5 %shard_map.77 = (bf16[6,7,32,256]{3,2,1,0:T(8,128)(2,1)S(1)}, bf16[4,4,48,128]{3,2,1,0:T(8,128)(2,1)S(1)}, bf16[4,2,48,256]{3,2,1,0:T(8,128)(2,1)S(1)}, bf16[48,128]{1,0:T(8,128)(2,1)S(1)}, bf16[192,256]{1,0:T(8,128)(2,1)S(1)}) custom-call(bf16[128,256]{1,0:T(8,128)(2,1)S(1)} %shard_map.74.after.own, bf16[128,256]{1,0:T(8,128)(2,1)S(1)} %collective-permute-done.2.twin, ...), custom_call_target="tpu_custom_call" | custom-call | flops 1000000000 | bytes 3000000 | tf_op jit(solution)/shard_map/pallas_call | solution.py:576
  18.0 1.4 %shard_map.79 = (f32[4,5,32,256]{3,2,1,0:T(8,128)S(1)}, bf16[4,1024,256]{2,1,0:T(8,128)(2,1)S(1)}) custom-call(bf16[6,7,32,256]{3,2,1,0:T(8,128)(2,1)S(1)} %get-tuple-element.37.fine_near, bf16[27,16,48]{2,1,0:T(8,128)(2,1)S(1)} %get-tuple-element.38.fine, bf16[2304,256]{1,0:T(8,128)(2,1)S(1)} %shard_map.78.w_fine_skip), custom_call_target="tpu_custom_call" | custom-call | flops 1000000000 | bytes 4000000 | tf_op jit(solution)/shard_map/pallas_call | solution.py:598
  19.3 2.2 %collective-permute-done.3.edge = bf16[176,256]{1,0:T(8,128)(2,1)S(1)} collective-permute-done((bf16[176,256]{1,0:T(8,128)(2,1)S(1)}, bf16[176,256]{1,0:T(8,128)(2,1)S(1)}, u32[]{:S(2)}, u32[]{:S(2)}) %collective-permute-start.3) | collective-permute-done | bytes 90144 | tf_op jit(solution)/shard_map/ppermute | solution.py:574
  21.5 1.0 %shard_map.80 = (bf16[6,3,32,256]{3,2,1,0:T(8,128)(2,1)S(1)}, bf16[4,2,48,128]{3,2,1,0:T(8,128)(2,1)S(1)}, bf16[4,2,48,256]{3,2,1,0:T(8,128)(2,1)S(1)}, bf16[3,2...) custom-call(bf16[128,256]{1,0:T(8,128)(2,1)S(1)} %shard_map.74.after.own, ...), custom_call_target="tpu_custom_call" | custom-call | flops 1000000000 | bytes 3000000 | tf_op jit(solution)/shard_map/pallas_call | solution.py:608
  22.6 0.1 collective-permute-start.4
  22.7 1.4 %shard_map.81 = (bf16[4,2,48,256]{3,2,1,0:T(8,128)(2,1)S(1)}, bf16[3,2,48,128]{3,2,1,0:T(8,128)(2,1)S(1)}) custom-call(bf16[176,256]{1,0:T(8,128)(2,1)S(1)} %collective-permute-done.3.edge, bf16[192,256]{1,0:T(8,128)(2,1)S(1)} %get-tuple-element.31.pick, bf16[2,192,256]{2,1,0:T(8,128)(2,1)S(1)} %get-tuple-element.32.w_first, ...), custom_call_target="tpu_custom_call" | custom-call | flops 2000000000 | bytes 3000000 | tf_op jit(solution)/shard_map/pallas_call | solution.py:627
  24.1 0.0 collective-permute-done.4.from_twin
  24.1 5.0 %shard_map.82 = f32[16,8,128]{2,1,0:T(8,128)} custom-call(bf16[240,256]{1,0:T(8,128)(2,1)S(1)} %collective-permute-done.4.from_twin, bf16[6,7,32,256]{3,2,1,0:T(8,128)(2,1)S(1)} %get-tuple-element.37.fine_near, bf16[6,3,32,256]{3,2,1,0:T(8,128)(2,1)S(1)} %get-tuple-element.41.fine_far, f32[4,5,32,256]{3,2,1,0:T(8,128)S(1)} %get-tuple-element.39.after.skip_near, ...), custom_call_target="tpu_custom_call" | custom-call | flops 6000000000 | bytes 9000000 | tf_op jit(solution)/shard_map/pallas_call | solution.py:637
  (1 shorter events, 0.0 us)
Async XLA Ops:
  0.0 7.4 %copy-start = (bf16[16,8,128]{2,1,0:T(8,128)(2,1)S(1)}, bf16[16,8,128]{2,1,0:T(8,128)(2,1)}, u32[]{:S(2)}) copy-start(bf16[16,8,128]{2,1,0:T(8,128)(2,1)} %own.1) | copy-start | bytes 98308
  0.0 5.1 %collective-permute-start = (bf16[16,8,128]{2,1,0:T(8,128)(2,1)}, bf16[16,8,128]{2,1,0:T(8,128)(2,1)S(1)}, u32[]{:S(2)}, u32[]{:S(2)}) collective-permute-start(bf16[16,8,128]{2,1,0:T(8,128)(2,1)} %own.1), channel_id=1, source_target_pairs={{0,1},{1,0},{2,3},{3,2},{4,5},{5,4},{6,7},{7,6},{8,9},{9,8},{10,11... | collective-permute-start | bytes 98312 | tf_op jit(solution)/shard_map/ppermute | solution.py:544
  1.6 5.8 %collective-permute-start.1 = (bf16[16,8,128]{2,1,0:T(8,128)(2,1)}, bf16[16,8,128]{2,1,0:T(8,128)(2,1)S(1)}, u32[]{:S(2)}, u32[]{:S(2)}) collective-permute-start(bf16[16,8,128]{2,1,0:T(8,128)(2,1)} %own.1), channel_id=1, source_target_pairs={{1,2},{2,1},{3,4},{4,3},{5,6},{6,5},{9,10},{10,9},{11,12},{12,11},... | collective-permute-start | bytes 98312 | tf_op jit(solution)/shard_map/ppermute | solution.py:545
  7.6 3.3 %collective-permute-start.2 = (bf16[128,256]{1,0:T(8,128)(2,1)S(1)}, bf16[128,256]{1,0:T(8,128)(2,1)S(1)}, u32[]{:S(2)}, u32[]{:S(2)}) collective-permute-start(bf16[128,256]{1,0:T(8,128)(2,1)S(1)} %shard_map.74.after.own), channel_id=1, source_target_pairs={{0,8},{8,0},{16,24},{24,16},{32,40},{40,32},{48,56},{56,48},{64,72... | collective-permute-start | bytes 196616 | tf_op jit(solution)/shard_map/ppermute | solution.py:556
  10.9 10.6 %collective-permute-start.3 = (bf16[176,256]{1,0:T(8,128)(2,1)S(1)}, bf16[176,256]{1,0:T(8,128)(2,1)S(1)}, u32[]{:S(2)}, u32[]{:S(2)}) collective-permute-start(bf16[176,256]{1,0:T(8,128)(2,1)S(1)} %shard_map.76.after), channel_id=1, source_target_pairs={{8,16},{16,8},{24,32},{32,24},{40,48},{48,40},{56,64},{64,56},{72,... | collective-permute-start | bytes 270344 | tf_op jit(solution)/shard_map/ppermute | solution.py:574
  22.6 1.5 %collective-permute-start.4 = (bf16[240,256]{1,0:T(8,128)(2,1)S(1)}, bf16[240,256]{1,0:T(8,128)(2,1)S(1)}, u32[]{:S(2)}, u32[]{:S(2)}) collective-permute-start(bf16[240,256]{1,0:T(8,128)(2,1)S(1)} %get-tuple-element.40.after), channel_id=1, source_target_pairs={{0,8},{8,0},{16,24},{24,16},{32,40},{40,32},{48,56},{56,48},{64,72... | collective-permute-start | bytes 368648 | tf_op jit(solution)/shard_map/ppermute | solution.py:626

commit v8 on v7

--- a/solution.py
+++ b/solution.py
@@ -7,7 +7,7 @@
 
 BF = jnp.bfloat16
 F32 = jnp.float32
-J = 48
+J = 40
 VMEM = pl.BlockSpec(memory_space=pltpu.VMEM)
 ANY = pl.BlockSpec(memory_space=pl.ANY)
 
@@ -67,7 +67,7 @@
 
 
 def cell_of(j):
-    return jnp.where(j < 40, j, j - J)
+    return jnp.where(j < 36, j, j - J)
 
 
 def cell_inside(axis, held, cell):
@@ -147,7 +147,7 @@
 
     w_first[...] = jnp.zeros_like(w_first)
     for dx in range(3):
-        rows = [dot(first[dz * 3 + dx], r16) for dz in range(3)]
+        rows = [dot(first[dz * 3 + dx], r16) * 0.5 for dz in range(3)]
         place = halves(16)(iota((16, 256), 1))
         depth = iota((16, 256), 0)
         for dy in range(3):
@@ -159,12 +159,12 @@
                 w_first[even, pl.ds(dy * 64 + (even + dx) * 16, 16), :] = block
 
     flat = down[...].reshape(27 * 16, 32)
-    all_taps = (dot(flat, r32) * (1 / 8)).astype(BF)
+    all_taps = (dot(flat, r32) * (1 / 16)).astype(BF)
     taps = [[all_taps[(dz * 9 + xy) * 16 : (dz * 9 + xy + 1) * 16] for xy in range(9)] for dz in range(3)]
     banded(w_down, taps, 16, list(range(8)), halves(32))
 
     flat = coarse[...].reshape(27 * 32, 64)
-    all_taps = (dot(flat, r64) * (1 / 8)).astype(BF)
+    all_taps = (dot(flat, r64) * (1 / 16)).astype(BF)
     taps = [[all_taps[(dz * 9 + xy) * 32 : (dz * 9 + xy + 1) * 32] for xy in range(9)] for dz in range(3)]
     banded(w_coarse, taps, 32, list(range(4)), natural(64))
 
@@ -177,7 +177,7 @@
 def mid_weights_kernel(middle, after, w_mid_skip, w_mid_up, tiled):
     r32 = repeat_matrix(32)
     for tap in range(27):
-        tiled[tap] = dot_tn(middle[tap], r32)
+        tiled[tap] = dot_tn(middle[tap], r32) * 0.5
     taps = [[tiled[dz * 9 + xy, 64:96, :].astype(BF) for xy in range(9)] for dz in range(3)]
     banded(w_mid_skip, taps, 32, [0, 2, 4, 6, 1, 3, 5, 7], natural(32))
     folded(w_mid_up, lambda dz, dx, dy: tiled[dz * 9 + dx * 3 + dy, 0:64, :], 64, 4, natural(32))
@@ -185,7 +185,7 @@
 
 def fine_weights_kernel(fine, after, w_fine_skip):
     r16 = repeat_matrix(16)
-    tiled = [dot_tn(fine[tap], r16)[32:].astype(BF) for tap in range(27)]
+    tiled = [(dot_tn(fine[tap], r16)[32:] * 0.5).astype(BF) for tap in range(27)]
     taps = [tiled[dz * 9 : dz * 9 + 9] for dz in range(3)]
     banded(w_fine_skip, taps, 16, list(range(0, 16, 2)) + list(range(1, 16, 2)), natural(16))
 
@@ -211,8 +211,8 @@
     out[...] = jnp.where(odd, for_high, for_low)
 
 
-def silu(u):
-    return u * (1.0 / (1.0 + jnp.exp(-u)))
+def silu_half(h):
+    return h + h * jnp.tanh(h)
 
 
 def row_flag(cell):
@@ -238,7 +238,7 @@
         lhs = (dot_nt(pick[...], window) * row_flag(m // 2)).astype(BF)
         sums = [jnp.zeros((J, 128), F32) for _ in range(2)]
         for even in range(2):
-            value = silu(dot(lhs, w_first[even])).reshape(4, J, 256)
+            value = silu_half(dot(lhs, w_first[even])).reshape(4, J, 256)
             for part in range(2):
                 both = value[2 * part] + value[2 * part + 1]
                 sums[part] = sums[part] + both[:, :128] + both[:, 128:]
@@ -273,7 +273,7 @@
         ],
         axis=1,
     )
-    value = silu(dot(lhs, w_down[...])).reshape(2, count, J, 256)
+    value = silu_half(dot(lhs, w_down[...])).reshape(2, count, J, 256)
     mask = y_mask()
     rows = [
         [value[py, at] * (mask * row_flag((first + at) // 2)) for at in range(count)]
@@ -322,7 +322,7 @@
     out[...] = dot(lhs, w_fine_skip[...]).reshape(4, 5, 32, 256)
     r16 = repeat_matrix(16)
     for tap in range(27):
-        tiled[tap] = dot_tn(fine[tap], r16)[:32]
+        tiled[tap] = dot_tn(fine[tap], r16)[:32] * 0.5
     folded(w_fine_up, lambda dz, dx, dy: tiled[dz * 9 + dx * 3 + dy], 32, 8, natural(16))
 
 
@@ -422,7 +422,7 @@
         ],
         axis=1,
     )
-    value = silu(dot(lhs, w_coarse[...])).reshape(4, J, 256)
+    value = silu_half(dot(lhs, w_coarse[...])).reshape(4, J, 256)
     for at in range(4):
         put_three(coarse_s, at, value[at] * (mask * row_flag(at - 1)))
 
@@ -448,7 +448,7 @@
             up = dot(lhs, w_mid_up[px * 2 + py]).reshape(3, J, 256)
             for k in range(3):
                 at = 2 * k if px else 2 * k + 1
-                value = silu(skip[py, at] + up[k])
+                value = silu_half(skip[py, at] + up[k])
                 masked = value * (mask * row_flag((at - 1) // 2))
                 up_s[py + 1, at] = masked[:32].astype(BF)
                 shift = 1 if py else J - 1
@@ -469,7 +469,7 @@
                 group = 2 * half + py
                 for k in range(4):
                     x = 2 * k + px
-                    value = silu(skip_s[group, x] + up[half, k])
+                    value = silu_half(skip_s[group, x] + up[half, k])
                     last_s[x, pl.ds(group * 32, 32), :] = value.astype(BF)
 
     heads = jnp.concatenate([dot_nt(w_head[...], last_s[x]) for x in range(8)], axis=0)

time: 29.3 us -> 29 us (0.990)
  Pallas kernels: 13.6 us -> 12.8 us
  waiting for transfers between devices: 4.51 us -> 4.92 us
    pallas_call x1, Pallas kernels: 1.47 us -> 1.11 us  [body(): pl.pallas_call(encode_near_kernel, out_shape=(shape(6, 7, 32, 256), shape...]
    ppermute x1, waiting for transfers between devices: 2.19 us -> 2.54 us  [body(): chip_edge = lax.ppermute(edge, 'gx', between)]
  transfers between devices with their start and end apart: 5 -> 5, of which waited for: 2 -> 3; matrix products, arithmetic and copies ran while one was open for 0% -> 0% of each run, Pallas kernels for 25% -> 24%
where the time goes in v8:
time: 29 us; the launch traced here: 28.8 us
  Pallas kernels  12.8 us (44%)
  starting transfers between devices  10.9 us (38%)
  waiting for transfers between devices  4.92 us (17%)
    ppermute x1, starting transfers between devices, body(): chip_edge = lax.ppermute(edge, 'gx', between)  5.03 us
    pallas_call x1, Pallas kernels, body(): pl.pallas_call(net_kernel, out_shape=shape(16, 8, 128, kind=F32), in_spec...  4.81 us
    ppermute x1, waiting for transfers between devices, body(): chip_edge = lax.ppermute(edge, 'gx', between)  2.54 us
    ppermute x1, waiting for transfers between devices, body(): y_outer = lax.ppermute(noisy_field, 'gy', swap_out)  2.31 us
    ppermute x1, starting transfers between devices, body(): twin = lax.ppermute(own, 'gx', in_chip)  2.19 us
    ppermute x1, starting transfers between devices, body(): y_outer = lax.ppermute(noisy_field, 'gy', swap_out)  1.92 us
    ppermute x1, starting transfers between devices, body(): y_inner = lax.ppermute(noisy_field, 'gy', swap_in)  1.64 us
    pallas_call x1, Pallas kernels, body(): pl.pallas_call(encoder_weights_kernel, out_shape=(shape(2, 192, 256), sha...  1.49 us
  transfers between devices with their start and end apart: 5, of which 3 were waited for; matrix products, arithmetic and copies ran while one was open for 0% of the time, Pallas kernels for 24%

profile of v8, /device:TPU:79, one launch (start us, length us, event | category | flops | bytes accessed | tf_op | source)
XLA Modules:
  0.0 28.8 jit_solution(8270084857415466906)
XLA Ops:
  0.0 0.0 copy-start
  0.0 1.6 %collective-permute-start = (bf16[16,8,128]{2,1,0:T(8,128)(2,1)}, bf16[16,8,128]{2,1,0:T(8,128)(2,1)S(1)}, u32[]{:S(2)}, u32[]{:S(2)}) collective-permute-start(bf16[16,8,128]{2,1,0:T(8,128)(2,1)} %own.1), channel_id=1, source_target_pairs={{0,1},{1,0},{2,3},{3,2},{4,5},{5,4},{6,7},{7,6},{8,9},{9,8},{10,11... | collective-permute-start | bytes 98312 | tf_op jit(solution)/shard_map/ppermute | solution.py:544
  1.6 1.9 %collective-permute-start.1 = (bf16[16,8,128]{2,1,0:T(8,128)(2,1)}, bf16[16,8,128]{2,1,0:T(8,128)(2,1)S(1)}, u32[]{:S(2)}, u32[]{:S(2)}) collective-permute-start(bf16[16,8,128]{2,1,0:T(8,128)(2,1)} %own.1), channel_id=1, source_target_pairs={{1,2},{2,1},{3,4},{4,3},{5,6},{6,5},{9,10},{10,9},{11,12},{12,11},... | collective-permute-start | bytes 98312 | tf_op jit(solution)/shard_map/ppermute | solution.py:545
  3.6 1.5 %shard_map.73 = (bf16[2,192,256]{2,1,0:T(8,128)(2,1)S(1)}, bf16[1152,256]{1,0:T(8,128)(2,1)S(1)}, bf16[1152,256]{1,0:T(8,128)(2,1)S(1)}, bf16[16,256]{1,0:T(8,12...) custom-call(bf16[9,3,16]{2,1,0:T(4,128)(2,1)} %bitcast.20, ...), custom_call_target="tpu_custom_call" | custom-call | flops 1000000000 | bytes 3000000 | tf_op jit(solution)/shard_map/pallas_call | solution.py:502
  5.1 0.0 collective-permute-done.inner
  5.1 2.3 %collective-permute-done.1.outer = bf16[16,8,128]{2,1,0:T(8,128)(2,1)S(1)} collective-permute-done((bf16[16,8,128]{2,1,0:T(8,128)(2,1)}, bf16[16,8,128]{2,1,0:T(8,128)(2,1)S(1)}, u32[]{:S(2)}, u32[]{:S(2)}) %collective-permute-start.1) | collective-permute-done | bytes 32800 | tf_op jit(solution)/shard_map/ppermute | solution.py:545
  7.4 0.0 copy-done
  7.4 0.2 shard_map.74.after.own
  7.6 2.2 %collective-permute-start.2 = (bf16[128,256]{1,0:T(8,128)(2,1)S(1)}, bf16[128,256]{1,0:T(8,128)(2,1)S(1)}, u32[]{:S(2)}, u32[]{:S(2)}) collective-permute-start(bf16[128,256]{1,0:T(8,128)(2,1)S(1)} %shard_map.74.after.own), channel_id=1, source_target_pairs={{0,8},{8,0},{16,24},{24,16},{32,40},{40,32},{48,56},{56,48},{64,72... | collective-permute-start | bytes 196616 | tf_op jit(solution)/shard_map/ppermute | solution.py:556
  9.8 1.3 %shard_map.75 = (bf16[2304,256]{1,0:T(8,128)(2,1)S(1)}, bf16[4,1024,256]{2,1,0:T(8,128)(2,1)S(1)}) custom-call(bf16[27,32,96]{2,1,0:T(8,128)(2,1)S(1)} %get-tuple-element.29.middle, bf16[128,256]{1,0:T(8,128)(2,1)S(1)} %shard_map.74.after.own), custom_call_target="tpu_custom_call" | custom-call | flops 1000000000 | bytes 4000000 | tf_op jit(solution)/shard_map/pallas_call | solution.py:557
  11.0 0.0 collective-permute-done.2.twin
  11.1 5.0 %collective-permute-start.3 = (bf16[176,256]{1,0:T(8,128)(2,1)S(1)}, bf16[176,256]{1,0:T(8,128)(2,1)S(1)}, u32[]{:S(2)}, u32[]{:S(2)}) collective-permute-start(bf16[176,256]{1,0:T(8,128)(2,1)S(1)} %shard_map.76.after), channel_id=1, source_target_pairs={{8,16},{16,8},{24,32},{32,24},{40,48},{48,40},{56,64},{64,56},{72,... | collective-permute-start | bytes 270344 | tf_op jit(solution)/shard_map/ppermute | solution.py:574
  16.1 0.4 %shard_map.78.w_fine_skip = bf16[2304,256]{1,0:T(8,128)(2,1)S(1)} custom-call(bf16[27,16,48]{2,1,0:T(8,128)(2,1)S(1)} %get-tuple-element.38.fine, bf16[176,256]{1,0:T(8,128)(2,1)S(1)} %shard_map.76.after), custom_call_target="tpu_custom_call" | custom-call | flops 1000000000 | bytes 2000000 | tf_op jit(solution)/shard_map/pallas_call | solution.py:590
  16.5 1.1 %shard_map.77 = (bf16[6,7,32,256]{3,2,1,0:T(8,128)(2,1)S(1)}, bf16[4,4,40,128]{3,2,1,0:T(8,128)(2,1)S(1)}, bf16[4,2,40,256]{3,2,1,0:T(8,128)(2,1)S(1)}, bf16[40,128]{1,0:T(8,128)(2,1)S(1)}, bf16[160,256]{1,0:T(8,128)(2,1)S(1)}) custom-call(bf16[128,256]{1,0:T(8,128)(2,1)S(1)} %shard_map.74.after.own, bf16[128,256]{1,0:T(8,128)(2,1)S(1)} %collective-permute-done.2.twin, ...), custom_call_target="tpu_custom_call" | custom-call | flops 1000000000 | bytes 3000000 | tf_op jit(solution)/shard_map/pallas_call | solution.py:576
  17.7 1.4 %shard_map.79 = (f32[4,5,32,256]{3,2,1,0:T(8,128)S(1)}, bf16[4,1024,256]{2,1,0:T(8,128)(2,1)S(1)}) custom-call(bf16[6,7,32,256]{3,2,1,0:T(8,128)(2,1)S(1)} %get-tuple-element.37.fine_near, bf16[27,16,48]{2,1,0:T(8,128)(2,1)S(1)} %get-tuple-element.38.fine, bf16[2304,256]{1,0:T(8,128)(2,1)S(1)} %shard_map.78.w_fine_skip), custom_call_target="tpu_custom_call" | custom-call | flops 1000000000 | bytes 4000000 | tf_op jit(solution)/shard_map/pallas_call | solution.py:598
  19.1 2.5 %collective-permute-done.3.edge = bf16[176,256]{1,0:T(8,128)(2,1)S(1)} collective-permute-done((bf16[176,256]{1,0:T(8,128)(2,1)S(1)}, bf16[176,256]{1,0:T(8,128)(2,1)S(1)}, u32[]{:S(2)}, u32[]{:S(2)}) %collective-permute-start.3) | collective-permute-done | bytes 90144 | tf_op jit(solution)/shard_map/ppermute | solution.py:574
  21.6 0.9 %shard_map.80 = (bf16[6,3,32,256]{3,2,1,0:T(8,128)(2,1)S(1)}, bf16[4,2,40,128]{3,2,1,0:T(8,128)(2,1)S(1)}, bf16[4,2,40,256]{3,2,1,0:T(8,128)(2,1)S(1)}, bf16[3,2...) custom-call(bf16[128,256]{1,0:T(8,128)(2,1)S(1)} %shard_map.74.after.own, ...), custom_call_target="tpu_custom_call" | custom-call | flops 1000000000 | bytes 3000000 | tf_op jit(solution)/shard_map/pallas_call | solution.py:608
  22.6 0.1 collective-permute-start.4
  22.7 1.2 %shard_map.81 = (bf16[4,2,40,256]{3,2,1,0:T(8,128)(2,1)S(1)}, bf16[3,2,40,128]{3,2,1,0:T(8,128)(2,1)S(1)}) custom-call(bf16[176,256]{1,0:T(8,128)(2,1)S(1)} %collective-permute-done.3.edge, bf16[160,256]{1,0:T(8,128)(2,1)S(1)} %get-tuple-element.31.pick, bf16[2,192,256]{2,1,0:T(8,128)(2,1)S(1)} %get-tuple-element.32.w_first, ...), custom_call_target="tpu_custom_call" | custom-call | flops 2000000000 | bytes 3000000 | tf_op jit(solution)/shard_map/pallas_call | solution.py:627
  23.9 0.1 collective-permute-done.4.from_twin
  23.9 4.8 %shard_map.82 = f32[16,8,128]{2,1,0:T(8,128)} custom-call(bf16[200,256]{1,0:T(8,128)(2,1)S(1)} %collective-permute-done.4.from_twin, bf16[6,7,32,256]{3,2,1,0:T(8,128)(2,1)S(1)} %get-tuple-element.37.fine_near, bf16[6,3,32,256]{3,2,1,0:T(8,128)(2,1)S(1)} %get-tuple-element.41.fine_far, f32[4,5,32,256]{3,2,1,0:T(8,128)S(1)} %get-tuple-element.39.after.skip_near, ...), custom_call_target="tpu_custom_call" | custom-call | flops 6000000000 | bytes 9000000 | tf_op jit(solution)/shard_map/pallas_call | solution.py:637
  (1 shorter events, 0.0 us)
Async XLA Ops:
  0.0 7.4 %copy-start = (bf16[16,8,128]{2,1,0:T(8,128)(2,1)S(1)}, bf16[16,8,128]{2,1,0:T(8,128)(2,1)}, u32[]{:S(2)}) copy-start(bf16[16,8,128]{2,1,0:T(8,128)(2,1)} %own.1) | copy-start | bytes 98308
  0.0 5.1 %collective-permute-start = (bf16[16,8,128]{2,1,0:T(8,128)(2,1)}, bf16[16,8,128]{2,1,0:T(8,128)(2,1)S(1)}, u32[]{:S(2)}, u32[]{:S(2)}) collective-permute-start(bf16[16,8,128]{2,1,0:T(8,128)(2,1)} %own.1), channel_id=1, source_target_pairs={{0,1},{1,0},{2,3},{3,2},{4,5},{5,4},{6,7},{7,6},{8,9},{9,8},{10,11... | collective-permute-start | bytes 98312 | tf_op jit(solution)/shard_map/ppermute | solution.py:544
  1.6 5.8 %collective-permute-start.1 = (bf16[16,8,128]{2,1,0:T(8,128)(2,1)}, bf16[16,8,128]{2,1,0:T(8,128)(2,1)S(1)}, u32[]{:S(2)}, u32[]{:S(2)}) collective-permute-start(bf16[16,8,128]{2,1,0:T(8,128)(2,1)} %own.1), channel_id=1, source_target_pairs={{1,2},{2,1},{3,4},{4,3},{5,6},{6,5},{9,10},{10,9},{11,12},{12,11},... | collective-permute-start | bytes 98312 | tf_op jit(solution)/shard_map/ppermute | solution.py:545
  7.6 3.5 %collective-permute-start.2 = (bf16[128,256]{1,0:T(8,128)(2,1)S(1)}, bf16[128,256]{1,0:T(8,128)(2,1)S(1)}, u32[]{:S(2)}, u32[]{:S(2)}) collective-permute-start(bf16[128,256]{1,0:T(8,128)(2,1)S(1)} %shard_map.74.after.own), channel_id=1, source_target_pairs={{0,8},{8,0},{16,24},{24,16},{32,40},{40,32},{48,56},{56,48},{64,72... | collective-permute-start | bytes 196616 | tf_op jit(solution)/shard_map/ppermute | solution.py:556
  11.1 10.6 %collective-permute-start.3 = (bf16[176,256]{1,0:T(8,128)(2,1)S(1)}, bf16[176,256]{1,0:T(8,128)(2,1)S(1)}, u32[]{:S(2)}, u32[]{:S(2)}) collective-permute-start(bf16[176,256]{1,0:T(8,128)(2,1)S(1)} %shard_map.76.after), channel_id=1, source_target_pairs={{8,16},{16,8},{24,32},{32,24},{40,48},{48,40},{56,64},{64,56},{72,... | collective-permute-start | bytes 270344 | tf_op jit(solution)/shard_map/ppermute | solution.py:574
  22.6 1.4 %collective-permute-start.4 = (bf16[200,256]{1,0:T(8,128)(2,1)S(1)}, bf16[200,256]{1,0:T(8,128)(2,1)S(1)}, u32[]{:S(2)}, u32[]{:S(2)}) collective-permute-start(bf16[200,256]{1,0:T(8,128)(2,1)S(1)} %get-tuple-element.40.after), channel_id=1, source_target_pairs={{0,8},{8,0},{16,24},{24,16},{32,40},{40,32},{48,56},{56,48},{64,72... | collective-permute-start | bytes 307208 | tf_op jit(solution)/shard_map/ppermute | solution.py:626

commit v9 on v8

--- a/solution.py
+++ b/solution.py
@@ -81,11 +81,14 @@
 def banded(out, taps, channels, row_depths, depth_of):
     size = channels * len(row_depths)
     places = depth_of(iota((channels, 256), 1))
-    for lanes, held in tiles(depth_of):
-        for at, depth in enumerate(row_depths):
-            for xy in range(9):
-                terms = [((depth + 1 - dz,), taps[dz][xy]) for dz in range(3)]
-                row = xy * size + at * channels
+
+    @pl.loop(0, 9)
+    def _(xy):
+        values = [taps(dz * 9 + xy) for dz in range(3)]
+        for lanes, held in tiles(depth_of):
+            for at, depth in enumerate(row_depths):
+                terms = [((depth + 1 - dz,), values[dz]) for dz in range(3)]
+                row = pl.multiple_of(xy * size + at * channels, 16)
                 place_block(out, (), row, channels, terms, places, held, lanes)
 
 
@@ -120,7 +123,7 @@
 def encoder_weights_kernel(
     raw_first, raw_down, raw_coarse, raw_middle, raw_fine, raw_head,
     w_first, w_down, w_coarse, w_head, middle, fine, pick,
-    first, down, coarse, head, sems,
+    first, down, coarse, head, tiled, sems,
 ):
     copies = [
         pltpu.make_async_copy(source, target, sems.at[at])
@@ -159,14 +162,12 @@
                 w_first[even, pl.ds(dy * 64 + (even + dx) * 16, 16), :] = block
 
     flat = down[...].reshape(27 * 16, 32)
-    all_taps = (dot(flat, r32) * (1 / 16)).astype(BF)
-    taps = [[all_taps[(dz * 9 + xy) * 16 : (dz * 9 + xy + 1) * 16] for xy in range(9)] for dz in range(3)]
-    banded(w_down, taps, 16, list(range(8)), halves(32))
+    tiled[pl.ds(0, 27 * 16), :] = (dot(flat, r32) * (1 / 16)).astype(BF)
+    banded(w_down, lambda tap: tiled[pl.ds(pl.multiple_of(tap * 16, 16), 16), :], 16, list(range(8)), halves(32))
 
     flat = coarse[...].reshape(27 * 32, 64)
-    all_taps = (dot(flat, r64) * (1 / 16)).astype(BF)
-    taps = [[all_taps[(dz * 9 + xy) * 32 : (dz * 9 + xy + 1) * 32] for xy in range(9)] for dz in range(3)]
-    banded(w_coarse, taps, 32, list(range(4)), natural(64))
+    tiled[...] = (dot(flat, r64) * (1 / 16)).astype(BF)
+    banded(w_coarse, lambda tap: tiled[pl.ds(pl.multiple_of(tap * 32, 32), 32), :], 32, list(range(4)), natural(64))
 
     row = dot(jnp.broadcast_to(head[...], (16, 16)), r16)
     w_head[...] = jnp.where(iota((16, 256), 1) // 16 == iota((16, 256), 0), row, 0.0).astype(BF)
@@ -176,18 +177,19 @@
 
 def mid_weights_kernel(middle, after, w_mid_skip, w_mid_up, tiled):
     r32 = repeat_matrix(32)
-    for tap in range(27):
-        tiled[tap] = dot_tn(middle[tap], r32) * 0.5
-    taps = [[tiled[dz * 9 + xy, 64:96, :].astype(BF) for xy in range(9)] for dz in range(3)]
-    banded(w_mid_skip, taps, 32, [0, 2, 4, 6, 1, 3, 5, 7], natural(32))
+
+    @pl.loop(0, 9)
+    def _(xy):
+        for dz in range(3):
+            tiled[dz * 9 + xy] = dot_tn(middle[dz * 9 + xy], r32) * 0.5
+
+    banded(w_mid_skip, lambda tap: tiled[tap, 64:96, :].astype(BF), 32, [0, 2, 4, 6, 1, 3, 5, 7], natural(32))
     folded(w_mid_up, lambda dz, dx, dy: tiled[dz * 9 + dx * 3 + dy, 0:64, :], 64, 4, natural(32))
 
 
 def fine_weights_kernel(fine, after, w_fine_skip):
     r16 = repeat_matrix(16)
-    tiled = [(dot_tn(fine[tap], r16)[32:] * 0.5).astype(BF) for tap in range(27)]
-    taps = [tiled[dz * 9 : dz * 9 + 9] for dz in range(3)]
-    banded(w_fine_skip, taps, 16, list(range(0, 16, 2)) + list(range(1, 16, 2)), natural(16))
+    banded(w_fine_skip, lambda tap: (dot_tn(fine[tap], r16)[32:] * 0.5).astype(BF), 16, list(range(0, 16, 2)) + list(range(1, 16, 2)), natural(16))
 
 
 def join_kernel(own, inner, outer, after, out):
@@ -311,15 +313,18 @@
 
 
 def skip_near_kernel(fine_near, fine, w_fine_skip, out, w_fine_up, tiled):
-    lhs = jnp.concatenate(
-        [
-            fine_near[dy : dy + 4, dx : dx + 5].reshape(640, 256)
-            for dx in range(3)
-            for dy in range(3)
-        ],
-        axis=1,
-    )
-    out[...] = dot(lhs, w_fine_skip[...]).reshape(4, 5, 32, 256)
+    @pl.loop(0, 4)
+    def _(group):
+        lhs = jnp.concatenate(
+            [
+                fine_near[group + dy, dx : dx + 5].reshape(160, 256)
+                for dx in range(3)
+                for dy in range(3)
+            ],
+            axis=1,
+        )
+        out[group] = dot(lhs, w_fine_skip[...]).reshape(5, 32, 256)
+
     r16 = repeat_matrix(16)
     for tap in range(27):
         tiled[tap] = dot_tn(fine[tap], r16)[:32] * 0.5
@@ -454,23 +459,24 @@
                 shift = 1 if py else J - 1
                 up_s[0 if py else 3, at] = pltpu.roll(masked, shift, 0)[:32].astype(BF)
 
-    for py in range(2):
-        for px in range(2):
-            lhs = jnp.concatenate(
-                [
-                    up_s[py + ty : py + ty + 2, px + tx : px + tx + 4].reshape(256, 256)
-                    for tx in range(2)
-                    for ty in range(2)
-                ],
-                axis=1,
-            )
-            up = dot(lhs, w_fine_up[px * 2 + py]).reshape(2, 4, 32, 256)
-            for half in range(2):
-                group = 2 * half + py
-                for k in range(4):
-                    x = 2 * k + px
-                    value = silu_half(skip_s[group, x] + up[half, k])
-                    last_s[x, pl.ds(group * 32, 32), :] = value.astype(BF)
+    @pl.loop(0, 4)
+    def _(parity):
+        px, py = parity // 2, parity % 2
+        lhs = jnp.concatenate(
+            [
+                up_s[pl.ds(py + ty, 2), pl.ds(px + tx, 4)].reshape(256, 256)
+                for tx in range(2)
+                for ty in range(2)
+            ],
+            axis=1,
+        )
+        up = dot(lhs, w_fine_up[parity]).reshape(2, 4, 32, 256)
+        for half in range(2):
+            group = 2 * half + py
+            for k in range(4):
+                value = silu_half(skip_s[group, 2 * k + px] + up[half, k])
+                row = pl.multiple_of(group * 32, 32)
+                last_s[2 * k + px, pl.ds(row, 32), :] = value.astype(BF)
 
     heads = jnp.concatenate([dot_nt(w_head[...], last_s[x]) for x in range(8)], axis=0)
     high = heads.astype(BF)
@@ -517,6 +523,7 @@
             pltpu.VMEM((27, 16, 32), BF),
             pltpu.VMEM((27, 32, 64), BF),
             pltpu.VMEM((1, 16), BF),
+            pltpu.VMEM((27 * 32, 256), BF),
             pltpu.SemaphoreType.DMA((6,)),
         ],
         compiler_params=small(16),

time: 29 us -> 30 us (1.034)
  Pallas kernels: 12.8 us -> 16.8 us
  waiting for transfers between devices: 4.92 us -> 2.01 us
    ppermute x1, waiting for transfers between devices: 2.54 us -> 0.18 us  [body(): chip_edge = lax.ppermute(edge, 'gx', between)]
    pallas_call x1, Pallas kernels: 1.25 us -> 2.94 us  [body(): pl.pallas_call(mid_weights_kernel, out_shape=(shape(2304, 256), shape(4,...]
    pallas_call x1, Pallas kernels: 0.44 us -> 2 us  [body(): pl.pallas_call(fine_weights_kernel, out_shape=shape(2304, 256), in_specs=...]
    pallas_call x1, Pallas kernels: 1.44 us -> 2.24 us  [body(): pl.pallas_call(skip_near_kernel, out_shape=(shape(4, 5, 32, 256, kind=F32...]
    pallas_call x1, Pallas kernels: 4.81 us -> 4.16 us  [body(): pl.pallas_call(net_kernel, out_shape=shape(16, 8, 128, kind=F32), in_spec...]
    pallas_call x1, Pallas kernels: 1.49 us -> 2.05 us  [body(): pl.pallas_call(encoder_weights_kernel, out_shape=(shape(2, 192, 256), sha...]
    ppermute x1, waiting for transfers between devices: 2.31 us -> 1.76 us  [body(): y_outer = lax.ppermute(noisy_field, 'gy', swap_out)]
  transfers between devices with their start and end apart: 5 -> 5, of which waited for: 3 -> 3; matrix products, arithmetic and copies ran while one was open for 0% -> 0% of each run, Pallas kernels for 24% -> 39%
where the time goes in v9:
time: 30 us; the launch traced here: 29.8 us
  Pallas kernels  16.8 us (56%)
  starting transfers between devices  10.9 us (36%)
  waiting for transfers between devices  2.01 us (7%)
    ppermute x1, starting transfers between devices, body(): chip_edge = lax.ppermute(edge, 'gx', between)  5.03 us
    pallas_call x1, Pallas kernels, body(): pl.pallas_call(net_kernel, out_shape=shape(16, 8, 128, kind=F32), in_spec...  4.16 us
    pallas_call x1, Pallas kernels, body(): pl.pallas_call(mid_weights_kernel, out_shape=(shape(2304, 256), shape(4,...  2.94 us
    pallas_call x1, Pallas kernels, body(): pl.pallas_call(skip_near_kernel, out_shape=(shape(4, 5, 32, 256, kind=F32...  2.24 us
    ppermute x1, starting transfers between devices, body(): twin = lax.ppermute(own, 'gx', in_chip)  2.19 us
    pallas_call x1, Pallas kernels, body(): pl.pallas_call(encoder_weights_kernel, out_shape=(shape(2, 192, 256), sha...  2.05 us
    pallas_call x1, Pallas kernels, body(): pl.pallas_call(fine_weights_kernel, out_shape=shape(2304, 256), in_specs=...  2 us
    ppermute x1, starting transfers between devices, body(): y_outer = lax.ppermute(noisy_field, 'gy', swap_out)  1.92 us
  transfers between devices with their start and end apart: 5, of which 3 were waited for; matrix products, arithmetic and copies ran while one was open for 0% of the time, Pallas kernels for 39%

profile of v9, /device:TPU:79, one launch (start us, length us, event | category | flops | bytes accessed | tf_op | source)
XLA Modules:
  0.0 29.8 jit_solution(9684638928014516041)
XLA Ops:
  0.0 0.0 copy-start
  0.0 1.6 %collective-permute-start = (bf16[16,8,128]{2,1,0:T(8,128)(2,1)}, bf16[16,8,128]{2,1,0:T(8,128)(2,1)S(1)}, u32[]{:S(2)}, u32[]{:S(2)}) collective-permute-start(bf16[16,8,128]{2,1,0:T(8,128)(2,1)} %own.1), channel_id=1, source_target_pairs={{0,1},{1,0},{2,3},{3,2},{4,5},{5,4},{6,7},{7,6},{8,9},{9,8},{10,11... | collective-permute-start | bytes 98312 | tf_op jit(solution)/shard_map/ppermute | solution.py:551
  1.6 1.9 %collective-permute-start.1 = (bf16[16,8,128]{2,1,0:T(8,128)(2,1)}, bf16[16,8,128]{2,1,0:T(8,128)(2,1)S(1)}, u32[]{:S(2)}, u32[]{:S(2)}) collective-permute-start(bf16[16,8,128]{2,1,0:T(8,128)(2,1)} %own.1), channel_id=1, source_target_pairs={{1,2},{2,1},{3,4},{4,3},{5,6},{6,5},{9,10},{10,9},{11,12},{12,11},... | collective-permute-start | bytes 98312 | tf_op jit(solution)/shard_map/ppermute | solution.py:552
  3.6 2.0 %shard_map.73 = (bf16[2,192,256]{2,1,0:T(8,128)(2,1)S(1)}, bf16[1152,256]{1,0:T(8,128)(2,1)S(1)}, bf16[1152,256]{1,0:T(8,128)(2,1)S(1)}, bf16[16,256]{1,0:T(8,12...) custom-call(bf16[9,3,16]{2,1,0:T(4,128)(2,1)} %bitcast.20, ...), custom_call_target="tpu_custom_call" | custom-call | flops 1000000000 | bytes 3000000 | tf_op jit(solution)/shard_map/pallas_call | solution.py:508
  5.6 0.0 collective-permute-done.inner
  5.6 1.8 %collective-permute-done.1.outer = bf16[16,8,128]{2,1,0:T(8,128)(2,1)S(1)} collective-permute-done((bf16[16,8,128]{2,1,0:T(8,128)(2,1)}, bf16[16,8,128]{2,1,0:T(8,128)(2,1)S(1)}, u32[]{:S(2)}, u32[]{:S(2)}) %collective-permute-start.1) | collective-permute-done | bytes 32800 | tf_op jit(solution)/shard_map/ppermute | solution.py:552
  7.4 0.0 copy-done
  7.4 0.2 shard_map.74.after.own
  7.6 2.2 %collective-permute-start.2 = (bf16[128,256]{1,0:T(8,128)(2,1)S(1)}, bf16[128,256]{1,0:T(8,128)(2,1)S(1)}, u32[]{:S(2)}, u32[]{:S(2)}) collective-permute-start(bf16[128,256]{1,0:T(8,128)(2,1)S(1)} %shard_map.74.after.own), channel_id=1, source_target_pairs={{0,8},{8,0},{16,24},{24,16},{32,40},{40,32},{48,56},{56,48},{64,72... | collective-permute-start | bytes 196616 | tf_op jit(solution)/shard_map/ppermute | solution.py:563
  9.8 2.9 %shard_map.75 = (bf16[2304,256]{1,0:T(8,128)(2,1)S(1)}, bf16[4,1024,256]{2,1,0:T(8,128)(2,1)S(1)}) custom-call(bf16[27,32,96]{2,1,0:T(8,128)(2,1)S(1)} %get-tuple-element.29.middle, bf16[128,256]{1,0:T(8,128)(2,1)S(1)} %shard_map.74.after.own), custom_call_target="tpu_custom_call" | custom-call | flops 1000000000 | bytes 4000000 | tf_op jit(solution)/shard_map/pallas_call | solution.py:564
  12.7 0.0 collective-permute-done.2.twin
  12.7 5.0 %collective-permute-start.3 = (bf16[176,256]{1,0:T(8,128)(2,1)S(1)}, bf16[176,256]{1,0:T(8,128)(2,1)S(1)}, u32[]{:S(2)}, u32[]{:S(2)}) collective-permute-start(bf16[176,256]{1,0:T(8,128)(2,1)S(1)} %shard_map.76.after), channel_id=1, source_target_pairs={{8,16},{16,8},{24,32},{32,24},{40,48},{48,40},{56,64},{64,56},{72,... | collective-permute-start | bytes 270344 | tf_op jit(solution)/shard_map/ppermute | solution.py:581
  17.8 2.0 %shard_map.78.w_fine_skip = bf16[2304,256]{1,0:T(8,128)(2,1)S(1)} custom-call(bf16[27,16,48]{2,1,0:T(8,128)(2,1)S(1)} %get-tuple-element.38.fine, bf16[176,256]{1,0:T(8,128)(2,1)S(1)} %shard_map.76.after), custom_call_target="tpu_custom_call" | custom-call | flops 1000000000 | bytes 2000000 | tf_op jit(solution)/shard_map/pallas_call | solution.py:597
  19.8 1.1 %shard_map.77 = (bf16[6,7,32,256]{3,2,1,0:T(8,128)(2,1)S(1)}, bf16[4,4,40,128]{3,2,1,0:T(8,128)(2,1)S(1)}, bf16[4,2,40,256]{3,2,1,0:T(8,128)(2,1)S(1)}, bf16[40,128]{1,0:T(8,128)(2,1)S(1)}, bf16[160,256]{1,0:T(8,128)(2,1)S(1)}) custom-call(bf16[128,256]{1,0:T(8,128)(2,1)S(1)} %shard_map.74.after.own, bf16[128,256]{1,0:T(8,128)(2,1)S(1)} %collective-permute-done.2.twin, ...), custom_call_target="tpu_custom_call" | custom-call | flops 1000000000 | bytes 3000000 | tf_op jit(solution)/shard_map/pallas_call | solution.py:583
  20.9 2.2 %shard_map.79 = (f32[4,5,32,256]{3,2,1,0:T(8,128)S(1)}, bf16[4,1024,256]{2,1,0:T(8,128)(2,1)S(1)}) custom-call(bf16[6,7,32,256]{3,2,1,0:T(8,128)(2,1)S(1)} %get-tuple-element.37.fine_near, bf16[27,16,48]{2,1,0:T(8,128)(2,1)S(1)} %get-tuple-element.38.fine, bf16[2304,256]{1,0:T(8,128)(2,1)S(1)} %shard_map.78.w_fine_skip), custom_call_target="tpu_custom_call" | custom-call | flops 1000000000 | bytes 4000000 | tf_op jit(solution)/shard_map/pallas_call | solution.py:605
  23.1 0.2 collective-permute-done.3.edge
  23.3 0.9 %shard_map.80 = (bf16[6,3,32,256]{3,2,1,0:T(8,128)(2,1)S(1)}, bf16[4,2,40,128]{3,2,1,0:T(8,128)(2,1)S(1)}, bf16[4,2,40,256]{3,2,1,0:T(8,128)(2,1)S(1)}, bf16[3,2...) custom-call(bf16[128,256]{1,0:T(8,128)(2,1)S(1)} %shard_map.74.after.own, ...), custom_call_target="tpu_custom_call" | custom-call | flops 1000000000 | bytes 3000000 | tf_op jit(solution)/shard_map/pallas_call | solution.py:615
  24.2 0.1 collective-permute-start.4
  24.3 1.2 %shard_map.81 = (bf16[4,2,40,256]{3,2,1,0:T(8,128)(2,1)S(1)}, bf16[3,2,40,128]{3,2,1,0:T(8,128)(2,1)S(1)}) custom-call(bf16[176,256]{1,0:T(8,128)(2,1)S(1)} %collective-permute-done.3.edge, bf16[160,256]{1,0:T(8,128)(2,1)S(1)} %get-tuple-element.31.pick, bf16[2,192,256]{2,1,0:T(8,128)(2,1)S(1)} %get-tuple-element.32.w_first, ...), custom_call_target="tpu_custom_call" | custom-call | flops 2000000000 | bytes 3000000 | tf_op jit(solution)/shard_map/pallas_call | solution.py:634
  25.6 0.1 collective-permute-done.4.from_twin
  25.6 4.2 %shard_map.82 = f32[16,8,128]{2,1,0:T(8,128)} custom-call(bf16[200,256]{1,0:T(8,128)(2,1)S(1)} %collective-permute-done.4.from_twin, bf16[6,7,32,256]{3,2,1,0:T(8,128)(2,1)S(1)} %get-tuple-element.37.fine_near, bf16[6,3,32,256]{3,2,1,0:T(8,128)(2,1)S(1)} %get-tuple-element.41.fine_far, f32[4,5,32,256]{3,2,1,0:T(8,128)S(1)} %get-tuple-element.39.after.skip_near, ...), custom_call_target="tpu_custom_call" | custom-call | flops 6000000000 | bytes 9000000 | tf_op jit(solution)/shard_map/pallas_call | solution.py:644
  (1 shorter events, 0.0 us)
Async XLA Ops:
  0.0 7.4 %copy-start = (bf16[16,8,128]{2,1,0:T(8,128)(2,1)S(1)}, bf16[16,8,128]{2,1,0:T(8,128)(2,1)}, u32[]{:S(2)}) copy-start(bf16[16,8,128]{2,1,0:T(8,128)(2,1)} %own.1) | copy-start | bytes 98308
  0.0 5.6 %collective-permute-start = (bf16[16,8,128]{2,1,0:T(8,128)(2,1)}, bf16[16,8,128]{2,1,0:T(8,128)(2,1)S(1)}, u32[]{:S(2)}, u32[]{:S(2)}) collective-permute-start(bf16[16,8,128]{2,1,0:T(8,128)(2,1)} %own.1), channel_id=1, source_target_pairs={{0,1},{1,0},{2,3},{3,2},{4,5},{5,4},{6,7},{7,6},{8,9},{9,8},{10,11... | collective-permute-start | bytes 98312 | tf_op jit(solution)/shard_map/ppermute | solution.py:551
  1.6 5.8 %collective-permute-start.1 = (bf16[16,8,128]{2,1,0:T(8,128)(2,1)}, bf16[16,8,128]{2,1,0:T(8,128)(2,1)S(1)}, u32[]{:S(2)}, u32[]{:S(2)}) collective-permute-start(bf16[16,8,128]{2,1,0:T(8,128)(2,1)} %own.1), channel_id=1, source_target_pairs={{1,2},{2,1},{3,4},{4,3},{5,6},{6,5},{9,10},{10,9},{11,12},{12,11},... | collective-permute-start | bytes 98312 | tf_op jit(solution)/shard_map/ppermute | solution.py:552
  7.6 5.1 %collective-permute-start.2 = (bf16[128,256]{1,0:T(8,128)(2,1)S(1)}, bf16[128,256]{1,0:T(8,128)(2,1)S(1)}, u32[]{:S(2)}, u32[]{:S(2)}) collective-permute-start(bf16[128,256]{1,0:T(8,128)(2,1)S(1)} %shard_map.74.after.own), channel_id=1, source_target_pairs={{0,8},{8,0},{16,24},{24,16},{32,40},{40,32},{48,56},{56,48},{64,72... | collective-permute-start | bytes 196616 | tf_op jit(solution)/shard_map/ppermute | solution.py:563
  12.7 10.6 %collective-permute-start.3 = (bf16[176,256]{1,0:T(8,128)(2,1)S(1)}, bf16[176,256]{1,0:T(8,128)(2,1)S(1)}, u32[]{:S(2)}, u32[]{:S(2)}) collective-permute-start(bf16[176,256]{1,0:T(8,128)(2,1)S(1)} %shard_map.76.after), channel_id=1, source_target_pairs={{8,16},{16,8},{24,32},{32,24},{40,48},{48,40},{56,64},{64,56},{72,... | collective-permute-start | bytes 270344 | tf_op jit(solution)/shard_map/ppermute | solution.py:581
  24.2 1.4 %collective-permute-start.4 = (bf16[200,256]{1,0:T(8,128)(2,1)S(1)}, bf16[200,256]{1,0:T(8,128)(2,1)S(1)}, u32[]{:S(2)}, u32[]{:S(2)}) collective-permute-start(bf16[200,256]{1,0:T(8,128)(2,1)S(1)} %get-tuple-element.40.after), channel_id=1, source_target_pairs={{0,8},{8,0},{16,24},{24,16},{32,40},{40,32},{48,56},{56,48},{64,72... | collective-permute-start | bytes 307208 | tf_op jit(solution)/shard_map/ppermute | solution.py:633

commit v10 on v8

--- a/solution.py
+++ b/solution.py
@@ -326,20 +326,19 @@
     folded(w_fine_up, lambda dz, dx, dy: tiled[dz * 9 + dx * 3 + dy], 32, 8, natural(16))
 
 
-def encode_inner_kernel(
+def encode_far_kernel(
     own, edge, pick, w_first, w_down, pool_near, pool_mid_near, for_twin_near, after,
     fine, pool_far, mid, pool_mid, for_twin, pool_s,
 ):
     def work(core):
+        parts = [own[80:], edge[...]] if core else [edge[...], own[:48]]
+        field = jnp.concatenate(parts, axis=0)
+        pairs = range(3, 9) if core else range(-5, 1)
+        encode(field, pick, w_first, pairs, fine, 6 if core else -1, pool_far, 0)
         if core:
-            field = jnp.concatenate([own[80:], edge[:48]], axis=0)
-            pool_s[:, 0:2] = pool_near[:, 2:4]
+            pool_s[:, 0:2], pool_s[:, 2:4] = pool_near[:, 2:4], pool_far[:, 0:2]
         else:
-            field = jnp.concatenate([edge[128:], own[:48]], axis=0)
-            pool_s[:, 2:4] = pool_near[:, 0:2]
-        pairs, far = ((3, 4), 2) if core else ((-1, 0), 0)
-        encode(field, pick, w_first, pairs, fine, 6 if core else -1, pool_s, far)
-        pool_far[...] = pool_s[:, far : far + 2]
+            pool_s[:, 0:2], pool_s[:, 2:4] = pool_far[:, 4:6], pool_near[:, 0:2]
         rows, pooled = middle_rows(pool_s, w_down, 2 if core else 0, 2)
         for at in range(2):
             for py in range(2):
@@ -354,30 +353,40 @@
     for_each_core(work)
 
 
-def encode_outer_kernel(
-    edge, pick, w_first, w_down, pool_far, after, mid, pool_mid, pool_s
+def middle_outer_kernel(
+    pool_far, w_down, fine_near, fine_far, skip_near, w_fine_skip, after,
+    mid, pool_mid, skip, fine_s,
 ):
     def work(core):
-        field = edge[16:] if core else edge[:160]
-        far, outer = (0, 2) if core else (4, 0)
-        pairs = range(5, 9) if core else range(-5, -1)
-        pool_s[:, far : far + 2] = pool_far[...]
-        encode(field, pick, w_first, pairs, None, 0, pool_s, outer)
-        rows, pooled = middle_rows(pool_s, w_down, 4 if core else -4, 4)
+        rows, pooled = middle_rows(pool_far, w_down, 4 if core else -4, 4)
         for at in range(2):
             put_three(pool_mid, at, pooled[at])
             for py in range(2):
                 put_shifts(mid, at, py, rows[py][at if core else at + 2])
+        if core:
+            fine_s[:, 0:2], fine_s[:, 2:5] = fine_near[:, 5:7], fine_far[...]
+        else:
+            fine_s[:, 0:3], fine_s[:, 3:5] = fine_far[...], fine_near[:, 0:2]
+        lhs = jnp.concatenate(
+            [
+                fine_s[dy : dy + 4, dx : dx + 3].reshape(384, 256)
+                for dx in range(3)
+                for dy in range(3)
+            ],
+            axis=1,
+        )
+        near, far = (0, 5) if core else (3, 0)
+        skip[:, far : far + 3] = dot(lhs, w_fine_skip[...]).reshape(4, 3, 32, 256)
+        skip[:, near : near + 5] = skip_near[...]
 
     for_each_core(work)
 
 
 def net_kernel(
-    from_twin, fine_near, fine_far, skip_near, mid_near, mid_far, mid_out,
-    pool_mid_in, pool_mid_out,
-    w_coarse, w_mid_skip, w_mid_up, w_fine_skip, w_fine_up, w_head,
+    from_twin, skip_s, mid_near, mid_far, mid_out, pool_mid_in, pool_mid_out,
+    w_coarse, w_mid_skip, w_mid_up, w_fine_up, w_head,
     out,
-    fine_s, mid_s, pool_mid_s, coarse_s, up_s, skip_s, last_s,
+    mid_s, pool_mid_s, coarse_s, up_s, mid_skip_s, last_s,
 ):
     mask = y_mask()
 
@@ -394,23 +403,6 @@
                 put_shifts(mid_s, last + at, py, from_twin[row : row + J].astype(F32))
             lanes = slice(at * 128, at * 128 + 128)
             put_three(pool_mid_s, 4 - cell + at, from_twin[4 * J :, lanes].astype(F32))
-        if core:
-            fine_s[:, 0:2], fine_s[:, 2:5] = fine_near[:, 5:7], fine_far[...]
-        else:
-            fine_s[:, 0:3], fine_s[:, 3:5] = fine_far[...], fine_near[:, 0:2]
-        lhs = jnp.concatenate(
-            [
-                fine_s[dy : dy + 4, dx : dx + 3].reshape(384, 256)
-                for dx in range(3)
-                for dy in range(3)
-            ],
-            axis=1,
-        )
-        skip = dot(lhs, w_fine_skip[...]).reshape(4, 3, 32, 256)
-        if core:
-            skip_s[:, 0:5], skip_s[:, 5:8] = skip_near[...], skip
-        else:
-            skip_s[:, 0:3], skip_s[:, 3:8] = skip, skip_near[...]
 
     for_each_core(gather)
 
@@ -434,43 +426,46 @@
         ],
         axis=1,
     )
-    skip = dot(lhs, w_mid_skip[...]).reshape(2, 6, J, 256)
-    for py in range(2):
+    mid_skip_s[...] = dot(lhs, w_mid_skip[...]).reshape(2, 6, J, 256)
+
+    @pl.loop(0, 2)
+    def _(px):
+        for py in range(2):
+            lhs = jnp.concatenate(
+                [
+                    coarse_s[py + ty, tx : tx + 3].reshape(3 * J, 256)
+                    for tx in range(2)
+                    for ty in range(2)
+                ],
+                axis=1,
+            )
+            up = dot(lhs, w_mid_up[px * 2 + py]).reshape(3, J, 256)
+            for k in range(3):
+                at = 2 * k + 1 - px
+                value = silu_half(mid_skip_s[py, at] + up[k])
+                masked = value * (mask * row_flag(lax.shift_right_arithmetic(at - 1, 1)))
+                up_s[py + 1, at] = masked[:32].astype(BF)
+                shift = 1 if py else J - 1
+                up_s[0 if py else 3, at] = pltpu.roll(masked, shift, 0)[:32].astype(BF)
+
+    @pl.loop(0, 4)
+    def _(parity):
+        px, py = parity // 2, parity % 2
         lhs = jnp.concatenate(
             [
-                coarse_s[py + ty, tx : tx + 3].reshape(3 * J, 256)
+                up_s[pl.ds(py + ty, 2), pl.ds(px + tx, 4)].reshape(256, 256)
                 for tx in range(2)
                 for ty in range(2)
             ],
             axis=1,
         )
-        for px in range(2):
-            up = dot(lhs, w_mid_up[px * 2 + py]).reshape(3, J, 256)
-            for k in range(3):
-                at = 2 * k if px else 2 * k + 1
-                value = silu_half(skip[py, at] + up[k])
-                masked = value * (mask * row_flag((at - 1) // 2))
-                up_s[py + 1, at] = masked[:32].astype(BF)
-                shift = 1 if py else J - 1
-                up_s[0 if py else 3, at] = pltpu.roll(masked, shift, 0)[:32].astype(BF)
-
-    for py in range(2):
-        for px in range(2):
-            lhs = jnp.concatenate(
-                [
-                    up_s[py + ty : py + ty + 2, px + tx : px + tx + 4].reshape(256, 256)
-                    for tx in range(2)
-                    for ty in range(2)
-                ],
-                axis=1,
-            )
-            up = dot(lhs, w_fine_up[px * 2 + py]).reshape(2, 4, 32, 256)
-            for half in range(2):
-                group = 2 * half + py
-                for k in range(4):
-                    x = 2 * k + px
-                    value = silu_half(skip_s[group, x] + up[half, k])
-                    last_s[x, pl.ds(group * 32, 32), :] = value.astype(BF)
+        up = dot(lhs, w_fine_up[parity]).reshape(2, 4, 32, 256)
+        for half in range(2):
+            group = 2 * half + py
+            for k in range(4):
+                value = silu_half(skip_s[group, 2 * k + px] + up[half, k])
+                row = pl.multiple_of(group * 32, 32)
+                last_s[2 * k + px, pl.ds(row, 32), :] = value.astype(BF)
 
     heads = jnp.concatenate([dot_nt(w_head[...], last_s[x]) for x in range(8)], axis=0)
     high = heads.astype(BF)
@@ -606,10 +601,10 @@
     )(fine_near, fine, w_fine_skip)
 
     fine_far, pool_far, mid_far, pool_mid_in, for_twin = pl.pallas_call(
-        encode_inner_kernel,
+        encode_far_kernel,
         out_shape=(
             shape(6, 3, 32, 256),
-            shape(4, 2, J, 128),
+            shape(4, 6, J, 128),
             shape(4, 2, J, 256),
             shape(3, 2, J, 128),
             shape(5 * J, 256),
@@ -624,28 +619,31 @@
         skip_near,
     )
     from_twin = lax.ppermute(for_twin, "gx", in_chip)
-    mid_out, pool_mid_out = pl.pallas_call(
-        encode_outer_kernel,
-        out_shape=(shape(4, 2, J, 256), shape(3, 2, J, 128)),
-        in_specs=[VMEM] * 5 + [ANY],
-        out_specs=(VMEM,) * 2,
-        scratch_shapes=[pltpu.VMEM((4, 6, J, 128), BF)],
+    mid_out, pool_mid_out, skip = pl.pallas_call(
+        middle_outer_kernel,
+        out_shape=(
+            shape(4, 2, J, 256),
+            shape(3, 2, J, 128),
+            shape(4, 8, 32, 256, kind=F32),
+        ),
+        in_specs=[VMEM] * 6 + [ANY],
+        out_specs=(VMEM,) * 3,
+        scratch_shapes=[pltpu.VMEM((6, 5, 32, 256), BF)],
         compiler_params=small(16),
         cost_estimate=cost(2 * 10**9, 3 * 10**6),
-    )(chip_edge, pick, w_first, w_down, pool_far, for_twin)
+    )(pool_far, w_down, fine_near, fine_far, skip_near, w_fine_skip, for_twin)
 
     return pl.pallas_call(
         net_kernel,
         out_shape=shape(16, 8, 128, kind=F32),
-        in_specs=[VMEM] * 15,
+        in_specs=[VMEM] * 12,
         out_specs=VMEM,
         scratch_shapes=[
-            pltpu.VMEM((6, 5, 32, 256), BF),
             pltpu.VMEM((4, 8, J, 256), BF),
             pltpu.VMEM((3, 6, J, 128), BF),
             pltpu.VMEM((3, 4, J, 256), BF),
             pltpu.VMEM((4, 6, 32, 256), BF),
-            pltpu.VMEM((4, 8, 32, 256), F32),
+            pltpu.VMEM((2, 6, J, 256), F32),
             pltpu.VMEM((8, 128, 256), BF),
         ],
         compiler_params=small(32),
@@ -653,9 +651,8 @@
             flops=6 * 10**9, bytes_accessed=9 * 10**6, transcendentals=10**6
         ),
     )(
-        from_twin, fine_near, fine_far, skip_near, mid_near, mid_far, mid_out,
-        pool_mid_in, pool_mid_out,
-        w_coarse, w_mid_skip, w_mid_up, w_fine_skip, w_fine_up, w_head,
+        from_twin, skip, mid_near, mid_far, mid_out, pool_mid_in, pool_mid_out,
+        w_coarse, w_mid_skip, w_mid_up, w_fine_up, w_head,
     )
 
 

time: 29 us -> 28.7 us (0.990)
  Pallas kernels: 12.8 us -> 12.2 us
  waiting for transfers between devices: 4.92 us -> 5.27 us
    pallas_call x1, Pallas kernels: 4.81 us -> 3.95 us  [body(): pl.pallas_call(net_kernel, out_shape=shape(16, 8, 128, kind=F32), in_spec...]
    ppermute x1, waiting for transfers between devices: 0.06 us -> 0.42 us  [body(): from_twin = lax.ppermute(for_twin, 'gx', in_chip)]
  transfers between devices with their start and end apart: 5 -> 5, of which waited for: 3 -> 3; matrix products, arithmetic and copies ran while one was open for 0% -> 0% of each run, Pallas kernels for 24% -> 23%
where the time goes in v10:
time: 28.7 us; the launch traced here: 28.5 us
  Pallas kernels  12.2 us (43%)
  starting transfers between devices  10.9 us (38%)
  waiting for transfers between devices  5.27 us (18%)
    ppermute x1, starting transfers between devices, body(): chip_edge = lax.ppermute(edge, 'gx', between)  5.03 us
    pallas_call x1, Pallas kernels, body(): pl.pallas_call(net_kernel, out_shape=shape(16, 8, 128, kind=F32), in_spec...  3.95 us
    ppermute x1, waiting for transfers between devices, body(): chip_edge = lax.ppermute(edge, 'gx', between)  2.54 us
    ppermute x1, waiting for transfers between devices, body(): y_outer = lax.ppermute(noisy_field, 'gy', swap_out)  2.31 us
    ppermute x1, starting transfers between devices, body(): twin = lax.ppermute(own, 'gx', in_chip)  2.19 us
    ppermute x1, starting transfers between devices, body(): y_outer = lax.ppermute(noisy_field, 'gy', swap_out)  1.92 us
    ppermute x1, starting transfers between devices, body(): y_inner = lax.ppermute(noisy_field, 'gy', swap_in)  1.64 us
    pallas_call x1, Pallas kernels, body(): pl.pallas_call(encoder_weights_kernel, out_shape=(shape(2, 192, 256), sha...  1.49 us
  transfers between devices with their start and end apart: 5, of which 3 were waited for; matrix products, arithmetic and copies ran while one was open for 0% of the time, Pallas kernels for 23%

profile of v10, /device:TPU:79, one launch (start us, length us, event | category | flops | bytes accessed | tf_op | source)
XLA Modules:
  0.0 28.5 jit_solution(2504799206242632866)
XLA Ops:
  0.0 0.0 copy-start
  0.0 1.6 %collective-permute-start = (bf16[16,8,128]{2,1,0:T(8,128)(2,1)}, bf16[16,8,128]{2,1,0:T(8,128)(2,1)S(1)}, u32[]{:S(2)}, u32[]{:S(2)}) collective-permute-start(bf16[16,8,128]{2,1,0:T(8,128)(2,1)} %own.1), channel_id=1, source_target_pairs={{0,1},{1,0},{2,3},{3,2},{4,5},{5,4},{6,7},{7,6},{8,9},{9,8},{10,11... | collective-permute-start | bytes 98312 | tf_op jit(solution)/shard_map/ppermute | solution.py:539
  1.6 1.9 %collective-permute-start.1 = (bf16[16,8,128]{2,1,0:T(8,128)(2,1)}, bf16[16,8,128]{2,1,0:T(8,128)(2,1)S(1)}, u32[]{:S(2)}, u32[]{:S(2)}) collective-permute-start(bf16[16,8,128]{2,1,0:T(8,128)(2,1)} %own.1), channel_id=1, source_target_pairs={{1,2},{2,1},{3,4},{4,3},{5,6},{6,5},{9,10},{10,9},{11,12},{12,11},... | collective-permute-start | bytes 98312 | tf_op jit(solution)/shard_map/ppermute | solution.py:540
  3.6 1.5 %shard_map.73 = (bf16[2,192,256]{2,1,0:T(8,128)(2,1)S(1)}, bf16[1152,256]{1,0:T(8,128)(2,1)S(1)}, bf16[1152,256]{1,0:T(8,128)(2,1)S(1)}, bf16[16,256]{1,0:T(8,12...) custom-call(bf16[9,3,16]{2,1,0:T(4,128)(2,1)} %bitcast.20, ...), custom_call_target="tpu_custom_call" | custom-call | flops 1000000000 | bytes 3000000 | tf_op jit(solution)/shard_map/pallas_call | solution.py:497
  5.1 0.0 collective-permute-done.inner
  5.1 2.3 %collective-permute-done.1.outer = bf16[16,8,128]{2,1,0:T(8,128)(2,1)S(1)} collective-permute-done((bf16[16,8,128]{2,1,0:T(8,128)(2,1)}, bf16[16,8,128]{2,1,0:T(8,128)(2,1)S(1)}, u32[]{:S(2)}, u32[]{:S(2)}) %collective-permute-start.1) | collective-permute-done | bytes 32800 | tf_op jit(solution)/shard_map/ppermute | solution.py:540
  7.4 0.0 copy-done
  7.4 0.2 shard_map.74.after.own
  7.6 2.2 %collective-permute-start.2 = (bf16[128,256]{1,0:T(8,128)(2,1)S(1)}, bf16[128,256]{1,0:T(8,128)(2,1)S(1)}, u32[]{:S(2)}, u32[]{:S(2)}) collective-permute-start(bf16[128,256]{1,0:T(8,128)(2,1)S(1)} %shard_map.74.after.own), channel_id=1, source_target_pairs={{0,8},{8,0},{16,24},{24,16},{32,40},{40,32},{48,56},{56,48},{64,72... | collective-permute-start | bytes 196616 | tf_op jit(solution)/shard_map/ppermute | solution.py:551
  9.8 1.3 %shard_map.75 = (bf16[2304,256]{1,0:T(8,128)(2,1)S(1)}, bf16[4,1024,256]{2,1,0:T(8,128)(2,1)S(1)}) custom-call(bf16[27,32,96]{2,1,0:T(8,128)(2,1)S(1)} %get-tuple-element.30.middle, bf16[128,256]{1,0:T(8,128)(2,1)S(1)} %shard_map.74.after.own), custom_call_target="tpu_custom_call" | custom-call | flops 1000000000 | bytes 4000000 | tf_op jit(solution)/shard_map/pallas_call | solution.py:552
  11.0 0.0 collective-permute-done.2.twin
  11.1 5.0 %collective-permute-start.3 = (bf16[176,256]{1,0:T(8,128)(2,1)S(1)}, bf16[176,256]{1,0:T(8,128)(2,1)S(1)}, u32[]{:S(2)}, u32[]{:S(2)}) collective-permute-start(bf16[176,256]{1,0:T(8,128)(2,1)S(1)} %shard_map.76.after), channel_id=1, source_target_pairs={{8,16},{16,8},{24,32},{32,24},{40,48},{48,40},{56,64},{64,56},{72,... | collective-permute-start | bytes 270344 | tf_op jit(solution)/shard_map/ppermute | solution.py:569
  16.1 0.4 %shard_map.78.w_fine_skip = bf16[2304,256]{1,0:T(8,128)(2,1)S(1)} custom-call(bf16[27,16,48]{2,1,0:T(8,128)(2,1)S(1)} %get-tuple-element.39.fine, bf16[176,256]{1,0:T(8,128)(2,1)S(1)} %shard_map.76.after), custom_call_target="tpu_custom_call" | custom-call | flops 1000000000 | bytes 2000000 | tf_op jit(solution)/shard_map/pallas_call | solution.py:585
  16.5 1.1 %shard_map.77 = (bf16[6,7,32,256]{3,2,1,0:T(8,128)(2,1)S(1)}, bf16[4,4,40,128]{3,2,1,0:T(8,128)(2,1)S(1)}, bf16[4,2,40,256]{3,2,1,0:T(8,128)(2,1)S(1)}, bf16[40,128]{1,0:T(8,128)(2,1)S(1)}, bf16[160,256]{1,0:T(8,128)(2,1)S(1)}) custom-call(bf16[128,256]{1,0:T(8,128)(2,1)S(1)} %shard_map.74.after.own, bf16[128,256]{1,0:T(8,128)(2,1)S(1)} %collective-permute-done.2.twin, ...), custom_call_target="tpu_custom_call" | custom-call | flops 1000000000 | bytes 3000000 | tf_op jit(solution)/shard_map/pallas_call | solution.py:571
  17.7 1.4 %shard_map.79 = (f32[4,5,32,256]{3,2,1,0:T(8,128)S(1)}, bf16[4,1024,256]{2,1,0:T(8,128)(2,1)S(1)}) custom-call(bf16[6,7,32,256]{3,2,1,0:T(8,128)(2,1)S(1)} %get-tuple-element.38.fine_near, bf16[27,16,48]{2,1,0:T(8,128)(2,1)S(1)} %get-tuple-element.39.fine, bf16[2304,256]{1,0:T(8,128)(2,1)S(1)} %shard_map.78.w_fine_skip), custom_call_target="tpu_custom_call" | custom-call | flops 1000000000 | bytes 4000000 | tf_op jit(solution)/shard_map/pallas_call | solution.py:593
  19.1 2.5 %collective-permute-done.3.edge = bf16[176,256]{1,0:T(8,128)(2,1)S(1)} collective-permute-done((bf16[176,256]{1,0:T(8,128)(2,1)S(1)}, bf16[176,256]{1,0:T(8,128)(2,1)S(1)}, u32[]{:S(2)}, u32[]{:S(2)}) %collective-permute-start.3) | collective-permute-done | bytes 90144 | tf_op jit(solution)/shard_map/ppermute | solution.py:569
  21.6 1.5 %shard_map.80 = (bf16[6,3,32,256]{3,2,1,0:T(8,128)(2,1)S(1)}, bf16[4,6,40,128]{3,2,1,0:T(8,128)(2,1)S(1)}, bf16[4,2,40,256]{3,2,1,0:T(8,128)(2,1)S(1)}, bf16[3,2...) custom-call(bf16[128,256]{1,0:T(8,128)(2,1)S(1)} %shard_map.74.after.own, ...), custom_call_target="tpu_custom_call" | custom-call | flops 1000000000 | bytes 3000000 | tf_op jit(solution)/shard_map/pallas_call | solution.py:603
  23.1 0.1 collective-permute-start.4
  23.2 0.9 %shard_map.81 = (bf16[4,2,40,256]{3,2,1,0:T(8,128)(2,1)S(1)}, bf16[3,2,40,128]{3,2,1,0:T(8,128)(2,1)S(1)}, f32[4,8,32,256]{3,2,1,0:T(8,128)S(1)}) custom-call(bf16[4,6,40,128]{3,2,1,0:T(8,128)(2,1)S(1)} %get-tuple-element.42.pool_far, bf16[1152,256]{1,0:T(8,128)(2,1)S(1)} %get-tuple-element.34.w_down, ...), custom_call_target="tpu_custom_call" | custom-call | flops 2000000000 | bytes 3000000 | tf_op jit(solution)/shard_map/pallas_call | solution.py:622
  24.1 0.4 %collective-permute-done.4.from_twin = bf16[200,256]{1,0:T(8,128)(2,1)S(1)} collective-permute-done((bf16[200,256]{1,0:T(8,128)(2,1)S(1)}, bf16[200,256]{1,0:T(8,128)(2,1)S(1)}, u32[]{:S(2)}, u32[]{:S(2)}) %collective-permute-start.4) | collective-permute-done | bytes 102432 | tf_op jit(solution)/shard_map/ppermute | solution.py:621
  24.5 4.0 %shard_map.82 = f32[16,8,128]{2,1,0:T(8,128)} custom-call(bf16[200,256]{1,0:T(8,128)(2,1)S(1)} %collective-permute-done.4.from_twin, f32[4,8,32,256]{3,2,1,0:T(8,128)S(1)} %get-tuple-element.44.skip_s, bf16[4,2,40,256]{3,2,1,0:T(8,128)(2,1)S(1)} %get-tuple-element.45.mid_near, bf16[4,2,40,256]{3,2,1,0:T(8,128)(2,1)S(1)} %get-tuple-element.46.mid_far, ...), custom_call_target="tpu_custom_call" | custom-call | flops 6000000000 | bytes 9000000 | tf_op jit(solution)/shard_map/pallas_call | solution.py:636
  (1 shorter events, 0.0 us)
Async XLA Ops:
  0.0 7.4 %copy-start = (bf16[16,8,128]{2,1,0:T(8,128)(2,1)S(1)}, bf16[16,8,128]{2,1,0:T(8,128)(2,1)}, u32[]{:S(2)}) copy-start(bf16[16,8,128]{2,1,0:T(8,128)(2,1)} %own.1) | copy-start | bytes 98308
  0.0 5.1 %collective-permute-start = (bf16[16,8,128]{2,1,0:T(8,128)(2,1)}, bf16[16,8,128]{2,1,0:T(8,128)(2,1)S(1)}, u32[]{:S(2)}, u32[]{:S(2)}) collective-permute-start(bf16[16,8,128]{2,1,0:T(8,128)(2,1)} %own.1), channel_id=1, source_target_pairs={{0,1},{1,0},{2,3},{3,2},{4,5},{5,4},{6,7},{7,6},{8,9},{9,8},{10,11... | collective-permute-start | bytes 98312 | tf_op jit(solution)/shard_map/ppermute | solution.py:539
  1.6 5.8 %collective-permute-start.1 = (bf16[16,8,128]{2,1,0:T(8,128)(2,1)}, bf16[16,8,128]{2,1,0:T(8,128)(2,1)S(1)}, u32[]{:S(2)}, u32[]{:S(2)}) collective-permute-start(bf16[16,8,128]{2,1,0:T(8,128)(2,1)} %own.1), channel_id=1, source_target_pairs={{1,2},{2,1},{3,4},{4,3},{5,6},{6,5},{9,10},{10,9},{11,12},{12,11},... | collective-permute-start | bytes 98312 | tf_op jit(solution)/shard_map/ppermute | solution.py:540
  7.6 3.5 %collective-permute-start.2 = (bf16[128,256]{1,0:T(8,128)(2,1)S(1)}, bf16[128,256]{1,0:T(8,128)(2,1)S(1)}, u32[]{:S(2)}, u32[]{:S(2)}) collective-permute-start(bf16[128,256]{1,0:T(8,128)(2,1)S(1)} %shard_map.74.after.own), channel_id=1, source_target_pairs={{0,8},{8,0},{16,24},{24,16},{32,40},{40,32},{48,56},{56,48},{64,72... | collective-permute-start | bytes 196616 | tf_op jit(solution)/shard_map/ppermute | solution.py:551
  11.1 10.6 %collective-permute-start.3 = (bf16[176,256]{1,0:T(8,128)(2,1)S(1)}, bf16[176,256]{1,0:T(8,128)(2,1)S(1)}, u32[]{:S(2)}, u32[]{:S(2)}) collective-permute-start(bf16[176,256]{1,0:T(8,128)(2,1)S(1)} %shard_map.76.after), channel_id=1, source_target_pairs={{8,16},{16,8},{24,32},{32,24},{40,48},{48,40},{56,64},{64,56},{72,... | collective-permute-start | bytes 270344 | tf_op jit(solution)/shard_map/ppermute | solution.py:569
  23.1 1.4 %collective-permute-start.4 = (bf16[200,256]{1,0:T(8,128)(2,1)S(1)}, bf16[200,256]{1,0:T(8,128)(2,1)S(1)}, u32[]{:S(2)}, u32[]{:S(2)}) collective-permute-start(bf16[200,256]{1,0:T(8,128)(2,1)S(1)} %get-tuple-element.41.after), channel_id=1, source_target_pairs={{0,8},{8,0},{16,24},{24,16},{32,40},{40,32},{48,56},{56,48},{64,72... | collective-permute-start | bytes 307208 | tf_op jit(solution)/shard_map/ppermute | solution.py:621

commit v11 on v8

--- a/solution.py
+++ b/solution.py
@@ -190,7 +190,7 @@
     banded(w_fine_skip, taps, 16, list(range(0, 16, 2)) + list(range(1, 16, 2)), natural(16))
 
 
-def join_kernel(own, inner, outer, after, out):
+def join_kernel(own, outer, inner, after, out):
     from_inner = (iota((128, 128), 1) < 64) == (lax.axis_index("gy") % 2 == 0)
     mine = own[...].astype(F32).reshape(128, 128)
     rim = jnp.where(
@@ -454,23 +454,24 @@
                 shift = 1 if py else J - 1
                 up_s[0 if py else 3, at] = pltpu.roll(masked, shift, 0)[:32].astype(BF)
 
-    for py in range(2):
-        for px in range(2):
-            lhs = jnp.concatenate(
-                [
-                    up_s[py + ty : py + ty + 2, px + tx : px + tx + 4].reshape(256, 256)
-                    for tx in range(2)
-                    for ty in range(2)
-                ],
-                axis=1,
-            )
-            up = dot(lhs, w_fine_up[px * 2 + py]).reshape(2, 4, 32, 256)
-            for half in range(2):
-                group = 2 * half + py
-                for k in range(4):
-                    x = 2 * k + px
-                    value = silu_half(skip_s[group, x] + up[half, k])
-                    last_s[x, pl.ds(group * 32, 32), :] = value.astype(BF)
+    @pl.loop(0, 4)
+    def _(parity):
+        px, py = parity // 2, parity % 2
+        lhs = jnp.concatenate(
+            [
+                up_s[pl.ds(py + ty, 2), pl.ds(px + tx, 4)].reshape(256, 256)
+                for tx in range(2)
+                for ty in range(2)
+            ],
+            axis=1,
+        )
+        up = dot(lhs, w_fine_up[parity]).reshape(2, 4, 32, 256)
+        for half in range(2):
+            group = 2 * half + py
+            for k in range(4):
+                value = silu_half(skip_s[group, 2 * k + px] + up[half, k])
+                row = pl.multiple_of(group * 32, 32)
+                last_s[2 * k + px, pl.ds(row, 32), :] = value.astype(BF)
 
     heads = jnp.concatenate([dot_nt(w_head[...], last_s[x]) for x in range(8)], axis=0)
     high = heads.astype(BF)
@@ -541,8 +542,8 @@
         return inner, [(i, ((i + 1) ^ 1) - 1) for i in range(1, count - 1)]
 
     swap_in, swap_out = pairs("gy")
+    y_outer = lax.ppermute(noisy_field, "gy", swap_out)
     y_inner = lax.ppermute(noisy_field, "gy", swap_in)
-    y_outer = lax.ppermute(noisy_field, "gy", swap_out)
     own = pl.pallas_call(
         join_kernel,
         out_shape=shape(128, 256),
@@ -550,7 +551,7 @@
         out_specs=VMEM,
         compiler_params=small(4),
         cost_estimate=cost(10**7, 2 * 10**5),
-    )(noisy_field, y_inner, y_outer, w_head)
+    )(noisy_field, y_outer, y_inner, w_head)
 
     in_chip, between = pairs("gx")
     twin = lax.ppermute(own, "gx", in_chip)

time: 29 us -> 28.1 us (0.969)
  waiting for transfers between devices: 4.92 us -> 3.5 us
  starting transfers between devices: 10.9 us -> 12 us
  Pallas kernels: 12.8 us -> 12.2 us
    ppermute x1, waiting for transfers between devices: 2.31 us -> 0.01 us  [body(): y_outer = lax.ppermute(noisy_field, 'gy', swap_out)]
    ppermute x1, starting transfers between devices: 1.92 us -> 3.55 us  [body(): y_outer = lax.ppermute(noisy_field, 'gy', swap_out)]
    ppermute x1, waiting for transfers between devices: 0.01 us -> 0.81 us  [body(): y_inner = lax.ppermute(noisy_field, 'gy', swap_in)]
    pallas_call x1, Pallas kernels: 4.81 us -> 4.16 us  [body(): pl.pallas_call(net_kernel, out_shape=shape(16, 8, 128, kind=F32), in_spec...]
    ppermute x1, starting transfers between devices: 1.64 us -> 1.04 us  [body(): y_inner = lax.ppermute(noisy_field, 'gy', swap_in)]
    ppermute x1, starting transfers between devices: 5.03 us -> 5.38 us  [body(): chip_edge = lax.ppermute(edge, 'gx', between)]
    ppermute x1, starting transfers between devices: 2.19 us -> 1.9 us  [body(): twin = lax.ppermute(own, 'gx', in_chip)]
  transfers between devices with their start and end apart: 5 -> 5, of which waited for: 3 -> 3; matrix products, arithmetic and copies ran while one was open for 0% -> 0% of each run, Pallas kernels for 24% -> 25%
where the time goes in v11:
time: 28.1 us; the launch traced here: 27.8 us
  Pallas kernels  12.2 us (43%)
  starting transfers between devices  12 us (43%)
  waiting for transfers between devices  3.5 us (12%)
    ppermute x1, starting transfers between devices, body(): chip_edge = lax.ppermute(edge, 'gx', between)  5.38 us
    pallas_call x1, Pallas kernels, body(): pl.pallas_call(net_kernel, out_shape=shape(16, 8, 128, kind=F32), in_spec...  4.16 us
    ppermute x1, starting transfers between devices, body(): y_outer = lax.ppermute(noisy_field, 'gy', swap_out)  3.55 us
    ppermute x1, waiting for transfers between devices, body(): chip_edge = lax.ppermute(edge, 'gx', between)  2.63 us
    ppermute x1, starting transfers between devices, body(): twin = lax.ppermute(own, 'gx', in_chip)  1.9 us
    pallas_call x1, Pallas kernels, body(): pl.pallas_call(encoder_weights_kernel, out_shape=(shape(2, 192, 256), sha...  1.49 us
    pallas_call x1, Pallas kernels, body(): pl.pallas_call(skip_near_kernel, out_shape=(shape(4, 5, 32, 256, kind=F32...  1.44 us
    pallas_call x1, Pallas kernels, body(): pl.pallas_call(mid_weights_kernel, out_shape=(shape(2304, 256), shape(4,...  1.25 us
  transfers between devices with their start and end apart: 5, of which 3 were waited for; matrix products, arithmetic and copies ran while one was open for 0% of the time, Pallas kernels for 25%

profile of v11, /device:TPU:79, one launch (start us, length us, event | category | flops | bytes accessed | tf_op | source)
XLA Modules:
  0.0 27.8 jit_solution(14852048163862587717)
XLA Ops:
  0.0 0.0 copy-start
  0.0 3.6 %collective-permute-start = (bf16[16,8,128]{2,1,0:T(8,128)(2,1)}, bf16[16,8,128]{2,1,0:T(8,128)(2,1)S(1)}, u32[]{:S(2)}, u32[]{:S(2)}) collective-permute-start(bf16[16,8,128]{2,1,0:T(8,128)(2,1)} %own.1), channel_id=1, source_target_pairs={{1,2},{2,1},{3,4},{4,3},{5,6},{6,5},{9,10},{10,9},{11,12},{12,11},... | collective-permute-start | bytes 98312 | tf_op jit(solution)/shard_map/ppermute | solution.py:545
  3.6 1.0 %collective-permute-start.1 = (bf16[16,8,128]{2,1,0:T(8,128)(2,1)}, bf16[16,8,128]{2,1,0:T(8,128)(2,1)S(1)}, u32[]{:S(2)}, u32[]{:S(2)}) collective-permute-start(bf16[16,8,128]{2,1,0:T(8,128)(2,1)} %own.1), channel_id=1, source_target_pairs={{0,1},{1,0},{2,3},{3,2},{4,5},{5,4},{6,7},{7,6},{8,9},{9,8},{10,11... | collective-permute-start | bytes 98312 | tf_op jit(solution)/shard_map/ppermute | solution.py:546
  4.6 1.5 %shard_map.73 = (bf16[2,192,256]{2,1,0:T(8,128)(2,1)S(1)}, bf16[1152,256]{1,0:T(8,128)(2,1)S(1)}, bf16[1152,256]{1,0:T(8,128)(2,1)S(1)}, bf16[16,256]{1,0:T(8,12...) custom-call(bf16[9,3,16]{2,1,0:T(4,128)(2,1)} %bitcast.20, ...), custom_call_target="tpu_custom_call" | custom-call | flops 1000000000 | bytes 3000000 | tf_op jit(solution)/shard_map/pallas_call | solution.py:503
  6.1 0.0 collective-permute-done.outer
  6.1 0.8 %collective-permute-done.1.inner = bf16[16,8,128]{2,1,0:T(8,128)(2,1)S(1)} collective-permute-done((bf16[16,8,128]{2,1,0:T(8,128)(2,1)}, bf16[16,8,128]{2,1,0:T(8,128)(2,1)S(1)}, u32[]{:S(2)}, u32[]{:S(2)}) %collective-permute-start.1) | collective-permute-done | bytes 32800 | tf_op jit(solution)/shard_map/ppermute | solution.py:546
  6.9 0.0 copy-done
  6.9 0.2 shard_map.74.after.own
  7.1 1.9 %collective-permute-start.2 = (bf16[128,256]{1,0:T(8,128)(2,1)S(1)}, bf16[128,256]{1,0:T(8,128)(2,1)S(1)}, u32[]{:S(2)}, u32[]{:S(2)}) collective-permute-start(bf16[128,256]{1,0:T(8,128)(2,1)S(1)} %shard_map.74.after.own), channel_id=1, source_target_pairs={{0,8},{8,0},{16,24},{24,16},{32,40},{40,32},{48,56},{56,48},{64,72... | collective-permute-start | bytes 196616 | tf_op jit(solution)/shard_map/ppermute | solution.py:557
  9.0 1.3 %shard_map.75 = (bf16[2304,256]{1,0:T(8,128)(2,1)S(1)}, bf16[4,1024,256]{2,1,0:T(8,128)(2,1)S(1)}) custom-call(bf16[27,32,96]{2,1,0:T(8,128)(2,1)S(1)} %get-tuple-element.29.middle, bf16[128,256]{1,0:T(8,128)(2,1)S(1)} %shard_map.74.after.own), custom_call_target="tpu_custom_call" | custom-call | flops 1000000000 | bytes 4000000 | tf_op jit(solution)/shard_map/pallas_call | solution.py:558
  10.2 0.0 collective-permute-done.2.twin
  10.3 5.4 %collective-permute-start.3 = (bf16[176,256]{1,0:T(8,128)(2,1)S(1)}, bf16[176,256]{1,0:T(8,128)(2,1)S(1)}, u32[]{:S(2)}, u32[]{:S(2)}) collective-permute-start(bf16[176,256]{1,0:T(8,128)(2,1)S(1)} %shard_map.76.after), channel_id=1, source_target_pairs={{8,16},{16,8},{24,32},{32,24},{40,48},{48,40},{56,64},{64,56},{72,... | collective-permute-start | bytes 270344 | tf_op jit(solution)/shard_map/ppermute | solution.py:575
  15.7 0.4 %shard_map.78.w_fine_skip = bf16[2304,256]{1,0:T(8,128)(2,1)S(1)} custom-call(bf16[27,16,48]{2,1,0:T(8,128)(2,1)S(1)} %get-tuple-element.38.fine, bf16[176,256]{1,0:T(8,128)(2,1)S(1)} %shard_map.76.after), custom_call_target="tpu_custom_call" | custom-call | flops 1000000000 | bytes 2000000 | tf_op jit(solution)/shard_map/pallas_call | solution.py:591
  16.1 1.1 %shard_map.77 = (bf16[6,7,32,256]{3,2,1,0:T(8,128)(2,1)S(1)}, bf16[4,4,40,128]{3,2,1,0:T(8,128)(2,1)S(1)}, bf16[4,2,40,256]{3,2,1,0:T(8,128)(2,1)S(1)}, bf16[40,128]{1,0:T(8,128)(2,1)S(1)}, bf16[160,256]{1,0:T(8,128)(2,1)S(1)}) custom-call(bf16[128,256]{1,0:T(8,128)(2,1)S(1)} %shard_map.74.after.own, bf16[128,256]{1,0:T(8,128)(2,1)S(1)} %collective-permute-done.2.twin, ...), custom_call_target="tpu_custom_call" | custom-call | flops 1000000000 | bytes 3000000 | tf_op jit(solution)/shard_map/pallas_call | solution.py:577
  17.2 1.4 %shard_map.79 = (f32[4,5,32,256]{3,2,1,0:T(8,128)S(1)}, bf16[4,1024,256]{2,1,0:T(8,128)(2,1)S(1)}) custom-call(bf16[6,7,32,256]{3,2,1,0:T(8,128)(2,1)S(1)} %get-tuple-element.37.fine_near, bf16[27,16,48]{2,1,0:T(8,128)(2,1)S(1)} %get-tuple-element.38.fine, bf16[2304,256]{1,0:T(8,128)(2,1)S(1)} %shard_map.78.w_fine_skip), custom_call_target="tpu_custom_call" | custom-call | flops 1000000000 | bytes 4000000 | tf_op jit(solution)/shard_map/pallas_call | solution.py:599
  18.7 2.6 %collective-permute-done.3.edge = bf16[176,256]{1,0:T(8,128)(2,1)S(1)} collective-permute-done((bf16[176,256]{1,0:T(8,128)(2,1)S(1)}, bf16[176,256]{1,0:T(8,128)(2,1)S(1)}, u32[]{:S(2)}, u32[]{:S(2)}) %collective-permute-start.3) | collective-permute-done | bytes 90144 | tf_op jit(solution)/shard_map/ppermute | solution.py:575
  21.3 0.9 %shard_map.80 = (bf16[6,3,32,256]{3,2,1,0:T(8,128)(2,1)S(1)}, bf16[4,2,40,128]{3,2,1,0:T(8,128)(2,1)S(1)}, bf16[4,2,40,256]{3,2,1,0:T(8,128)(2,1)S(1)}, bf16[3,2...) custom-call(bf16[128,256]{1,0:T(8,128)(2,1)S(1)} %shard_map.74.after.own, ...), custom_call_target="tpu_custom_call" | custom-call | flops 1000000000 | bytes 3000000 | tf_op jit(solution)/shard_map/pallas_call | solution.py:609
  22.2 0.1 collective-permute-start.4
  22.3 1.2 %shard_map.81 = (bf16[4,2,40,256]{3,2,1,0:T(8,128)(2,1)S(1)}, bf16[3,2,40,128]{3,2,1,0:T(8,128)(2,1)S(1)}) custom-call(bf16[176,256]{1,0:T(8,128)(2,1)S(1)} %collective-permute-done.3.edge, bf16[160,256]{1,0:T(8,128)(2,1)S(1)} %get-tuple-element.31.pick, bf16[2,192,256]{2,1,0:T(8,128)(2,1)S(1)} %get-tuple-element.32.w_first, ...), custom_call_target="tpu_custom_call" | custom-call | flops 2000000000 | bytes 3000000 | tf_op jit(solution)/shard_map/pallas_call | solution.py:628
  23.6 0.1 collective-permute-done.4.from_twin
  23.6 4.2 %shard_map.82 = f32[16,8,128]{2,1,0:T(8,128)} custom-call(bf16[200,256]{1,0:T(8,128)(2,1)S(1)} %collective-permute-done.4.from_twin, bf16[6,7,32,256]{3,2,1,0:T(8,128)(2,1)S(1)} %get-tuple-element.37.fine_near, bf16[6,3,32,256]{3,2,1,0:T(8,128)(2,1)S(1)} %get-tuple-element.41.fine_far, f32[4,5,32,256]{3,2,1,0:T(8,128)S(1)} %get-tuple-element.39.after.skip_near, ...), custom_call_target="tpu_custom_call" | custom-call | flops 6000000000 | bytes 9000000 | tf_op jit(solution)/shard_map/pallas_call | solution.py:638
  (1 shorter events, 0.0 us)
Async XLA Ops:
  0.0 6.9 %copy-start = (bf16[16,8,128]{2,1,0:T(8,128)(2,1)S(1)}, bf16[16,8,128]{2,1,0:T(8,128)(2,1)}, u32[]{:S(2)}) copy-start(bf16[16,8,128]{2,1,0:T(8,128)(2,1)} %own.1) | copy-start | bytes 98308
  0.0 6.1 %collective-permute-start = (bf16[16,8,128]{2,1,0:T(8,128)(2,1)}, bf16[16,8,128]{2,1,0:T(8,128)(2,1)S(1)}, u32[]{:S(2)}, u32[]{:S(2)}) collective-permute-start(bf16[16,8,128]{2,1,0:T(8,128)(2,1)} %own.1), channel_id=1, source_target_pairs={{1,2},{2,1},{3,4},{4,3},{5,6},{6,5},{9,10},{10,9},{11,12},{12,11},... | collective-permute-start | bytes 98312 | tf_op jit(solution)/shard_map/ppermute | solution.py:545
  3.6 3.4 %collective-permute-start.1 = (bf16[16,8,128]{2,1,0:T(8,128)(2,1)}, bf16[16,8,128]{2,1,0:T(8,128)(2,1)S(1)}, u32[]{:S(2)}, u32[]{:S(2)}) collective-permute-start(bf16[16,8,128]{2,1,0:T(8,128)(2,1)} %own.1), channel_id=1, source_target_pairs={{0,1},{1,0},{2,3},{3,2},{4,5},{5,4},{6,7},{7,6},{8,9},{9,8},{10,11... | collective-permute-start | bytes 98312 | tf_op jit(solution)/shard_map/ppermute | solution.py:546
  7.1 3.2 %collective-permute-start.2 = (bf16[128,256]{1,0:T(8,128)(2,1)S(1)}, bf16[128,256]{1,0:T(8,128)(2,1)S(1)}, u32[]{:S(2)}, u32[]{:S(2)}) collective-permute-start(bf16[128,256]{1,0:T(8,128)(2,1)S(1)} %shard_map.74.after.own), channel_id=1, source_target_pairs={{0,8},{8,0},{16,24},{24,16},{32,40},{40,32},{48,56},{56,48},{64,72... | collective-permute-start | bytes 196616 | tf_op jit(solution)/shard_map/ppermute | solution.py:557
  10.3 11.0 %collective-permute-start.3 = (bf16[176,256]{1,0:T(8,128)(2,1)S(1)}, bf16[176,256]{1,0:T(8,128)(2,1)S(1)}, u32[]{:S(2)}, u32[]{:S(2)}) collective-permute-start(bf16[176,256]{1,0:T(8,128)(2,1)S(1)} %shard_map.76.after), channel_id=1, source_target_pairs={{8,16},{16,8},{24,32},{32,24},{40,48},{48,40},{56,64},{64,56},{72,... | collective-permute-start | bytes 270344 | tf_op jit(solution)/shard_map/ppermute | solution.py:575
  22.2 1.4 %collective-permute-start.4 = (bf16[200,256]{1,0:T(8,128)(2,1)S(1)}, bf16[200,256]{1,0:T(8,128)(2,1)S(1)}, u32[]{:S(2)}, u32[]{:S(2)}) collective-permute-start(bf16[200,256]{1,0:T(8,128)(2,1)S(1)} %get-tuple-element.40.after), channel_id=1, source_target_pairs={{0,8},{8,0},{16,24},{24,16},{32,40},{40,32},{48,56},{56,48},{64,72... | collective-permute-start | bytes 307208 | tf_op jit(solution)/shard_map/ppermute | solution.py:627

commit v12 on v11

--- a/solution.py
+++ b/solution.py
@@ -174,13 +174,18 @@
         copy.wait()
 
 
-def mid_weights_kernel(middle, after, w_mid_skip, w_mid_up, tiled):
+def mid_skip_weights_kernel(middle, w_mid_skip):
+    r32 = repeat_matrix(32)
+    tiled = [(dot_tn(middle[tap], r32)[64:] * 0.5).astype(BF) for tap in range(27)]
+    taps = [tiled[dz * 9 : dz * 9 + 9] for dz in range(3)]
+    banded(w_mid_skip, taps, 32, [0, 2, 4, 6, 1, 3, 5, 7], natural(32))
+
+
+def mid_up_weights_kernel(middle, after, w_mid_up, tiled):
     r32 = repeat_matrix(32)
     for tap in range(27):
-        tiled[tap] = dot_tn(middle[tap], r32) * 0.5
-    taps = [[tiled[dz * 9 + xy, 64:96, :].astype(BF) for xy in range(9)] for dz in range(3)]
-    banded(w_mid_skip, taps, 32, [0, 2, 4, 6, 1, 3, 5, 7], natural(32))
-    folded(w_mid_up, lambda dz, dx, dy: tiled[dz * 9 + dx * 3 + dy, 0:64, :], 64, 4, natural(32))
+        tiled[tap] = dot_tn(middle[tap], r32)[:64] * 0.5
+    folded(w_mid_up, lambda dz, dx, dy: tiled[dz * 9 + dx * 3 + dy], 64, 4, natural(32))
 
 
 def fine_weights_kernel(fine, after, w_fine_skip):
@@ -190,7 +195,7 @@
     banded(w_fine_skip, taps, 16, list(range(0, 16, 2)) + list(range(1, 16, 2)), natural(16))
 
 
-def join_kernel(own, outer, inner, after, out):
+def join_kernel(own, outer, inner, after, also_after, out):
     from_inner = (iota((128, 128), 1) < 64) == (lax.axis_index("gy") % 2 == 0)
     mine = own[...].astype(F32).reshape(128, 128)
     rim = jnp.where(
@@ -355,14 +360,30 @@
 
 
 def encode_outer_kernel(
-    edge, pick, w_first, w_down, pool_far, after, mid, pool_mid, pool_s
+    edge, pick, w_first, w_down, pool_far, fine_near, fine_far, skip_near, w_fine_skip, after,
+    mid, pool_mid, skip, pool_s, fine_s,
 ):
     def work(core):
+        if core:
+            fine_s[:, 0:2], fine_s[:, 2:5] = fine_near[:, 5:7], fine_far[...]
+        else:
+            fine_s[:, 0:3], fine_s[:, 3:5] = fine_far[...], fine_near[:, 0:2]
         field = edge[16:] if core else edge[:160]
         far, outer = (0, 2) if core else (4, 0)
         pairs = range(5, 9) if core else range(-5, -1)
         pool_s[:, far : far + 2] = pool_far[...]
         encode(field, pick, w_first, pairs, None, 0, pool_s, outer)
+        lhs = jnp.concatenate(
+            [
+                fine_s[dy : dy + 4, dx : dx + 3].reshape(384, 256)
+                for dx in range(3)
+                for dy in range(3)
+            ],
+            axis=1,
+        )
+        near, rest = (0, 5) if core else (3, 0)
+        skip[:, rest : rest + 3] = dot(lhs, w_fine_skip[...]).reshape(4, 3, 32, 256)
+        skip[:, near : near + 5] = skip_near[...]
         rows, pooled = middle_rows(pool_s, w_down, 4 if core else -4, 4)
         for at in range(2):
             put_three(pool_mid, at, pooled[at])
@@ -373,11 +394,10 @@
 
 
 def net_kernel(
-    from_twin, fine_near, fine_far, skip_near, mid_near, mid_far, mid_out,
-    pool_mid_in, pool_mid_out,
-    w_coarse, w_mid_skip, w_mid_up, w_fine_skip, w_fine_up, w_head,
+    from_twin, skip_s, mid_near, mid_far, mid_out, pool_mid_in, pool_mid_out,
+    w_coarse, w_mid_skip, w_mid_up, w_fine_up, w_head,
     out,
-    fine_s, mid_s, pool_mid_s, coarse_s, up_s, skip_s, last_s,
+    mid_s, pool_mid_s, coarse_s, up_s, last_s,
 ):
     mask = y_mask()
 
@@ -394,23 +414,6 @@
                 put_shifts(mid_s, last + at, py, from_twin[row : row + J].astype(F32))
             lanes = slice(at * 128, at * 128 + 128)
             put_three(pool_mid_s, 4 - cell + at, from_twin[4 * J :, lanes].astype(F32))
-        if core:
-            fine_s[:, 0:2], fine_s[:, 2:5] = fine_near[:, 5:7], fine_far[...]
-        else:
-            fine_s[:, 0:3], fine_s[:, 3:5] = fine_far[...], fine_near[:, 0:2]
-        lhs = jnp.concatenate(
-            [
-                fine_s[dy : dy + 4, dx : dx + 3].reshape(384, 256)
-                for dx in range(3)
-                for dy in range(3)
-            ],
-            axis=1,
-        )
-        skip = dot(lhs, w_fine_skip[...]).reshape(4, 3, 32, 256)
-        if core:
-            skip_s[:, 0:5], skip_s[:, 5:8] = skip_near[...], skip
-        else:
-            skip_s[:, 0:3], skip_s[:, 3:8] = skip, skip_near[...]
 
     for_each_core(gather)
 
@@ -536,6 +539,15 @@
         )
     )
 
+    w_mid_skip = pl.pallas_call(
+        mid_skip_weights_kernel,
+        out_shape=shape(2304, 256),
+        in_specs=[VMEM],
+        out_specs=VMEM,
+        compiler_params=small(16),
+        cost_estimate=cost(10**9, 2 * 10**6),
+    )(middle)
+
     def pairs(axis):
         count = lax.axis_size(axis)
         inner = [(i, i ^ 1) for i in range(count)]
@@ -547,20 +559,20 @@
     own = pl.pallas_call(
         join_kernel,
         out_shape=shape(128, 256),
-        in_specs=[VMEM] * 3 + [ANY],
+        in_specs=[VMEM] * 3 + [ANY] * 2,
         out_specs=VMEM,
         compiler_params=small(4),
         cost_estimate=cost(10**7, 2 * 10**5),
-    )(noisy_field, y_outer, y_inner, w_head)
+    )(noisy_field, y_outer, y_inner, w_head, w_mid_skip)
 
     in_chip, between = pairs("gx")
     twin = lax.ppermute(own, "gx", in_chip)
-    w_mid_skip, w_mid_up = pl.pallas_call(
-        mid_weights_kernel,
-        out_shape=(shape(2304, 256), shape(4, 1024, 256)),
+    w_mid_up = pl.pallas_call(
+        mid_up_weights_kernel,
+        out_shape=shape(4, 1024, 256),
         in_specs=[VMEM, ANY],
-        out_specs=(VMEM,) * 2,
-        scratch_shapes=[pltpu.VMEM((27, 96, 256), F32)],
+        out_specs=VMEM,
+        scratch_shapes=[pltpu.VMEM((27, 64, 256), F32)],
         compiler_params=small(24),
         cost_estimate=cost(10**9, 4 * 10**6),
     )(middle, own)
@@ -571,7 +583,7 @@
         out_specs=VMEM,
         compiler_params=small(4),
         cost_estimate=cost(10**5, 3 * 10**5),
-    )(own, twin, w_mid_skip)
+    )(own, twin, w_mid_up)
     chip_edge = lax.ppermute(edge, "gx", between)
 
     fine_near, pool_near, mid_near, pool_mid_near, for_twin_near = pl.pallas_call(
@@ -625,28 +637,33 @@
         skip_near,
     )
     from_twin = lax.ppermute(for_twin, "gx", in_chip)
-    mid_out, pool_mid_out = pl.pallas_call(
+    mid_out, pool_mid_out, skip = pl.pallas_call(
         encode_outer_kernel,
-        out_shape=(shape(4, 2, J, 256), shape(3, 2, J, 128)),
-        in_specs=[VMEM] * 5 + [ANY],
-        out_specs=(VMEM,) * 2,
-        scratch_shapes=[pltpu.VMEM((4, 6, J, 128), BF)],
+        out_shape=(
+            shape(4, 2, J, 256),
+            shape(3, 2, J, 128),
+            shape(4, 8, 32, 256, kind=F32),
+        ),
+        in_specs=[VMEM] * 9 + [ANY],
+        out_specs=(VMEM,) * 3,
+        scratch_shapes=[pltpu.VMEM((4, 6, J, 128), BF), pltpu.VMEM((6, 5, 32, 256), BF)],
         compiler_params=small(16),
         cost_estimate=cost(2 * 10**9, 3 * 10**6),
-    )(chip_edge, pick, w_first, w_down, pool_far, for_twin)
+    )(
+        chip_edge, pick, w_first, w_down, pool_far, fine_near, fine_far, skip_near, w_fine_skip,
+        for_twin,
+    )
 
     return pl.pallas_call(
         net_kernel,
         out_shape=shape(16, 8, 128, kind=F32),
-        in_specs=[VMEM] * 15,
+        in_specs=[VMEM] * 12,
         out_specs=VMEM,
         scratch_shapes=[
-            pltpu.VMEM((6, 5, 32, 256), BF),
             pltpu.VMEM((4, 8, J, 256), BF),
             pltpu.VMEM((3, 6, J, 128), BF),
             pltpu.VMEM((3, 4, J, 256), BF),
             pltpu.VMEM((4, 6, 32, 256), BF),
-            pltpu.VMEM((4, 8, 32, 256), F32),
             pltpu.VMEM((8, 128, 256), BF),
         ],
         compiler_params=small(32),
@@ -654,9 +671,8 @@
             flops=6 * 10**9, bytes_accessed=9 * 10**6, transcendentals=10**6
         ),
     )(
-        from_twin, fine_near, fine_far, skip_near, mid_near, mid_far, mid_out,
-        pool_mid_in, pool_mid_out,
-        w_coarse, w_mid_skip, w_mid_up, w_fine_skip, w_fine_up, w_head,
+        from_twin, skip, mid_near, mid_far, mid_out, pool_mid_in, pool_mid_out,
+        w_coarse, w_mid_skip, w_mid_up, w_fine_up, w_head,
     )
 
 

time: 28.1 us -> 27.7 us (0.986)
  waiting for transfers between devices: 3.5 us -> 2.73 us
    pallas_call x1, Pallas kernels: 4.16 us -> 3.56 us  [body(): pl.pallas_call(net_kernel, out_shape=shape(16, 8, 128, kind=F32), in_spec...]
    ppermute x1, waiting for transfers between devices: 0.81 us -> 0.23 us  [body(): y_inner = lax.ppermute(noisy_field, 'gy', swap_in)]
    pallas_call x1, Pallas kernels: 1.23 us -> 1.65 us  [body(): pl.pallas_call(encode_outer_kernel, out_shape=(shape(4, 2, J, 256), shape...]
    pallas_call x1 -> x2, Pallas kernels: 1.25 us -> 1.64 us  [the longest x1 1.08 us: body(): pl.pallas_call(mid_up_weights_kernel, out_shape=shape(4, 1024, 256), in_s...]
  transfers between devices with their start and end apart: 5 -> 5, of which waited for: 3 -> 2; matrix products, arithmetic and copies ran while one was open for 0% -> 0% of each run, Pallas kernels for 25% -> 29%
where the time goes in v12:
time: 27.7 us; the launch traced here: 27.2 us
  Pallas kernels  12.4 us (45%)
  starting transfers between devices  12 us (43%)
  waiting for transfers between devices  2.73 us (10%)
    ppermute x1, starting transfers between devices, body(): chip_edge = lax.ppermute(edge, 'gx', between)  5.51 us
    pallas_call x1, Pallas kernels, body(): pl.pallas_call(net_kernel, out_shape=shape(16, 8, 128, kind=F32), in_spec...  3.56 us
    ppermute x1, starting transfers between devices, body(): y_outer = lax.ppermute(noisy_field, 'gy', swap_out)  3.42 us
    ppermute x1, waiting for transfers between devices, body(): chip_edge = lax.ppermute(edge, 'gx', between)  2.5 us
    ppermute x1, starting transfers between devices, body(): twin = lax.ppermute(own, 'gx', in_chip)  1.9 us
    pallas_call x1, Pallas kernels, body(): pl.pallas_call(encode_outer_kernel, out_shape=(shape(4, 2, J, 256), shape...  1.65 us
    pallas_call x1, Pallas kernels, body(): pl.pallas_call(encoder_weights_kernel, out_shape=(shape(2, 192, 256), sha...  1.49 us
    pallas_call x1, Pallas kernels, body(): pl.pallas_call(skip_near_kernel, out_shape=(shape(4, 5, 32, 256, kind=F32...  1.44 us
  transfers between devices with their start and end apart: 5, of which 2 were waited for; matrix products, arithmetic and copies ran while one was open for 0% of the time, Pallas kernels for 29%

profile of v12, /device:TPU:79, one launch (start us, length us, event | category | flops | bytes accessed | tf_op | source)
XLA Modules:
  0.0 27.2 jit_solution(10147284098464156456)
XLA Ops:
  0.0 3.4 %collective-permute-start = (bf16[16,8,128]{2,1,0:T(8,128)(2,1)}, bf16[16,8,128]{2,1,0:T(8,128)(2,1)S(1)}, u32[]{:S(2)}, u32[]{:S(2)}) collective-permute-start(bf16[16,8,128]{2,1,0:T(8,128)(2,1)} %own.1), channel_id=1, source_target_pairs={{1,2},{2,1},{3,4},{4,3},{5,6},{6,5},{9,10},{10,9},{11,12},{12,11},... | collective-permute-start | bytes 98312 | tf_op jit(solution)/shard_map/ppermute | solution.py:557
  3.4 1.0 %collective-permute-start.1 = (bf16[16,8,128]{2,1,0:T(8,128)(2,1)}, bf16[16,8,128]{2,1,0:T(8,128)(2,1)S(1)}, u32[]{:S(2)}, u32[]{:S(2)}) collective-permute-start(bf16[16,8,128]{2,1,0:T(8,128)(2,1)} %own.1), channel_id=1, source_target_pairs={{0,1},{1,0},{2,3},{3,2},{4,5},{5,4},{6,7},{7,6},{8,9},{9,8},{10,11... | collective-permute-start | bytes 98312 | tf_op jit(solution)/shard_map/ppermute | solution.py:558
  4.5 1.5 %shard_map.73 = (bf16[2,192,256]{2,1,0:T(8,128)(2,1)S(1)}, bf16[1152,256]{1,0:T(8,128)(2,1)S(1)}, bf16[1152,256]{1,0:T(8,128)(2,1)S(1)}, bf16[16,256]{1,0:T(8,12...) custom-call(bf16[9,3,16]{2,1,0:T(4,128)(2,1)} %bitcast.20, ...), custom_call_target="tpu_custom_call" | custom-call | flops 1000000000 | bytes 3000000 | tf_op jit(solution)/shard_map/pallas_call | solution.py:506
  6.0 0.0 copy-start
  6.0 0.6 %shard_map.74.also_after.w_mid_skip = bf16[2304,256]{1,0:T(8,128)(2,1)S(1)} custom-call(bf16[27,32,96]{2,1,0:T(8,128)(2,1)S(1)} %get-tuple-element.28.middle), custom_call_target="tpu_custom_call" | custom-call | flops 1000000000 | bytes 2000000 | tf_op jit(solution)/shard_map/pallas_call | solution.py:542
  6.5 0.0 collective-permute-done.outer
  6.6 0.2 collective-permute-done.1.inner
  6.8 0.0 copy-done
  6.8 0.2 shard_map.75.after.own
  7.0 1.9 %collective-permute-start.2 = (bf16[128,256]{1,0:T(8,128)(2,1)S(1)}, bf16[128,256]{1,0:T(8,128)(2,1)S(1)}, u32[]{:S(2)}, u32[]{:S(2)}) collective-permute-start(bf16[128,256]{1,0:T(8,128)(2,1)S(1)} %shard_map.75.after.own), channel_id=1, source_target_pairs={{0,8},{8,0},{16,24},{24,16},{32,40},{40,32},{48,56},{56,48},{64,72... | collective-permute-start | bytes 196616 | tf_op jit(solution)/shard_map/ppermute | solution.py:569
  8.8 1.1 %shard_map.76.after.w_mid_up = bf16[4,1024,256]{2,1,0:T(8,128)(2,1)S(1)} custom-call(bf16[27,32,96]{2,1,0:T(8,128)(2,1)S(1)} %get-tuple-element.28.middle, bf16[128,256]{1,0:T(8,128)(2,1)S(1)} %shard_map.75.after.own), custom_call_target="tpu_custom_call" | custom-call | flops 1000000000 | bytes 4000000 | tf_op jit(solution)/shard_map/pallas_call | solution.py:570
  9.9 0.0 collective-permute-done.2.twin
  10.0 5.5 %collective-permute-start.3 = (bf16[176,256]{1,0:T(8,128)(2,1)S(1)}, bf16[176,256]{1,0:T(8,128)(2,1)S(1)}, u32[]{:S(2)}, u32[]{:S(2)}) collective-permute-start(bf16[176,256]{1,0:T(8,128)(2,1)S(1)} %shard_map.77.after), channel_id=1, source_target_pairs={{8,16},{16,8},{24,32},{32,24},{40,48},{48,40},{56,64},{64,56},{72,... | collective-permute-start | bytes 270344 | tf_op jit(solution)/shard_map/ppermute | solution.py:587
  15.5 0.4 %shard_map.79.w_fine_skip = bf16[2304,256]{1,0:T(8,128)(2,1)S(1)} custom-call(bf16[27,16,48]{2,1,0:T(8,128)(2,1)S(1)} %get-tuple-element.36.fine, bf16[176,256]{1,0:T(8,128)(2,1)S(1)} %shard_map.77.after), custom_call_target="tpu_custom_call" | custom-call | flops 1000000000 | bytes 2000000 | tf_op jit(solution)/shard_map/pallas_call | solution.py:603
  15.9 1.1 %shard_map.78 = (bf16[6,7,32,256]{3,2,1,0:T(8,128)(2,1)S(1)}, bf16[4,4,40,128]{3,2,1,0:T(8,128)(2,1)S(1)}, bf16[4,2,40,256]{3,2,1,0:T(8,128)(2,1)S(1)}, bf16[40,128]{1,0:T(8,128)(2,1)S(1)}, bf16[160,256]{1,0:T(8,128)(2,1)S(1)}) custom-call(bf16[128,256]{1,0:T(8,128)(2,1)S(1)} %shard_map.75.after.own, bf16[128,256]{1,0:T(8,128)(2,1)S(1)} %collective-permute-done.2.twin, ...), custom_call_target="tpu_custom_call" | custom-call | flops 1000000000 | bytes 3000000 | tf_op jit(solution)/shard_map/pallas_call | solution.py:589
  17.1 1.4 %shard_map.80 = (f32[4,5,32,256]{3,2,1,0:T(8,128)S(1)}, bf16[4,1024,256]{2,1,0:T(8,128)(2,1)S(1)}) custom-call(bf16[6,7,32,256]{3,2,1,0:T(8,128)(2,1)S(1)} %get-tuple-element.35.fine_near, bf16[27,16,48]{2,1,0:T(8,128)(2,1)S(1)} %get-tuple-element.36.fine, bf16[2304,256]{1,0:T(8,128)(2,1)S(1)} %shard_map.79.w_fine_skip), custom_call_target="tpu_custom_call" | custom-call | flops 1000000000 | bytes 4000000 | tf_op jit(solution)/shard_map/pallas_call | solution.py:611
  18.5 2.5 %collective-permute-done.3.edge = bf16[176,256]{1,0:T(8,128)(2,1)S(1)} collective-permute-done((bf16[176,256]{1,0:T(8,128)(2,1)S(1)}, bf16[176,256]{1,0:T(8,128)(2,1)S(1)}, u32[]{:S(2)}, u32[]{:S(2)}) %collective-permute-start.3) | collective-permute-done | bytes 90144 | tf_op jit(solution)/shard_map/ppermute | solution.py:587
  21.0 0.9 %shard_map.81 = (bf16[6,3,32,256]{3,2,1,0:T(8,128)(2,1)S(1)}, bf16[4,2,40,128]{3,2,1,0:T(8,128)(2,1)S(1)}, bf16[4,2,40,256]{3,2,1,0:T(8,128)(2,1)S(1)}, bf16[3,2...) custom-call(bf16[128,256]{1,0:T(8,128)(2,1)S(1)} %shard_map.75.after.own, ...), custom_call_target="tpu_custom_call" | custom-call | flops 1000000000 | bytes 3000000 | tf_op jit(solution)/shard_map/pallas_call | solution.py:621
  21.9 0.1 collective-permute-start.4
  22.0 1.6 %shard_map.82 = (bf16[4,2,40,256]{3,2,1,0:T(8,128)(2,1)S(1)}, bf16[3,2,40,128]{3,2,1,0:T(8,128)(2,1)S(1)}, f32[4,8,32,256]{3,2,1,0:T(8,128)S(1)}) custom-call(bf16[176,256]{1,0:T(8,128)(2,1)S(1)} %collective-permute-done.3.edge, bf16[160,256]{1,0:T(8,128)(2,1)S(1)} %get-tuple-element.29.pick, bf16[2,192,256]{2,1,0:T(8,128)(2,1)S(1)} %get-tuple-element.30.w_first, ...), custom_call_target="tpu_custom_call" | custom-call | flops 2000000000 | bytes 3000000 | tf_op jit(solution)/shard_map/pallas_call | solution.py:640
  23.7 0.0 collective-permute-done.4.from_twin
  23.7 3.6 %shard_map.83 = f32[16,8,128]{2,1,0:T(8,128)} custom-call(bf16[200,256]{1,0:T(8,128)(2,1)S(1)} %collective-permute-done.4.from_twin, f32[4,8,32,256]{3,2,1,0:T(8,128)S(1)} %get-tuple-element.41.skip_s, bf16[4,2,40,256]{3,2,1,0:T(8,128)(2,1)S(1)} %get-tuple-element.42.mid_near, bf16[4,2,40,256]{3,2,1,0:T(8,128)(2,1)S(1)} %get-tuple-element.43.mid_far, ...), custom_call_target="tpu_custom_call" | custom-call | flops 6000000000 | bytes 9000000 | tf_op jit(solution)/shard_map/pallas_call | solution.py:657
  (1 shorter events, 0.0 us)
Async XLA Ops:
  0.0 6.5 %collective-permute-start = (bf16[16,8,128]{2,1,0:T(8,128)(2,1)}, bf16[16,8,128]{2,1,0:T(8,128)(2,1)S(1)}, u32[]{:S(2)}, u32[]{:S(2)}) collective-permute-start(bf16[16,8,128]{2,1,0:T(8,128)(2,1)} %own.1), channel_id=1, source_target_pairs={{1,2},{2,1},{3,4},{4,3},{5,6},{6,5},{9,10},{10,9},{11,12},{12,11},... | collective-permute-start | bytes 98312 | tf_op jit(solution)/shard_map/ppermute | solution.py:557
  3.4 3.4 %collective-permute-start.1 = (bf16[16,8,128]{2,1,0:T(8,128)(2,1)}, bf16[16,8,128]{2,1,0:T(8,128)(2,1)S(1)}, u32[]{:S(2)}, u32[]{:S(2)}) collective-permute-start(bf16[16,8,128]{2,1,0:T(8,128)(2,1)} %own.1), channel_id=1, source_target_pairs={{0,1},{1,0},{2,3},{3,2},{4,5},{5,4},{6,7},{7,6},{8,9},{9,8},{10,11... | collective-permute-start | bytes 98312 | tf_op jit(solution)/shard_map/ppermute | solution.py:558
  6.0 0.8 %copy-start = (bf16[16,8,128]{2,1,0:T(8,128)(2,1)S(1)}, bf16[16,8,128]{2,1,0:T(8,128)(2,1)}, u32[]{:S(2)}) copy-start(bf16[16,8,128]{2,1,0:T(8,128)(2,1)} %own.1) | copy-start | bytes 98308
  7.0 3.0 %collective-permute-start.2 = (bf16[128,256]{1,0:T(8,128)(2,1)S(1)}, bf16[128,256]{1,0:T(8,128)(2,1)S(1)}, u32[]{:S(2)}, u32[]{:S(2)}) collective-permute-start(bf16[128,256]{1,0:T(8,128)(2,1)S(1)} %shard_map.75.after.own), channel_id=1, source_target_pairs={{0,8},{8,0},{16,24},{24,16},{32,40},{40,32},{48,56},{56,48},{64,72... | collective-permute-start | bytes 196616 | tf_op jit(solution)/shard_map/ppermute | solution.py:569
  10.0 11.0 %collective-permute-start.3 = (bf16[176,256]{1,0:T(8,128)(2,1)S(1)}, bf16[176,256]{1,0:T(8,128)(2,1)S(1)}, u32[]{:S(2)}, u32[]{:S(2)}) collective-permute-start(bf16[176,256]{1,0:T(8,128)(2,1)S(1)} %shard_map.77.after), channel_id=1, source_target_pairs={{8,16},{16,8},{24,32},{32,24},{40,48},{48,40},{56,64},{64,56},{72,... | collective-permute-start | bytes 270344 | tf_op jit(solution)/shard_map/ppermute | solution.py:587
  21.9 1.8 %collective-permute-start.4 = (bf16[200,256]{1,0:T(8,128)(2,1)S(1)}, bf16[200,256]{1,0:T(8,128)(2,1)S(1)}, u32[]{:S(2)}, u32[]{:S(2)}) collective-permute-start(bf16[200,256]{1,0:T(8,128)(2,1)S(1)} %get-tuple-element.38.after), channel_id=1, source_target_pairs={{0,8},{8,0},{16,24},{24,16},{32,40},{40,32},{48,56},{56,48},{64,72... | collective-permute-start | bytes 307208 | tf_op jit(solution)/shard_map/ppermute | solution.py:639

commit v13 on v12

--- a/solution.py
+++ b/solution.py
@@ -142,8 +142,7 @@
     cell = cell_of(row % J)
     inside = cell_inside("gy", 32, cell)
     pick[...] = ((iota((4 * J, 256), 1) == (4 * cell + row // J + 256) % 256) & inside).astype(BF)
-    for copy in copies[:4]:
-        copy.wait()
+    copies[0].wait()
 
     w_first[...] = jnp.zeros_like(w_first)
     for dx in range(3):
@@ -158,16 +157,19 @@
             for even in range(2):
                 w_first[even, pl.ds(dy * 64 + (even + dx) * 16, 16), :] = block
 
+    copies[1].wait()
     flat = down[...].reshape(27 * 16, 32)
     all_taps = (dot(flat, r32) * (1 / 16)).astype(BF)
     taps = [[all_taps[(dz * 9 + xy) * 16 : (dz * 9 + xy + 1) * 16] for xy in range(9)] for dz in range(3)]
     banded(w_down, taps, 16, list(range(8)), halves(32))
 
+    copies[2].wait()
     flat = coarse[...].reshape(27 * 32, 64)
     all_taps = (dot(flat, r64) * (1 / 16)).astype(BF)
     taps = [[all_taps[(dz * 9 + xy) * 32 : (dz * 9 + xy + 1) * 32] for xy in range(9)] for dz in range(3)]
     banded(w_coarse, taps, 32, list(range(4)), natural(64))
 
+    copies[3].wait()
     row = dot(jnp.broadcast_to(head[...], (16, 16)), r16)
     w_head[...] = jnp.where(iota((16, 256), 1) // 16 == iota((16, 256), 0), row, 0.0).astype(BF)
     for copy in copies[4:]:
@@ -188,7 +190,7 @@
     folded(w_mid_up, lambda dz, dx, dy: tiled[dz * 9 + dx * 3 + dy], 64, 4, natural(32))
 
 
-def fine_weights_kernel(fine, after, w_fine_skip):
+def fine_skip_weights(fine, w_fine_skip):
     r16 = repeat_matrix(16)
     tiled = [(dot_tn(fine[tap], r16)[32:] * 0.5).astype(BF) for tap in range(27)]
     taps = [tiled[dz * 9 : dz * 9 + 9] for dz in range(3)]
@@ -296,9 +298,11 @@
 
 
 def encode_near_kernel(
-    own, twin, pick, w_first, w_down, after, fine, pooled, mid, pool_mid, for_twin
+    own, twin, pick, w_first, w_down, fine_taps, after,
+    fine, pooled, mid, pool_mid, for_twin, w_fine_skip,
 ):
     def work(core):
+        fine_skip_weights(fine_taps, w_fine_skip)
         if core:
             field = jnp.concatenate([twin[80:], own[:112]], axis=0)
         else:
@@ -457,24 +461,24 @@
                 shift = 1 if py else J - 1
                 up_s[0 if py else 3, at] = pltpu.roll(masked, shift, 0)[:32].astype(BF)
 
-    @pl.loop(0, 4)
-    def _(parity):
-        px, py = parity // 2, parity % 2
-        lhs = jnp.concatenate(
-            [
-                up_s[pl.ds(py + ty, 2), pl.ds(px + tx, 4)].reshape(256, 256)
-                for tx in range(2)
-                for ty in range(2)
-            ],
-            axis=1,
-        )
-        up = dot(lhs, w_fine_up[parity]).reshape(2, 4, 32, 256)
-        for half in range(2):
-            group = 2 * half + py
-            for k in range(4):
-                value = silu_half(skip_s[group, 2 * k + px] + up[half, k])
-                row = pl.multiple_of(group * 32, 32)
-                last_s[2 * k + px, pl.ds(row, 32), :] = value.astype(BF)
+    @pl.loop(0, 2)
+    def _(py):
+        for px in range(2):
+            lhs = jnp.concatenate(
+                [
+                    up_s[pl.ds(py + ty, 2), px + tx : px + tx + 4].reshape(256, 256)
+                    for tx in range(2)
+                    for ty in range(2)
+                ],
+                axis=1,
+            )
+            up = dot(lhs, w_fine_up[px * 2 + py]).reshape(2, 4, 32, 256)
+            for half in range(2):
+                group = 2 * half + py
+                for k in range(4):
+                    value = silu_half(skip_s[group, 2 * k + px] + up[half, k])
+                    row = pl.multiple_of(group * 32, 32)
+                    last_s[2 * k + px, pl.ds(row, 32), :] = value.astype(BF)
 
     heads = jnp.concatenate([dot_nt(w_head[...], last_s[x]) for x in range(8)], axis=0)
     high = heads.astype(BF)
@@ -586,7 +590,7 @@
     )(own, twin, w_mid_up)
     chip_edge = lax.ppermute(edge, "gx", between)
 
-    fine_near, pool_near, mid_near, pool_mid_near, for_twin_near = pl.pallas_call(
+    fine_near, pool_near, mid_near, pool_mid_near, for_twin_near, w_fine_skip = pl.pallas_call(
         encode_near_kernel,
         out_shape=(
             shape(6, 7, 32, 256),
@@ -594,20 +598,13 @@
             shape(4, 2, J, 256),
             shape(J, 128),
             shape(4 * J, 256),
+            shape(2304, 256),
         ),
-        in_specs=[VMEM] * 5 + [ANY],
-        out_specs=(VMEM,) * 5,
+        in_specs=[VMEM] * 6 + [ANY],
+        out_specs=(VMEM,) * 6,
         compiler_params=small(16),
         cost_estimate=cost(10**9, 3 * 10**6),
-    )(own, twin, pick, w_first, w_down, edge)
-    w_fine_skip = pl.pallas_call(
-        fine_weights_kernel,
-        out_shape=shape(2304, 256),
-        in_specs=[VMEM, ANY],
-        out_specs=VMEM,
-        compiler_params=small(16),
-        cost_estimate=cost(10**9, 2 * 10**6),
-    )(fine, edge)
+    )(own, twin, pick, w_first, w_down, fine, edge)
     skip_near, w_fine_up = pl.pallas_call(
         skip_near_kernel,
         out_shape=(shape(4, 5, 32, 256, kind=F32), shape(4, 1024, 256)),

time: 27.7 us -> 27.4 us (0.989)
    pallas_call x1 -> x0, Pallas kernels: 0.44 us -> none  [body(): pl.pallas_call(fine_weights_kernel, out_shape=shape(2304, 256), in_specs=...]
    pallas_call x1, Pallas kernels: 1.12 us -> 1.46 us  [body(): pl.pallas_call(encode_near_kernel, out_shape=(shape(6, 7, 32, 256), shape...]
    pallas_call x1, Pallas kernels: 3.56 us -> 3.23 us  [body(): pl.pallas_call(net_kernel, out_shape=shape(16, 8, 128, kind=F32), in_spec...]
  transfers between devices with their start and end apart: 5 -> 5, of which waited for: 2 -> 1; matrix products, arithmetic and copies ran while one was open for 0% -> 0% of each run, Pallas kernels for 29% -> 29%
where the time goes in v13:
time: 27.4 us; the launch traced here: 26.9 us
  Pallas kernels  12.2 us (45%)
  starting transfers between devices  11.9 us (43%)
  waiting for transfers between devices  2.55 us (9%)
    ppermute x1, starting transfers between devices, body(): chip_edge = lax.ppermute(edge, 'gx', between)  5.6 us
    ppermute x1, starting transfers between devices, body(): y_outer = lax.ppermute(noisy_field, 'gy', swap_out)  3.42 us
    pallas_call x1, Pallas kernels, body(): pl.pallas_call(net_kernel, out_shape=shape(16, 8, 128, kind=F32), in_spec...  3.23 us
    ppermute x1, waiting for transfers between devices, body(): chip_edge = lax.ppermute(edge, 'gx', between)  2.5 us
    ppermute x1, starting transfers between devices, body(): twin = lax.ppermute(own, 'gx', in_chip)  1.77 us
    pallas_call x1, Pallas kernels, body(): pl.pallas_call(encoder_weights_kernel, out_shape=(shape(2, 192, 256), sha...  1.68 us
    pallas_call x1, Pallas kernels, body(): pl.pallas_call(encode_outer_kernel, out_shape=(shape(4, 2, J, 256), shape...  1.65 us
    pallas_call x1, Pallas kernels, body(): pl.pallas_call(encode_near_kernel, out_shape=(shape(6, 7, 32, 256), shape...  1.46 us
  transfers between devices with their start and end apart: 5, of which 1 were waited for; matrix products, arithmetic and copies ran while one was open for 0% of the time, Pallas kernels for 29%

profile of v13, /device:TPU:79, one launch (start us, length us, event | category | flops | bytes accessed | tf_op | source)
XLA Modules:
  0.0 26.9 jit_solution(14923791971775090904)
XLA Ops:
  0.0 3.4 %collective-permute-start = (bf16[16,8,128]{2,1,0:T(8,128)(2,1)}, bf16[16,8,128]{2,1,0:T(8,128)(2,1)S(1)}, u32[]{:S(2)}, u32[]{:S(2)}) collective-permute-start(bf16[16,8,128]{2,1,0:T(8,128)(2,1)} %own.1), channel_id=1, source_target_pairs={{1,2},{2,1},{3,4},{4,3},{5,6},{6,5},{9,10},{10,9},{11,12},{12,11},... | collective-permute-start | bytes 98312 | tf_op jit(solution)/shard_map/ppermute | solution.py:561
  3.4 1.0 %collective-permute-start.1 = (bf16[16,8,128]{2,1,0:T(8,128)(2,1)}, bf16[16,8,128]{2,1,0:T(8,128)(2,1)S(1)}, u32[]{:S(2)}, u32[]{:S(2)}) collective-permute-start(bf16[16,8,128]{2,1,0:T(8,128)(2,1)} %own.1), channel_id=1, source_target_pairs={{0,1},{1,0},{2,3},{3,2},{4,5},{5,4},{6,7},{7,6},{8,9},{9,8},{10,11... | collective-permute-start | bytes 98312 | tf_op jit(solution)/shard_map/ppermute | solution.py:562
  4.5 1.7 %shard_map.73 = (bf16[2,192,256]{2,1,0:T(8,128)(2,1)S(1)}, bf16[1152,256]{1,0:T(8,128)(2,1)S(1)}, bf16[1152,256]{1,0:T(8,128)(2,1)S(1)}, bf16[16,256]{1,0:T(8,12...) custom-call(bf16[9,3,16]{2,1,0:T(4,128)(2,1)} %bitcast.20, ...), custom_call_target="tpu_custom_call" | custom-call | flops 1000000000 | bytes 3000000 | tf_op jit(solution)/shard_map/pallas_call | solution.py:510
  6.2 0.0 copy-start
  6.2 0.6 %shard_map.74.also_after.w_mid_skip = bf16[2304,256]{1,0:T(8,128)(2,1)S(1)} custom-call(bf16[27,32,96]{2,1,0:T(8,128)(2,1)S(1)} %get-tuple-element.29.middle), custom_call_target="tpu_custom_call" | custom-call | flops 1000000000 | bytes 2000000 | tf_op jit(solution)/shard_map/pallas_call | solution.py:546
  6.7 0.0 collective-permute-done.outer
  6.7 0.0 collective-permute-done.1.inner
  6.8 0.1 copy-done
  6.9 0.1 shard_map.75.after.own
  7.1 1.8 %collective-permute-start.2 = (bf16[128,256]{1,0:T(8,128)(2,1)S(1)}, bf16[128,256]{1,0:T(8,128)(2,1)S(1)}, u32[]{:S(2)}, u32[]{:S(2)}) collective-permute-start(bf16[128,256]{1,0:T(8,128)(2,1)S(1)} %shard_map.75.after.own), channel_id=1, source_target_pairs={{0,8},{8,0},{16,24},{24,16},{32,40},{40,32},{48,56},{56,48},{64,72... | collective-permute-start | bytes 196616 | tf_op jit(solution)/shard_map/ppermute | solution.py:573
  8.8 1.1 %shard_map.76.after.w_mid_up = bf16[4,1024,256]{2,1,0:T(8,128)(2,1)S(1)} custom-call(bf16[27,32,96]{2,1,0:T(8,128)(2,1)S(1)} %get-tuple-element.29.middle, bf16[128,256]{1,0:T(8,128)(2,1)S(1)} %shard_map.75.after.own), custom_call_target="tpu_custom_call" | custom-call | flops 1000000000 | bytes 4000000 | tf_op jit(solution)/shard_map/pallas_call | solution.py:574
  9.9 0.0 collective-permute-done.2.twin
  10.0 5.6 %collective-permute-start.3 = (bf16[176,256]{1,0:T(8,128)(2,1)S(1)}, bf16[176,256]{1,0:T(8,128)(2,1)S(1)}, u32[]{:S(2)}, u32[]{:S(2)}) collective-permute-start(bf16[176,256]{1,0:T(8,128)(2,1)S(1)} %shard_map.77.after), channel_id=1, source_target_pairs={{8,16},{16,8},{24,32},{32,24},{40,48},{48,40},{56,64},{64,56},{72,... | collective-permute-start | bytes 270344 | tf_op jit(solution)/shard_map/ppermute | solution.py:591
  15.6 1.5 %shard_map.78 = (bf16[6,7,32,256]{3,2,1,0:T(8,128)(2,1)S(1)}, bf16[4,4,40,128]{3,2,1,0:T(8,128)(2,1)S(1)}, bf16[4,2,40,256]{3,2,1,0:T(8,128)(2,1)S(1)}, bf16[40,...) custom-call(bf16[128,256]{1,0:T(8,128)(2,1)S(1)} %shard_map.75.after.own, ...), custom_call_target="tpu_custom_call" | custom-call | flops 1000000000 | bytes 3000000 | tf_op jit(solution)/shard_map/pallas_call | solution.py:593
  17.1 1.4 %shard_map.79 = (f32[4,5,32,256]{3,2,1,0:T(8,128)S(1)}, bf16[4,1024,256]{2,1,0:T(8,128)(2,1)S(1)}) custom-call(bf16[6,7,32,256]{3,2,1,0:T(8,128)(2,1)S(1)} %get-tuple-element.37.fine_near, bf16[27,16,48]{2,1,0:T(8,128)(2,1)S(1)} %get-tuple-element.33.fine_taps.fine, bf16[2304,256]{1,0:T(8,128)(2,1)S(1)} %get-tuple-element.38.w_fine_skip), custom_call_target="tpu_custom_call" | custom-call | flops 1000000000 | bytes 4000000 | tf_op jit(solution)/shard_map/pallas_call | solution.py:608
  18.5 2.5 %collective-permute-done.3.edge = bf16[176,256]{1,0:T(8,128)(2,1)S(1)} collective-permute-done((bf16[176,256]{1,0:T(8,128)(2,1)S(1)}, bf16[176,256]{1,0:T(8,128)(2,1)S(1)}, u32[]{:S(2)}, u32[]{:S(2)}) %collective-permute-start.3) | collective-permute-done | bytes 90144 | tf_op jit(solution)/shard_map/ppermute | solution.py:591
  21.0 0.9 %shard_map.80 = (bf16[6,3,32,256]{3,2,1,0:T(8,128)(2,1)S(1)}, bf16[4,2,40,128]{3,2,1,0:T(8,128)(2,1)S(1)}, bf16[4,2,40,256]{3,2,1,0:T(8,128)(2,1)S(1)}, bf16[3,2...) custom-call(bf16[128,256]{1,0:T(8,128)(2,1)S(1)} %shard_map.75.after.own, ...), custom_call_target="tpu_custom_call" | custom-call | flops 1000000000 | bytes 3000000 | tf_op jit(solution)/shard_map/pallas_call | solution.py:618
  21.9 0.1 collective-permute-start.4
  22.0 1.6 %shard_map.81 = (bf16[4,2,40,256]{3,2,1,0:T(8,128)(2,1)S(1)}, bf16[3,2,40,128]{3,2,1,0:T(8,128)(2,1)S(1)}, f32[4,8,32,256]{3,2,1,0:T(8,128)S(1)}) custom-call(bf16[176,256]{1,0:T(8,128)(2,1)S(1)} %collective-permute-done.3.edge, bf16[160,256]{1,0:T(8,128)(2,1)S(1)} %get-tuple-element.30.pick, bf16[2,192,256]{2,1,0:T(8,128)(2,1)S(1)} %get-tuple-element.31.w_first, ...), custom_call_target="tpu_custom_call" | custom-call | flops 2000000000 | bytes 3000000 | tf_op jit(solution)/shard_map/pallas_call | solution.py:637
  23.7 0.0 collective-permute-done.4.from_twin
  23.7 3.2 %shard_map.82 = f32[16,8,128]{2,1,0:T(8,128)} custom-call(bf16[200,256]{1,0:T(8,128)(2,1)S(1)} %collective-permute-done.4.from_twin, f32[4,8,32,256]{3,2,1,0:T(8,128)S(1)} %get-tuple-element.43.skip_s, bf16[4,2,40,256]{3,2,1,0:T(8,128)(2,1)S(1)} %get-tuple-element.44.mid_near, bf16[4,2,40,256]{3,2,1,0:T(8,128)(2,1)S(1)} %get-tuple-element.45.mid_far, ...), custom_call_target="tpu_custom_call" | custom-call | flops 6000000000 | bytes 9000000 | tf_op jit(solution)/shard_map/pallas_call | solution.py:654
  (1 shorter events, 0.0 us)
Async XLA Ops:
  0.0 6.7 %collective-permute-start = (bf16[16,8,128]{2,1,0:T(8,128)(2,1)}, bf16[16,8,128]{2,1,0:T(8,128)(2,1)S(1)}, u32[]{:S(2)}, u32[]{:S(2)}) collective-permute-start(bf16[16,8,128]{2,1,0:T(8,128)(2,1)} %own.1), channel_id=1, source_target_pairs={{1,2},{2,1},{3,4},{4,3},{5,6},{6,5},{9,10},{10,9},{11,12},{12,11},... | collective-permute-start | bytes 98312 | tf_op jit(solution)/shard_map/ppermute | solution.py:561
  3.4 3.4 %collective-permute-start.1 = (bf16[16,8,128]{2,1,0:T(8,128)(2,1)}, bf16[16,8,128]{2,1,0:T(8,128)(2,1)S(1)}, u32[]{:S(2)}, u32[]{:S(2)}) collective-permute-start(bf16[16,8,128]{2,1,0:T(8,128)(2,1)} %own.1), channel_id=1, source_target_pairs={{0,1},{1,0},{2,3},{3,2},{4,5},{5,4},{6,7},{7,6},{8,9},{9,8},{10,11... | collective-permute-start | bytes 98312 | tf_op jit(solution)/shard_map/ppermute | solution.py:562
  6.2 0.8 %copy-start = (bf16[16,8,128]{2,1,0:T(8,128)(2,1)S(1)}, bf16[16,8,128]{2,1,0:T(8,128)(2,1)}, u32[]{:S(2)}) copy-start(bf16[16,8,128]{2,1,0:T(8,128)(2,1)} %own.1) | copy-start | bytes 98308
  7.1 2.9 %collective-permute-start.2 = (bf16[128,256]{1,0:T(8,128)(2,1)S(1)}, bf16[128,256]{1,0:T(8,128)(2,1)S(1)}, u32[]{:S(2)}, u32[]{:S(2)}) collective-permute-start(bf16[128,256]{1,0:T(8,128)(2,1)S(1)} %shard_map.75.after.own), channel_id=1, source_target_pairs={{0,8},{8,0},{16,24},{24,16},{32,40},{40,32},{48,56},{56,48},{64,72... | collective-permute-start | bytes 196616 | tf_op jit(solution)/shard_map/ppermute | solution.py:573
  10.0 11.0 %collective-permute-start.3 = (bf16[176,256]{1,0:T(8,128)(2,1)S(1)}, bf16[176,256]{1,0:T(8,128)(2,1)S(1)}, u32[]{:S(2)}, u32[]{:S(2)}) collective-permute-start(bf16[176,256]{1,0:T(8,128)(2,1)S(1)} %shard_map.77.after), channel_id=1, source_target_pairs={{8,16},{16,8},{24,32},{32,24},{40,48},{48,40},{56,64},{64,56},{72,... | collective-permute-start | bytes 270344 | tf_op jit(solution)/shard_map/ppermute | solution.py:591
  21.9 1.8 %collective-permute-start.4 = (bf16[200,256]{1,0:T(8,128)(2,1)S(1)}, bf16[200,256]{1,0:T(8,128)(2,1)S(1)}, u32[]{:S(2)}, u32[]{:S(2)}) collective-permute-start(bf16[200,256]{1,0:T(8,128)(2,1)S(1)} %get-tuple-element.40.after), channel_id=1, source_target_pairs={{0,8},{8,0},{16,24},{24,16},{32,40},{40,32},{48,56},{56,48},{64,72... | collective-permute-start | bytes 307208 | tf_op jit(solution)/shard_map/ppermute | solution.py:636

commit v14 on v13

--- a/solution.py
+++ b/solution.py
@@ -142,7 +142,8 @@
     cell = cell_of(row % J)
     inside = cell_inside("gy", 32, cell)
     pick[...] = ((iota((4 * J, 256), 1) == (4 * cell + row // J + 256) % 256) & inside).astype(BF)
-    copies[0].wait()
+    for copy in copies[:4]:
+        copy.wait()
 
     w_first[...] = jnp.zeros_like(w_first)
     for dx in range(3):
@@ -157,19 +158,16 @@
             for even in range(2):
                 w_first[even, pl.ds(dy * 64 + (even + dx) * 16, 16), :] = block
 
-    copies[1].wait()
     flat = down[...].reshape(27 * 16, 32)
     all_taps = (dot(flat, r32) * (1 / 16)).astype(BF)
     taps = [[all_taps[(dz * 9 + xy) * 16 : (dz * 9 + xy + 1) * 16] for xy in range(9)] for dz in range(3)]
     banded(w_down, taps, 16, list(range(8)), halves(32))
 
-    copies[2].wait()
     flat = coarse[...].reshape(27 * 32, 64)
     all_taps = (dot(flat, r64) * (1 / 16)).astype(BF)
     taps = [[all_taps[(dz * 9 + xy) * 32 : (dz * 9 + xy + 1) * 32] for xy in range(9)] for dz in range(3)]
     banded(w_coarse, taps, 32, list(range(4)), natural(64))
 
-    copies[3].wait()
     row = dot(jnp.broadcast_to(head[...], (16, 16)), r16)
     w_head[...] = jnp.where(iota((16, 256), 1) // 16 == iota((16, 256), 0), row, 0.0).astype(BF)
     for copy in copies[4:]:
@@ -178,7 +176,7 @@
 
 def mid_skip_weights_kernel(middle, w_mid_skip):
     r32 = repeat_matrix(32)
-    tiled = [(dot_tn(middle[tap], r32)[64:] * 0.5).astype(BF) for tap in range(27)]
+    tiled = [(dot_tn(middle[tap, :, 64:96], r32) * 0.5).astype(BF) for tap in range(27)]
     taps = [tiled[dz * 9 : dz * 9 + 9] for dz in range(3)]
     banded(w_mid_skip, taps, 32, [0, 2, 4, 6, 1, 3, 5, 7], natural(32))
 
@@ -186,13 +184,13 @@
 def mid_up_weights_kernel(middle, after, w_mid_up, tiled):
     r32 = repeat_matrix(32)
     for tap in range(27):
-        tiled[tap] = dot_tn(middle[tap], r32)[:64] * 0.5
+        tiled[tap] = dot_tn(middle[tap, :, 0:64], r32) * 0.5
     folded(w_mid_up, lambda dz, dx, dy: tiled[dz * 9 + dx * 3 + dy], 64, 4, natural(32))
 
 
 def fine_skip_weights(fine, w_fine_skip):
     r16 = repeat_matrix(16)
-    tiled = [(dot_tn(fine[tap], r16)[32:] * 0.5).astype(BF) for tap in range(27)]
+    tiled = [(dot_tn(fine[tap, :, 32:48], r16) * 0.5).astype(BF) for tap in range(27)]
     taps = [tiled[dz * 9 : dz * 9 + 9] for dz in range(3)]
     banded(w_fine_skip, taps, 16, list(range(0, 16, 2)) + list(range(1, 16, 2)), natural(16))
 
@@ -331,7 +329,7 @@
     out[...] = dot(lhs, w_fine_skip[...]).reshape(4, 5, 32, 256)
     r16 = repeat_matrix(16)
     for tap in range(27):
-        tiled[tap] = dot_tn(fine[tap], r16)[:32] * 0.5
+        tiled[tap] = dot_tn(fine[tap, :, 0:32], r16) * 0.5
     folded(w_fine_up, lambda dz, dx, dy: tiled[dz * 9 + dx * 3 + dy], 32, 8, natural(16))
 
 

time: 27.4 us -> 27.4 us (level)
  Pallas kernels: 12.2 us -> 11.9 us
  transfers between devices with their start and end apart: 5 -> 5, of which waited for: 1 -> 2; matrix products, arithmetic and copies ran while one was open for 0% -> 0% of each run, Pallas kernels for 29% -> 28%
where the time goes in v14:
time: 27.4 us; the launch traced here: 26.9 us
  starting transfers between devices  12 us (44%)
  Pallas kernels  11.9 us (43%)
  waiting for transfers between devices  2.82 us (10%)
    ppermute x1, starting transfers between devices, body(): chip_edge = lax.ppermute(edge, 'gx', between)  5.54 us
    ppermute x1, starting transfers between devices, body(): y_outer = lax.ppermute(noisy_field, 'gy', swap_out)  3.42 us
    pallas_call x1, Pallas kernels, body(): pl.pallas_call(net_kernel, out_shape=shape(16, 8, 128, kind=F32), in_spec...  3.23 us
    ppermute x1, waiting for transfers between devices, body(): chip_edge = lax.ppermute(edge, 'gx', between)  2.6 us
    ppermute x1, starting transfers between devices, body(): twin = lax.ppermute(own, 'gx', in_chip)  1.9 us
    pallas_call x1, Pallas kernels, body(): pl.pallas_call(encode_outer_kernel, out_shape=(shape(4, 2, J, 256), shape...  1.65 us
    pallas_call x1, Pallas kernels, body(): pl.pallas_call(encoder_weights_kernel, out_shape=(shape(2, 192, 256), sha...  1.49 us
    pallas_call x1, Pallas kernels, body(): pl.pallas_call(encode_near_kernel, out_shape=(shape(6, 7, 32, 256), shape...  1.46 us
  transfers between devices with their start and end apart: 5, of which 2 were waited for; matrix products, arithmetic and copies ran while one was open for 0% of the time, Pallas kernels for 28%

profile of v14, /device:TPU:79, one launch (start us, length us, event | category | flops | bytes accessed | tf_op | source)
XLA Modules:
  0.0 26.9 jit_solution(678185761467035564)
XLA Ops:
  0.0 3.4 %collective-permute-start = (bf16[16,8,128]{2,1,0:T(8,128)(2,1)}, bf16[16,8,128]{2,1,0:T(8,128)(2,1)S(1)}, u32[]{:S(2)}, u32[]{:S(2)}) collective-permute-start(bf16[16,8,128]{2,1,0:T(8,128)(2,1)} %own.1), channel_id=1, source_target_pairs={{1,2},{2,1},{3,4},{4,3},{5,6},{6,5},{9,10},{10,9},{11,12},{12,11},... | collective-permute-start | bytes 98312 | tf_op jit(solution)/shard_map/ppermute | solution.py:559
  3.4 1.0 %collective-permute-start.1 = (bf16[16,8,128]{2,1,0:T(8,128)(2,1)}, bf16[16,8,128]{2,1,0:T(8,128)(2,1)S(1)}, u32[]{:S(2)}, u32[]{:S(2)}) collective-permute-start(bf16[16,8,128]{2,1,0:T(8,128)(2,1)} %own.1), channel_id=1, source_target_pairs={{0,1},{1,0},{2,3},{3,2},{4,5},{5,4},{6,7},{7,6},{8,9},{9,8},{10,11... | collective-permute-start | bytes 98312 | tf_op jit(solution)/shard_map/ppermute | solution.py:560
  4.5 1.5 %shard_map.73 = (bf16[2,192,256]{2,1,0:T(8,128)(2,1)S(1)}, bf16[1152,256]{1,0:T(8,128)(2,1)S(1)}, bf16[1152,256]{1,0:T(8,128)(2,1)S(1)}, bf16[16,256]{1,0:T(8,12...) custom-call(bf16[9,3,16]{2,1,0:T(4,128)(2,1)} %bitcast.20, ...), custom_call_target="tpu_custom_call" | custom-call | flops 1000000000 | bytes 3000000 | tf_op jit(solution)/shard_map/pallas_call | solution.py:508
  6.0 0.0 copy-start
  6.0 0.6 %shard_map.74.also_after.w_mid_skip = bf16[2304,256]{1,0:T(8,128)(2,1)S(1)} custom-call(bf16[27,32,96]{2,1,0:T(8,128)(2,1)S(1)} %get-tuple-element.29.middle), custom_call_target="tpu_custom_call" | custom-call | flops 1000000000 | bytes 2000000 | tf_op jit(solution)/shard_map/pallas_call | solution.py:544
  6.6 0.0 collective-permute-done.outer
  6.6 0.2 collective-permute-done.1.inner
  6.8 0.0 copy-done
  6.8 0.2 shard_map.75.after.own
  7.0 1.9 %collective-permute-start.2 = (bf16[128,256]{1,0:T(8,128)(2,1)S(1)}, bf16[128,256]{1,0:T(8,128)(2,1)S(1)}, u32[]{:S(2)}, u32[]{:S(2)}) collective-permute-start(bf16[128,256]{1,0:T(8,128)(2,1)S(1)} %shard_map.75.after.own), channel_id=1, source_target_pairs={{0,8},{8,0},{16,24},{24,16},{32,40},{40,32},{48,56},{56,48},{64,72... | collective-permute-start | bytes 196616 | tf_op jit(solution)/shard_map/ppermute | solution.py:571
  8.8 1.0 %shard_map.76.after.w_mid_up = bf16[4,1024,256]{2,1,0:T(8,128)(2,1)S(1)} custom-call(bf16[27,32,96]{2,1,0:T(8,128)(2,1)S(1)} %get-tuple-element.29.middle, bf16[128,256]{1,0:T(8,128)(2,1)S(1)} %shard_map.75.after.own), custom_call_target="tpu_custom_call" | custom-call | flops 1000000000 | bytes 4000000 | tf_op jit(solution)/shard_map/pallas_call | solution.py:572
  9.9 0.0 collective-permute-done.2.twin
  9.9 5.5 %collective-permute-start.3 = (bf16[176,256]{1,0:T(8,128)(2,1)S(1)}, bf16[176,256]{1,0:T(8,128)(2,1)S(1)}, u32[]{:S(2)}, u32[]{:S(2)}) collective-permute-start(bf16[176,256]{1,0:T(8,128)(2,1)S(1)} %shard_map.77.after), channel_id=1, source_target_pairs={{8,16},{16,8},{24,32},{32,24},{40,48},{48,40},{56,64},{64,56},{72,... | collective-permute-start | bytes 270344 | tf_op jit(solution)/shard_map/ppermute | solution.py:589
  15.5 1.5 %shard_map.78 = (bf16[6,7,32,256]{3,2,1,0:T(8,128)(2,1)S(1)}, bf16[4,4,40,128]{3,2,1,0:T(8,128)(2,1)S(1)}, bf16[4,2,40,256]{3,2,1,0:T(8,128)(2,1)S(1)}, bf16[40,...) custom-call(bf16[128,256]{1,0:T(8,128)(2,1)S(1)} %shard_map.75.after.own, ...), custom_call_target="tpu_custom_call" | custom-call | flops 1000000000 | bytes 3000000 | tf_op jit(solution)/shard_map/pallas_call | solution.py:591
  17.0 1.4 %shard_map.79 = (f32[4,5,32,256]{3,2,1,0:T(8,128)S(1)}, bf16[4,1024,256]{2,1,0:T(8,128)(2,1)S(1)}) custom-call(bf16[6,7,32,256]{3,2,1,0:T(8,128)(2,1)S(1)} %get-tuple-element.37.fine_near, bf16[27,16,48]{2,1,0:T(8,128)(2,1)S(1)} %get-tuple-element.33.fine_taps.fine, bf16[2304,256]{1,0:T(8,128)(2,1)S(1)} %get-tuple-element.38.w_fine_skip), custom_call_target="tpu_custom_call" | custom-call | flops 1000000000 | bytes 4000000 | tf_op jit(solution)/shard_map/pallas_call | solution.py:606
  18.4 2.6 %collective-permute-done.3.edge = bf16[176,256]{1,0:T(8,128)(2,1)S(1)} collective-permute-done((bf16[176,256]{1,0:T(8,128)(2,1)S(1)}, bf16[176,256]{1,0:T(8,128)(2,1)S(1)}, u32[]{:S(2)}, u32[]{:S(2)}) %collective-permute-start.3) | collective-permute-done | bytes 90144 | tf_op jit(solution)/shard_map/ppermute | solution.py:589
  21.0 0.9 %shard_map.80 = (bf16[6,3,32,256]{3,2,1,0:T(8,128)(2,1)S(1)}, bf16[4,2,40,128]{3,2,1,0:T(8,128)(2,1)S(1)}, bf16[4,2,40,256]{3,2,1,0:T(8,128)(2,1)S(1)}, bf16[3,2...) custom-call(bf16[128,256]{1,0:T(8,128)(2,1)S(1)} %shard_map.75.after.own, ...), custom_call_target="tpu_custom_call" | custom-call | flops 1000000000 | bytes 3000000 | tf_op jit(solution)/shard_map/pallas_call | solution.py:616
  21.9 0.1 collective-permute-start.4
  22.0 1.6 %shard_map.81 = (bf16[4,2,40,256]{3,2,1,0:T(8,128)(2,1)S(1)}, bf16[3,2,40,128]{3,2,1,0:T(8,128)(2,1)S(1)}, f32[4,8,32,256]{3,2,1,0:T(8,128)S(1)}) custom-call(bf16[176,256]{1,0:T(8,128)(2,1)S(1)} %collective-permute-done.3.edge, bf16[160,256]{1,0:T(8,128)(2,1)S(1)} %get-tuple-element.30.pick, bf16[2,192,256]{2,1,0:T(8,128)(2,1)S(1)} %get-tuple-element.31.w_first, ...), custom_call_target="tpu_custom_call" | custom-call | flops 2000000000 | bytes 3000000 | tf_op jit(solution)/shard_map/pallas_call | solution.py:635
  23.6 0.0 collective-permute-done.4.from_twin
  23.6 3.2 %shard_map.82 = f32[16,8,128]{2,1,0:T(8,128)} custom-call(bf16[200,256]{1,0:T(8,128)(2,1)S(1)} %collective-permute-done.4.from_twin, f32[4,8,32,256]{3,2,1,0:T(8,128)S(1)} %get-tuple-element.43.skip_s, bf16[4,2,40,256]{3,2,1,0:T(8,128)(2,1)S(1)} %get-tuple-element.44.mid_near, bf16[4,2,40,256]{3,2,1,0:T(8,128)(2,1)S(1)} %get-tuple-element.45.mid_far, ...), custom_call_target="tpu_custom_call" | custom-call | flops 6000000000 | bytes 9000000 | tf_op jit(solution)/shard_map/pallas_call | solution.py:652
  (1 shorter events, 0.0 us)
Async XLA Ops:
  0.0 6.6 %collective-permute-start = (bf16[16,8,128]{2,1,0:T(8,128)(2,1)}, bf16[16,8,128]{2,1,0:T(8,128)(2,1)S(1)}, u32[]{:S(2)}, u32[]{:S(2)}) collective-permute-start(bf16[16,8,128]{2,1,0:T(8,128)(2,1)} %own.1), channel_id=1, source_target_pairs={{1,2},{2,1},{3,4},{4,3},{5,6},{6,5},{9,10},{10,9},{11,12},{12,11},... | collective-permute-start | bytes 98312 | tf_op jit(solution)/shard_map/ppermute | solution.py:559
  3.4 3.4 %collective-permute-start.1 = (bf16[16,8,128]{2,1,0:T(8,128)(2,1)}, bf16[16,8,128]{2,1,0:T(8,128)(2,1)S(1)}, u32[]{:S(2)}, u32[]{:S(2)}) collective-permute-start(bf16[16,8,128]{2,1,0:T(8,128)(2,1)} %own.1), channel_id=1, source_target_pairs={{0,1},{1,0},{2,3},{3,2},{4,5},{5,4},{6,7},{7,6},{8,9},{9,8},{10,11... | collective-permute-start | bytes 98312 | tf_op jit(solution)/shard_map/ppermute | solution.py:560
  6.0 0.8 %copy-start = (bf16[16,8,128]{2,1,0:T(8,128)(2,1)S(1)}, bf16[16,8,128]{2,1,0:T(8,128)(2,1)}, u32[]{:S(2)}) copy-start(bf16[16,8,128]{2,1,0:T(8,128)(2,1)} %own.1) | copy-start | bytes 98308
  7.0 3.0 %collective-permute-start.2 = (bf16[128,256]{1,0:T(8,128)(2,1)S(1)}, bf16[128,256]{1,0:T(8,128)(2,1)S(1)}, u32[]{:S(2)}, u32[]{:S(2)}) collective-permute-start(bf16[128,256]{1,0:T(8,128)(2,1)S(1)} %shard_map.75.after.own), channel_id=1, source_target_pairs={{0,8},{8,0},{16,24},{24,16},{32,40},{40,32},{48,56},{56,48},{64,72... | collective-permute-start | bytes 196616 | tf_op jit(solution)/shard_map/ppermute | solution.py:571
  9.9 11.0 %collective-permute-start.3 = (bf16[176,256]{1,0:T(8,128)(2,1)S(1)}, bf16[176,256]{1,0:T(8,128)(2,1)S(1)}, u32[]{:S(2)}, u32[]{:S(2)}) collective-permute-start(bf16[176,256]{1,0:T(8,128)(2,1)S(1)} %shard_map.77.after), channel_id=1, source_target_pairs={{8,16},{16,8},{24,32},{32,24},{40,48},{48,40},{56,64},{64,56},{72,... | collective-permute-start | bytes 270344 | tf_op jit(solution)/shard_map/ppermute | solution.py:589
  21.9 1.8 %collective-permute-start.4 = (bf16[200,256]{1,0:T(8,128)(2,1)S(1)}, bf16[200,256]{1,0:T(8,128)(2,1)S(1)}, u32[]{:S(2)}, u32[]{:S(2)}) collective-permute-start(bf16[200,256]{1,0:T(8,128)(2,1)S(1)} %get-tuple-element.40.after), channel_id=1, source_target_pairs={{0,8},{8,0},{16,24},{24,16},{32,40},{40,32},{48,56},{56,48},{64,72... | collective-permute-start | bytes 307208 | tf_op jit(solution)/shard_map/ppermute | solution.py:634

commit v15 on v14

--- a/solution.py
+++ b/solution.py
@@ -375,6 +375,11 @@
         pairs = range(5, 9) if core else range(-5, -1)
         pool_s[:, far : far + 2] = pool_far[...]
         encode(field, pick, w_first, pairs, None, 0, pool_s, outer)
+        rows, pooled = middle_rows(pool_s, w_down, 4 if core else -4, 4)
+        for at in range(2):
+            put_three(pool_mid, at, pooled[at])
+            for py in range(2):
+                put_shifts(mid, at, py, rows[py][at if core else at + 2])
         lhs = jnp.concatenate(
             [
                 fine_s[dy : dy + 4, dx : dx + 3].reshape(384, 256)
@@ -386,11 +391,6 @@
         near, rest = (0, 5) if core else (3, 0)
         skip[:, rest : rest + 3] = dot(lhs, w_fine_skip[...]).reshape(4, 3, 32, 256)
         skip[:, near : near + 5] = skip_near[...]
-        rows, pooled = middle_rows(pool_s, w_down, 4 if core else -4, 4)
-        for at in range(2):
-            put_three(pool_mid, at, pooled[at])
-            for py in range(2):
-                put_shifts(mid, at, py, rows[py][at if core else at + 2])
 
     for_each_core(work)
 

time: 27.4 us -> 27.4 us (level)
  no operation moved by 1% of the time
where the time goes in v15:
time: 27.4 us; the launch traced here: 26.9 us
  starting transfers between devices  12 us (44%)
  Pallas kernels  11.9 us (43%)
  waiting for transfers between devices  2.82 us (10%)
    ppermute x1, starting transfers between devices, body(): chip_edge = lax.ppermute(edge, 'gx', between)  5.54 us
    ppermute x1, starting transfers between devices, body(): y_outer = lax.ppermute(noisy_field, 'gy', swap_out)  3.42 us
    pallas_call x1, Pallas kernels, body(): pl.pallas_call(net_kernel, out_shape=shape(16, 8, 128, kind=F32), in_spec...  3.23 us
    ppermute x1, waiting for transfers between devices, body(): chip_edge = lax.ppermute(edge, 'gx', between)  2.6 us
    ppermute x1, starting transfers between devices, body(): twin = lax.ppermute(own, 'gx', in_chip)  1.9 us
    pallas_call x1, Pallas kernels, body(): pl.pallas_call(encode_outer_kernel, out_shape=(shape(4, 2, J, 256), shape...  1.62 us
    pallas_call x1, Pallas kernels, body(): pl.pallas_call(encoder_weights_kernel, out_shape=(shape(2, 192, 256), sha...  1.49 us
    pallas_call x1, Pallas kernels, body(): pl.pallas_call(encode_near_kernel, out_shape=(shape(6, 7, 32, 256), shape...  1.46 us
  transfers between devices with their start and end apart: 5, of which 2 were waited for; matrix products, arithmetic and copies ran while one was open for 0% of the time, Pallas kernels for 28%

profile of v15, /device:TPU:79, one launch (start us, length us, event | category | flops | bytes accessed | tf_op | source)
XLA Modules:
  0.0 26.9 jit_solution(1136658875199791306)
XLA Ops:
  0.0 3.4 %collective-permute-start = (bf16[16,8,128]{2,1,0:T(8,128)(2,1)}, bf16[16,8,128]{2,1,0:T(8,128)(2,1)S(1)}, u32[]{:S(2)}, u32[]{:S(2)}) collective-permute-start(bf16[16,8,128]{2,1,0:T(8,128)(2,1)} %own.1), channel_id=1, source_target_pairs={{1,2},{2,1},{3,4},{4,3},{5,6},{6,5},{9,10},{10,9},{11,12},{12,11},... | collective-permute-start | bytes 98312 | tf_op jit(solution)/shard_map/ppermute | solution.py:559
  3.4 1.0 %collective-permute-start.1 = (bf16[16,8,128]{2,1,0:T(8,128)(2,1)}, bf16[16,8,128]{2,1,0:T(8,128)(2,1)S(1)}, u32[]{:S(2)}, u32[]{:S(2)}) collective-permute-start(bf16[16,8,128]{2,1,0:T(8,128)(2,1)} %own.1), channel_id=1, source_target_pairs={{0,1},{1,0},{2,3},{3,2},{4,5},{5,4},{6,7},{7,6},{8,9},{9,8},{10,11... | collective-permute-start | bytes 98312 | tf_op jit(solution)/shard_map/ppermute | solution.py:560
  4.5 1.5 %shard_map.73 = (bf16[2,192,256]{2,1,0:T(8,128)(2,1)S(1)}, bf16[1152,256]{1,0:T(8,128)(2,1)S(1)}, bf16[1152,256]{1,0:T(8,128)(2,1)S(1)}, bf16[16,256]{1,0:T(8,12...) custom-call(bf16[9,3,16]{2,1,0:T(4,128)(2,1)} %bitcast.20, ...), custom_call_target="tpu_custom_call" | custom-call | flops 1000000000 | bytes 3000000 | tf_op jit(solution)/shard_map/pallas_call | solution.py:508
  6.0 0.0 copy-start
  6.0 0.6 %shard_map.74.also_after.w_mid_skip = bf16[2304,256]{1,0:T(8,128)(2,1)S(1)} custom-call(bf16[27,32,96]{2,1,0:T(8,128)(2,1)S(1)} %get-tuple-element.29.middle), custom_call_target="tpu_custom_call" | custom-call | flops 1000000000 | bytes 2000000 | tf_op jit(solution)/shard_map/pallas_call | solution.py:544
  6.6 0.0 collective-permute-done.outer
  6.6 0.2 collective-permute-done.1.inner
  6.8 0.0 copy-done
  6.8 0.2 shard_map.75.after.own
  7.0 1.9 %collective-permute-start.2 = (bf16[128,256]{1,0:T(8,128)(2,1)S(1)}, bf16[128,256]{1,0:T(8,128)(2,1)S(1)}, u32[]{:S(2)}, u32[]{:S(2)}) collective-permute-start(bf16[128,256]{1,0:T(8,128)(2,1)S(1)} %shard_map.75.after.own), channel_id=1, source_target_pairs={{0,8},{8,0},{16,24},{24,16},{32,40},{40,32},{48,56},{56,48},{64,72... | collective-permute-start | bytes 196616 | tf_op jit(solution)/shard_map/ppermute | solution.py:571
  8.8 1.0 %shard_map.76.after.w_mid_up = bf16[4,1024,256]{2,1,0:T(8,128)(2,1)S(1)} custom-call(bf16[27,32,96]{2,1,0:T(8,128)(2,1)S(1)} %get-tuple-element.29.middle, bf16[128,256]{1,0:T(8,128)(2,1)S(1)} %shard_map.75.after.own), custom_call_target="tpu_custom_call" | custom-call | flops 1000000000 | bytes 4000000 | tf_op jit(solution)/shard_map/pallas_call | solution.py:572
  9.9 0.0 collective-permute-done.2.twin
  9.9 5.5 %collective-permute-start.3 = (bf16[176,256]{1,0:T(8,128)(2,1)S(1)}, bf16[176,256]{1,0:T(8,128)(2,1)S(1)}, u32[]{:S(2)}, u32[]{:S(2)}) collective-permute-start(bf16[176,256]{1,0:T(8,128)(2,1)S(1)} %shard_map.77.after), channel_id=1, source_target_pairs={{8,16},{16,8},{24,32},{32,24},{40,48},{48,40},{56,64},{64,56},{72,... | collective-permute-start | bytes 270344 | tf_op jit(solution)/shard_map/ppermute | solution.py:589
  15.5 1.5 %shard_map.78 = (bf16[6,7,32,256]{3,2,1,0:T(8,128)(2,1)S(1)}, bf16[4,4,40,128]{3,2,1,0:T(8,128)(2,1)S(1)}, bf16[4,2,40,256]{3,2,1,0:T(8,128)(2,1)S(1)}, bf16[40,...) custom-call(bf16[128,256]{1,0:T(8,128)(2,1)S(1)} %shard_map.75.after.own, ...), custom_call_target="tpu_custom_call" | custom-call | flops 1000000000 | bytes 3000000 | tf_op jit(solution)/shard_map/pallas_call | solution.py:591
  17.0 1.4 %shard_map.79 = (f32[4,5,32,256]{3,2,1,0:T(8,128)S(1)}, bf16[4,1024,256]{2,1,0:T(8,128)(2,1)S(1)}) custom-call(bf16[6,7,32,256]{3,2,1,0:T(8,128)(2,1)S(1)} %get-tuple-element.37.fine_near, bf16[27,16,48]{2,1,0:T(8,128)(2,1)S(1)} %get-tuple-element.33.fine_taps.fine, bf16[2304,256]{1,0:T(8,128)(2,1)S(1)} %get-tuple-element.38.w_fine_skip), custom_call_target="tpu_custom_call" | custom-call | flops 1000000000 | bytes 4000000 | tf_op jit(solution)/shard_map/pallas_call | solution.py:606
  18.4 2.6 %collective-permute-done.3.edge = bf16[176,256]{1,0:T(8,128)(2,1)S(1)} collective-permute-done((bf16[176,256]{1,0:T(8,128)(2,1)S(1)}, bf16[176,256]{1,0:T(8,128)(2,1)S(1)}, u32[]{:S(2)}, u32[]{:S(2)}) %collective-permute-start.3) | collective-permute-done | bytes 90144 | tf_op jit(solution)/shard_map/ppermute | solution.py:589
  21.0 0.9 %shard_map.80 = (bf16[6,3,32,256]{3,2,1,0:T(8,128)(2,1)S(1)}, bf16[4,2,40,128]{3,2,1,0:T(8,128)(2,1)S(1)}, bf16[4,2,40,256]{3,2,1,0:T(8,128)(2,1)S(1)}, bf16[3,2...) custom-call(bf16[128,256]{1,0:T(8,128)(2,1)S(1)} %shard_map.75.after.own, ...), custom_call_target="tpu_custom_call" | custom-call | flops 1000000000 | bytes 3000000 | tf_op jit(solution)/shard_map/pallas_call | solution.py:616
  21.9 0.1 collective-permute-start.4
  22.0 1.6 %shard_map.81 = (bf16[4,2,40,256]{3,2,1,0:T(8,128)(2,1)S(1)}, bf16[3,2,40,128]{3,2,1,0:T(8,128)(2,1)S(1)}, f32[4,8,32,256]{3,2,1,0:T(8,128)S(1)}) custom-call(bf16[176,256]{1,0:T(8,128)(2,1)S(1)} %collective-permute-done.3.edge, bf16[160,256]{1,0:T(8,128)(2,1)S(1)} %get-tuple-element.30.pick, bf16[2,192,256]{2,1,0:T(8,128)(2,1)S(1)} %get-tuple-element.31.w_first, ...), custom_call_target="tpu_custom_call" | custom-call | flops 2000000000 | bytes 3000000 | tf_op jit(solution)/shard_map/pallas_call | solution.py:635
  23.6 0.0 collective-permute-done.4.from_twin
  23.6 3.2 %shard_map.82 = f32[16,8,128]{2,1,0:T(8,128)} custom-call(bf16[200,256]{1,0:T(8,128)(2,1)S(1)} %collective-permute-done.4.from_twin, f32[4,8,32,256]{3,2,1,0:T(8,128)S(1)} %get-tuple-element.43.skip_s, bf16[4,2,40,256]{3,2,1,0:T(8,128)(2,1)S(1)} %get-tuple-element.44.mid_near, bf16[4,2,40,256]{3,2,1,0:T(8,128)(2,1)S(1)} %get-tuple-element.45.mid_far, ...), custom_call_target="tpu_custom_call" | custom-call | flops 6000000000 | bytes 9000000 | tf_op jit(solution)/shard_map/pallas_call | solution.py:652
  (1 shorter events, 0.0 us)
Async XLA Ops:
  0.0 6.6 %collective-permute-start = (bf16[16,8,128]{2,1,0:T(8,128)(2,1)}, bf16[16,8,128]{2,1,0:T(8,128)(2,1)S(1)}, u32[]{:S(2)}, u32[]{:S(2)}) collective-permute-start(bf16[16,8,128]{2,1,0:T(8,128)(2,1)} %own.1), channel_id=1, source_target_pairs={{1,2},{2,1},{3,4},{4,3},{5,6},{6,5},{9,10},{10,9},{11,12},{12,11},... | collective-permute-start | bytes 98312 | tf_op jit(solution)/shard_map/ppermute | solution.py:559
  3.4 3.4 %collective-permute-start.1 = (bf16[16,8,128]{2,1,0:T(8,128)(2,1)}, bf16[16,8,128]{2,1,0:T(8,128)(2,1)S(1)}, u32[]{:S(2)}, u32[]{:S(2)}) collective-permute-start(bf16[16,8,128]{2,1,0:T(8,128)(2,1)} %own.1), channel_id=1, source_target_pairs={{0,1},{1,0},{2,3},{3,2},{4,5},{5,4},{6,7},{7,6},{8,9},{9,8},{10,11... | collective-permute-start | bytes 98312 | tf_op jit(solution)/shard_map/ppermute | solution.py:560
  6.0 0.8 %copy-start = (bf16[16,8,128]{2,1,0:T(8,128)(2,1)S(1)}, bf16[16,8,128]{2,1,0:T(8,128)(2,1)}, u32[]{:S(2)}) copy-start(bf16[16,8,128]{2,1,0:T(8,128)(2,1)} %own.1) | copy-start | bytes 98308
  7.0 3.0 %collective-permute-start.2 = (bf16[128,256]{1,0:T(8,128)(2,1)S(1)}, bf16[128,256]{1,0:T(8,128)(2,1)S(1)}, u32[]{:S(2)}, u32[]{:S(2)}) collective-permute-start(bf16[128,256]{1,0:T(8,128)(2,1)S(1)} %shard_map.75.after.own), channel_id=1, source_target_pairs={{0,8},{8,0},{16,24},{24,16},{32,40},{40,32},{48,56},{56,48},{64,72... | collective-permute-start | bytes 196616 | tf_op jit(solution)/shard_map/ppermute | solution.py:571
  9.9 11.0 %collective-permute-start.3 = (bf16[176,256]{1,0:T(8,128)(2,1)S(1)}, bf16[176,256]{1,0:T(8,128)(2,1)S(1)}, u32[]{:S(2)}, u32[]{:S(2)}) collective-permute-start(bf16[176,256]{1,0:T(8,128)(2,1)S(1)} %shard_map.77.after), channel_id=1, source_target_pairs={{8,16},{16,8},{24,32},{32,24},{40,48},{48,40},{56,64},{64,56},{72,... | collective-permute-start | bytes 270344 | tf_op jit(solution)/shard_map/ppermute | solution.py:589
  21.9 1.7 %collective-permute-start.4 = (bf16[200,256]{1,0:T(8,128)(2,1)S(1)}, bf16[200,256]{1,0:T(8,128)(2,1)S(1)}, u32[]{:S(2)}, u32[]{:S(2)}) collective-permute-start(bf16[200,256]{1,0:T(8,128)(2,1)S(1)} %get-tuple-element.40.after), channel_id=1, source_target_pairs={{0,8},{8,0},{16,24},{24,16},{32,40},{40,32},{48,56},{56,48},{64,72... | collective-permute-start | bytes 307208 | tf_op jit(solution)/shard_map/ppermute | solution.py:634
